TPU v7x, 32 devices: a whole 2x2x4 slice. The times are simulated.
32 devices in a mesh: pipe: 2 (over x), dp: 8 (over z, y), tensor: 2 (over core).
Axes of the slice: x: 2, y: 2, z: 4, core: 2. Of those that a mesh axis runs over, the one named last changes fastest.
Arguments:
- inputs: bfloat16 [4096, 768], P(('dp', 'tensor')), may hold values from -6 to 6
- cotangent: bfloat16 [4096, 768], P(('dp', 'tensor')), may hold values from -6 to 6
- dealing: int32 [4096], P(('dp', 'tensor')), may hold values from 0 to 4095, as said below
- routes: int32 [4096, 1], P(('dp', 'tensor')), may hold values from 0 to 3
- slot_order: int32 [4096], P(('dp', 'tensor')), may hold values from 0 to 4095, each once
- doc_lengths: int32 [16, 2], P('dp'), may hold values from 1 to 255, as said below
- attn_weight: bfloat16 [2, 768, 3, 768], P('pipe', 'dp', None, 'tensor'), may hold values from -0.21875 to 0.21875
- attn_out_weight: bfloat16 [2, 768, 768], P('pipe', ('tensor', 'dp')), may hold values from -0.875 to 0.875
- expert_in_weight: bfloat16 [2, 4, 768, 3072], P('pipe', None, 'dp', 'tensor'), may hold values from -0.21875 to 0.21875
- expert_out_weight: bfloat16 [2, 4, 3072, 768], P('pipe', None, ('tensor', 'dp')), may hold values from -0.4375 to 0.4375
- norm_gains: float32 [2, 2, 768], P('pipe', None, ('dp', 'tensor')), may hold values from 0.25 to 1.75
- router_weight: float32 [2, 768, 4], P('pipe', ('dp', 'tensor')), may hold values from -0.15625 to 0.15625
Outputs:
- activations: bfloat16 [2, 4096, 768], P('pipe', ('dp', 'tensor'))
- input_grads: bfloat16 [2, 4096, 768], P('pipe', ('dp', 'tensor'))
- grad_attn: float32 [2, 768, 3, 768], P('pipe', 'dp', None, 'tensor')
- grad_attn_out: float32 [2, 768, 768], P('pipe', ('tensor', 'dp'))
- grad_expert_in: float32 [2, 4, 768, 3072], P('pipe', None, 'dp', 'tensor')
- grad_expert_out: float32 [2, 4, 3072, 768], P('pipe', None, ('tensor', 'dp'))
- grad_gains: float32 [2, 2, 768], P('pipe', None, ('dp', 'tensor'))
- grad_router: float32 [2, 768, 4], P('pipe', ('dp', 'tensor'))
Inputs may be any that keep to these rules, and one draw needn't show every extreme that they name: dealing is a permutation of the 4096 places; the 256 arriving rows of each device send exactly 16 rows to the 256 places of each device. `doc_lengths`: each row holds 2 lengths that add up to 256; in every row one document covers positions on both sides of the pack's middle; some row has a document of exactly 255.
All inputs are finite; a program needn't handle non-finite values.
Results may differ from a plain program's by a relative error of at most 0.03.
Values may be sent and summed in bfloat16 or wider, within the bound.
No kernel may reach another device: no remote copies, remote signals or barrier semaphores. Data moves between devices by JAX's collectives and lax.ppermute only.
A program may use at most 192 MiB of HBM per device.

v0:
```python
import jax
import jax.numpy as jnp
from jax import lax
from jax.sharding import PartitionSpec as P

HEAD_DIM = 64
MB = 2
TOK_MB = 128


EPSILON = 1e-06
NEGATIVE = -1e30
HIGHEST_PREC = lax.Precision.HIGHEST


def passed_along(value, axis, steps):
    count = lax.axis_size(axis)
    initial, last = (max(0, -steps), min(count, count - steps))
    return lax.ppermute(value, axis, [(source, source + steps) for source in range(initial, last)])


def rms_norm(stream, gain_row):
    return (
        stream * lax.rsqrt(jnp.mean(stream * stream, axis=-1, keepdims=True) + EPSILON) * gain_row
    )


def spread(values):
    return lax.all_gather(values, "tensor", axis=0, tiled=True)


def collect(row_piece, row_count):
    return lax.psum_scatter(
        row_piece(jnp.int32(0), lax.axis_size("tensor") * row_count).astype(jnp.bfloat16),
        "tensor",
        scatter_dimension=0,
        tiled=True,
    ).astype(jnp.float32)


def slice_rows(source_rows):

    def row_piece(first_row, row_count):
        return lax.dynamic_slice_in_dim(source_rows, first_row, row_count, 0)

    return row_piece


def block_mask(doc_row, block_start, block_rows):
    pack_len = doc_row.shape[0]
    query_pos = block_start + jnp.arange(block_rows)
    key_pos = jnp.arange(pack_len)
    query_doc = doc_row[block_start : block_start + block_rows]
    return (query_doc[:, None] == doc_row[None, :]) & (key_pos[None, :] <= query_pos[:, None])


def split_heads(proj_qkv, local_heads):
    pack_len = proj_qkv.shape[0]
    head_width = local_heads * HEAD_DIM
    query_rows = proj_qkv[:, :head_width].reshape(pack_len, local_heads, HEAD_DIM)
    key_rows = proj_qkv[:, head_width : 2 * head_width].reshape(pack_len, local_heads, HEAD_DIM)
    value_rows = proj_qkv[:, 2 * head_width :].reshape(pack_len, local_heads, HEAD_DIM)
    return (query_rows, key_rows, value_rows)


def attend(proj_qkv, doc_row, local_heads):
    pack_len = proj_qkv.shape[0]
    query_rows, key_rows, value_rows = split_heads(proj_qkv, local_heads)
    scale = HEAD_DIM ** (-0.5)
    block_rows = min(512, pack_len)
    mixed_parts = []
    total_parts = []
    for block_start in range(0, pack_len, block_rows):
        scores = (
            jnp.einsum(
                "qhd,khd->hqk",
                query_rows[block_start : block_start + block_rows],
                key_rows,
                preferred_element_type=jnp.float32,
            )
            * scale
        )
        scores = jnp.where(block_mask(doc_row, block_start, block_rows)[None], scores, NEGATIVE)
        row_max = jnp.max(scores, axis=-1, keepdims=True)
        weights = jnp.exp(scores - row_max)
        totals = jnp.sum(weights, axis=-1, keepdims=True)
        attn_probs = (weights / totals).astype(jnp.bfloat16)
        mixed_parts.append(
            jnp.einsum("hqk,khd->qhd", attn_probs, value_rows, preferred_element_type=jnp.float32)
        )
        total_parts.append(row_max[..., 0] + jnp.log(totals[..., 0]))
    mixed_heads = (
        jnp.concatenate(mixed_parts, axis=0)
        .reshape(pack_len, local_heads * HEAD_DIM)
        .astype(jnp.bfloat16)
    )
    return (mixed_heads, jnp.concatenate(total_parts, axis=1))


def attend_back(proj_qkv, log_total, grad_mixed, doc_row, local_heads):
    pack_len = proj_qkv.shape[0]
    query_rows, key_rows, value_rows = split_heads(proj_qkv, local_heads)
    grad_heads = grad_mixed.reshape(pack_len, local_heads, HEAD_DIM)
    scale = HEAD_DIM ** (-0.5)
    block_rows = min(512, pack_len)
    grad_keys = jnp.zeros((pack_len, local_heads, HEAD_DIM), jnp.float32)
    grad_values = jnp.zeros((pack_len, local_heads, HEAD_DIM), jnp.float32)
    query_parts = []
    for block_start in range(0, pack_len, block_rows):
        query_block = query_rows[block_start : block_start + block_rows]
        grad_block = grad_heads[block_start : block_start + block_rows]
        scores = (
            jnp.einsum("qhd,khd->hqk", query_block, key_rows, preferred_element_type=jnp.float32)
            * scale
        )
        scores = jnp.where(block_mask(doc_row, block_start, block_rows)[None], scores, NEGATIVE)
        attn_probs = jnp.exp(scores - log_total[:, block_start : block_start + block_rows, None])
        grad_probs = jnp.einsum(
            "qhd,khd->hqk", grad_block, value_rows, preferred_element_type=jnp.float32
        )
        grad_scores = (
            attn_probs
            * (grad_probs - jnp.sum(attn_probs * grad_probs, axis=-1, keepdims=True))
            * scale
        )
        grad_scores = grad_scores.astype(jnp.bfloat16)
        query_parts.append(
            jnp.einsum("hqk,khd->qhd", grad_scores, key_rows, preferred_element_type=jnp.float32)
        )
        grad_keys = grad_keys + jnp.einsum(
            "hqk,qhd->khd", grad_scores, query_block, preferred_element_type=jnp.float32
        )
        grad_values = grad_values + jnp.einsum(
            "hqk,qhd->khd",
            attn_probs.astype(jnp.bfloat16),
            grad_block,
            preferred_element_type=jnp.float32,
        )
    head_width = local_heads * HEAD_DIM
    grad_query = jnp.concatenate(query_parts, axis=0).reshape(pack_len, head_width)
    joined = jnp.concatenate(
        [
            grad_query,
            grad_keys.reshape(pack_len, head_width),
            grad_values.reshape(pack_len, head_width),
        ],
        axis=1,
    )
    return joined.astype(jnp.bfloat16)


def slot_plan(expert_ids, priority, num_experts, capacity):
    pack_len = expert_ids.shape[0]
    same_expert = expert_ids[:, None] == expert_ids[None, :]
    earlier = priority[None, :] < priority[:, None]
    slot_rank = jnp.sum((same_expert & earlier).astype(jnp.int32), axis=1)
    is_kept = slot_rank < capacity
    slot_ids = jnp.arange(num_experts * capacity)
    slot_hit = (expert_ids[None, :] == (slot_ids // capacity)[:, None]) & (
        slot_rank[None, :] == (slot_ids % capacity)[:, None]
    )
    filled = jnp.any(slot_hit, axis=1)
    source = jnp.sum(jnp.where(slot_hit, jnp.arange(pack_len)[None, :], 0), axis=1)
    where_slot = jnp.clip(expert_ids * capacity + slot_rank, 0, num_experts * capacity - 1)
    return (is_kept, filled, source, where_slot)


def layer_forward(stream, big_weights, small_params, expert_ids, priority, doc_row):
    attn_weight, attn_out_weight, expert_in_weight, expert_out_weight = big_weights
    norm_gains, router_weight = small_params
    dev_rows = stream.shape[0]
    local_heads = attn_out_weight.shape[0] // HEAD_DIM
    num_experts = expert_in_weight.shape[0]
    pack_len = expert_ids.shape[0]
    capacity = pack_len // num_experts
    attn_in = spread(rms_norm(stream, norm_gains[0]).astype(jnp.bfloat16))
    proj_qkv = jnp.dot(
        attn_in, attn_weight.reshape(attn_weight.shape[0], -1), preferred_element_type=jnp.float32
    ).astype(jnp.bfloat16)
    mixed_heads, log_total = attend(proj_qkv, doc_row, local_heads)

    def attn_piece(first_row, row_count):
        return jnp.dot(
            lax.dynamic_slice_in_dim(mixed_heads, first_row, row_count, 0),
            attn_out_weight,
            preferred_element_type=jnp.float32,
        )

    mid_stream = stream + collect(attn_piece, dev_rows)
    mlp_in = spread(rms_norm(mid_stream, norm_gains[1]).astype(jnp.bfloat16))
    is_kept, filled, source, where_slot = slot_plan(expert_ids, priority, num_experts, capacity)
    logits = jnp.dot(mlp_in.astype(jnp.float32), router_weight, precision=HIGHEST_PREC)
    row_max = jnp.max(logits, axis=-1, keepdims=True)
    weights = jnp.exp(logits - row_max)
    router_probs = weights / jnp.sum(weights, axis=-1, keepdims=True)
    onehot = expert_ids[:, None] == jnp.arange(num_experts)[None, :]
    gate_value = jnp.sum(jnp.where(onehot, router_probs, 0.0), axis=1)
    dispatched = jnp.where(filled[:, None], mlp_in[source], jnp.zeros((), jnp.bfloat16)).reshape(
        num_experts, capacity, -1
    )
    pre_act = jnp.einsum(
        "ecd,edf->ecf", dispatched, expert_in_weight, preferred_element_type=jnp.float32
    )
    activated = jax.nn.gelu(pre_act).astype(jnp.bfloat16)
    expert_out = jnp.einsum(
        "ecf,efd->ecd", activated, expert_out_weight, preferred_element_type=jnp.float32
    )
    expert_out = expert_out.reshape(num_experts * capacity, -1)
    token_out = jnp.where(is_kept[:, None], expert_out[where_slot], 0.0)
    out_stream = mid_stream + collect(slice_rows(gate_value[:, None] * token_out), dev_rows)
    stored = (
        stream,
        mid_stream,
        attn_in,
        proj_qkv,
        log_total,
        mixed_heads,
        mlp_in,
        router_probs,
        gate_value,
        dispatched,
        pre_act,
        activated,
        token_out,
        is_kept,
        filled,
        source,
        where_slot,
    )
    return (out_stream, stored)


def layer_backward(grad_out, stored, big_weights, small_params, expert_ids, doc_row):
    (
        stream,
        mid_stream,
        attn_in,
        proj_qkv,
        log_total,
        mixed_heads,
        mlp_in,
        router_probs,
        gate_value,
        dispatched,
        pre_act,
        activated,
        token_out,
        is_kept,
        filled,
        source,
        where_slot,
    ) = stored
    attn_weight, attn_out_weight, expert_in_weight, expert_out_weight = big_weights
    norm_gains, router_weight = small_params
    dev_rows = stream.shape[0]
    local_heads = attn_out_weight.shape[0] // HEAD_DIM
    num_experts = expert_in_weight.shape[0]
    capacity = dispatched.shape[1]
    grad_branch = spread(grad_out)
    grad_gate = jnp.sum(grad_branch * token_out, axis=1)
    grad_token = grad_branch * gate_value[:, None]
    grad_slot = (
        jnp.where(filled[:, None], grad_token[source], 0.0)
        .astype(jnp.bfloat16)
        .reshape(num_experts, capacity, -1)
    )
    grad_act = jnp.einsum(
        "ecd,efd->ecf", grad_slot, expert_out_weight, preferred_element_type=jnp.float32
    )
    grad_pre = jax.vjp(jax.nn.gelu, pre_act)[1](grad_act)[0].astype(jnp.bfloat16)
    grad_disp = jnp.einsum(
        "ecf,edf->ecd", grad_pre, expert_in_weight, preferred_element_type=jnp.float32
    )
    grad_disp = grad_disp.reshape(num_experts * capacity, -1)
    onehot = (expert_ids[:, None] == jnp.arange(num_experts)[None, :]).astype(jnp.float32)
    grad_logits = (grad_gate * gate_value)[:, None] * (onehot - router_probs)
    grad_mlp = jnp.where(is_kept[:, None], grad_disp[where_slot], 0.0)
    grad_mlp = grad_mlp + jnp.dot(grad_logits, router_weight.T, precision=HIGHEST_PREC)
    grad_norm_two = collect(slice_rows(grad_mlp), dev_rows)
    grad_mid_norm, grad_gain_two = jax.vjp(rms_norm, mid_stream, norm_gains[1])[1](grad_norm_two)
    grad_mid = grad_out.astype(jnp.float32) + grad_mid_norm
    grad_resid = spread(grad_mid.astype(jnp.bfloat16))
    grad_mixed = jnp.einsum(
        "nd,kd->nk", grad_resid, attn_out_weight, preferred_element_type=jnp.float32
    ).astype(jnp.bfloat16)
    grad_proj = attend_back(proj_qkv, log_total, grad_mixed, doc_row, local_heads)
    flat_weight = attn_weight.reshape(attn_weight.shape[0], -1)

    def attn_piece(first_row, row_count):
        return jnp.einsum(
            "nk,dk->nd",
            lax.dynamic_slice_in_dim(grad_proj, first_row, row_count, 0),
            flat_weight,
            preferred_element_type=jnp.float32,
        )

    grad_norm_one = collect(attn_piece, dev_rows)
    grad_stream_norm, grad_gain_one = jax.vjp(rms_norm, stream, norm_gains[0])[1](grad_norm_one)
    grad_stream = grad_mid + grad_stream_norm
    record = (
        attn_in,
        grad_proj,
        mixed_heads,
        grad_resid,
        mlp_in,
        grad_logits,
        dispatched,
        grad_pre,
        activated,
        grad_slot,
        jnp.stack([grad_gain_one, grad_gain_two]),
    )
    return (grad_stream, record)


def weight_grads(record):
    (
        attn_in,
        grad_proj,
        mixed_heads,
        grad_resid,
        mlp_in,
        grad_logits,
        dispatched,
        grad_pre,
        activated,
        grad_slot,
        grad_gain_pair,
    ) = record
    model_width = attn_in.shape[1]
    grad_attn = jnp.einsum(
        "nd,nk->dk", attn_in, grad_proj, preferred_element_type=jnp.float32
    ).reshape(model_width, 3, -1)
    grad_attn_out = jnp.einsum(
        "nk,nd->kd", mixed_heads, grad_resid, preferred_element_type=jnp.float32
    )
    grad_expert_in = jnp.einsum(
        "ecd,ecf->edf", dispatched, grad_pre, preferred_element_type=jnp.float32
    )
    grad_expert_out = jnp.einsum(
        "ecf,ecd->efd", activated, grad_slot, preferred_element_type=jnp.float32
    )
    grad_router = jnp.dot(mlp_in.astype(jnp.float32).T, grad_logits, precision=HIGHEST_PREC)
    return (grad_attn, grad_attn_out, grad_expert_in, grad_expert_out, grad_gain_pair, grad_router)


def local(
    inputs,
    cotangent,
    dealing,
    routes,
    slot_order,
    doc_lengths,
    attn_weight,
    attn_out_weight,
    expert_in_weight,
    expert_out_weight,
    norm_gains,
    router_weight,
):
    section_index = lax.axis_index("pipe")
    dev_rows = inputs.shape[0]
    send_order = jnp.argsort(dealing)
    local_place = dealing % dev_rows
    incoming_rows = (
        lax.all_to_all(
            inputs[send_order], ("dp", "tensor"), split_axis=0, concat_axis=0, tiled=True
        ),
        lax.all_to_all(
            cotangent[send_order], ("dp", "tensor"), split_axis=0, concat_axis=0, tiled=True
        ),
        lax.all_to_all(
            local_place[send_order], ("dp", "tensor"), split_axis=0, concat_axis=0, tiled=True
        ),
        lax.all_to_all(
            routes[send_order, 0], ("dp", "tensor"), split_axis=0, concat_axis=0, tiled=True
        ),
        lax.all_to_all(
            slot_order[send_order], ("dp", "tensor"), split_axis=0, concat_axis=0, tiled=True
        ),
    )
    arrived_place = incoming_rows[2]
    placement = jnp.argsort(arrived_place)
    tok_inputs = incoming_rows[0][placement].reshape(MB, TOK_MB, -1)
    tok_cotangent = incoming_rows[1][placement].reshape(MB, TOK_MB, -1)
    pack_routes, pack_orders = (
        lax.all_gather(
            incoming_rows[3][placement].reshape(MB, TOK_MB), "tensor", axis=1, tiled=True
        ),
        lax.all_gather(
            incoming_rows[4][placement].reshape(MB, TOK_MB), "tensor", axis=1, tiled=True
        ),
    )
    pack_len = pack_routes.shape[1]
    doc_ends = jnp.cumsum(doc_lengths, axis=1)
    positions = jnp.arange(pack_len)
    doc_rows = jnp.sum((positions[None, :, None] >= doc_ends[:, None, :]).astype(jnp.int32), axis=2)

    def fetch_weights():
        return (
            lax.all_gather(attn_weight[0], "dp", axis=0, tiled=True),
            lax.all_gather(attn_out_weight[0], "dp", axis=0, tiled=True),
            lax.all_gather(expert_in_weight[0], "dp", axis=1, tiled=True),
            lax.all_gather(expert_out_weight[0], "dp", axis=1, tiled=True),
        )

    small_params = (
        lax.all_gather(norm_gains[0], ("dp", "tensor"), axis=1, tiled=True),
        lax.all_gather(router_weight[0], ("dp", "tensor"), axis=0, tiled=True),
    )
    big_weights = fetch_weights()

    def micro_meta(micro_index):
        return (
            lax.dynamic_index_in_dim(pack_routes, micro_index, 0, keepdims=False),
            lax.dynamic_index_in_dim(pack_orders, micro_index, 0, keepdims=False),
            lax.dynamic_index_in_dim(doc_rows, micro_index, 0, keepdims=False),
        )

    incoming = jnp.zeros_like(tok_inputs[0])
    forward_out = []
    forward_kept = []
    for step_index in range(MB + 1):
        own_rows = tok_inputs[min(step_index, MB - 1)]
        stream = jnp.where(section_index == 0, own_rows, incoming).astype(jnp.float32)
        micro_index = jnp.clip(step_index - section_index, 0, MB - 1)
        expert_ids, priority, doc_row = micro_meta(micro_index)
        out_stream, stored = layer_forward(
            stream, big_weights, small_params, expert_ids, priority, doc_row
        )
        out_low = out_stream.astype(jnp.bfloat16)
        forward_out.append(out_low)
        forward_kept.append(stored)
        if step_index < MB:
            incoming = passed_along(out_low, "pipe", 1)
    kept_stack = jax.tree.map(lambda *members: jnp.stack(members), *forward_kept)
    back_weights = fetch_weights()
    incoming_grad = jnp.zeros_like(tok_cotangent[0])
    grad_steps = []
    records = []
    for step_index in range(MB + 1):
        own_grad = tok_cotangent[min(step_index, MB - 1)]
        grad_out = jnp.where(section_index == 1, own_grad, incoming_grad)
        micro_index = jnp.clip(step_index - 1 + section_index, 0, MB - 1)
        forward_step = jnp.clip(step_index - 1 + 2 * section_index, 0, MB)
        stored = jax.tree.map(
            lambda member: lax.dynamic_index_in_dim(member, forward_step, 0, keepdims=False),
            kept_stack,
        )
        expert_ids, priority, doc_row = micro_meta(micro_index)
        grad_stream, record = layer_backward(
            grad_out, stored, back_weights, small_params, expert_ids, doc_row
        )
        grad_low = grad_stream.astype(jnp.bfloat16)
        grad_steps.append(grad_low)
        records.append(record)
        if step_index < MB:
            incoming_grad = passed_along(grad_low, "pipe", -1)
    record_stack = jax.tree.map(lambda *members: jnp.stack(members), *records)
    small_sum = None
    grad_sum = None
    for micro_index in range(MB):
        grads_now = weight_grads(
            jax.tree.map(
                lambda member: lax.dynamic_index_in_dim(
                    member, micro_index + 1 - section_index, 0, keepdims=False
                ),
                record_stack,
            )
        )
        grad_sum = grads_now if grad_sum is None else jax.tree.map(jnp.add, grad_sum, grads_now)
    shard_sum = (
        lax.psum_scatter(grad_sum[0], "dp", scatter_dimension=0, tiled=True),
        lax.psum_scatter(grad_sum[1], "dp", scatter_dimension=0, tiled=True),
        lax.psum_scatter(grad_sum[2], "dp", scatter_dimension=1, tiled=True),
        lax.psum_scatter(grad_sum[3], "dp", scatter_dimension=1, tiled=True),
    )
    small_sum = (grad_sum[4], grad_sum[5])
    small_shards = (
        lax.psum_scatter(small_sum[0], ("dp", "tensor"), scatter_dimension=1, tiled=True),
        lax.psum_scatter(small_sum[1], ("dp", "tensor"), scatter_dimension=0, tiled=True),
    )
    layer_out = lax.dynamic_slice_in_dim(jnp.stack(forward_out), section_index, MB, 0).reshape(
        dev_rows, -1
    )
    layer_grad = lax.dynamic_slice_in_dim(jnp.stack(grad_steps), 1 - section_index, MB, 0).reshape(
        dev_rows, -1
    )
    returned = (
        lax.all_to_all(
            layer_out[arrived_place], ("dp", "tensor"), split_axis=0, concat_axis=0, tiled=True
        ),
        lax.all_to_all(
            layer_grad[arrived_place], ("dp", "tensor"), split_axis=0, concat_axis=0, tiled=True
        ),
    )
    restore = jnp.argsort(send_order)
    activations = returned[0][restore][None]
    input_grads = returned[1][restore][None]
    return (
        activations,
        input_grads,
        shard_sum[0][None],
        shard_sum[1][None],
        shard_sum[2][None],
        shard_sum[3][None],
        small_shards[0][None],
        small_shards[1][None],
    )


def solution(mesh):
    in_specs = (
        P(("dp", "tensor"), None),
        P(("dp", "tensor"), None),
        P(("dp", "tensor")),
        P(("dp", "tensor"), None),
        P(("dp", "tensor")),
        P("dp", None),
        P("pipe", "dp", None, "tensor"),
        P("pipe", ("tensor", "dp"), None),
        P("pipe", None, "dp", "tensor"),
        P("pipe", None, ("tensor", "dp"), None),
        P("pipe", None, ("dp", "tensor")),
        P("pipe", ("dp", "tensor"), None),
    )
    out_specs = (
        P("pipe", ("dp", "tensor"), None),
        P("pipe", ("dp", "tensor"), None),
        P("pipe", "dp", None, "tensor"),
        P("pipe", ("tensor", "dp"), None),
        P("pipe", None, "dp", "tensor"),
        P("pipe", None, ("tensor", "dp"), None),
        P("pipe", None, ("dp", "tensor")),
        P("pipe", ("dp", "tensor"), None),
    )
    return jax.shard_map(local, mesh=mesh, in_specs=in_specs, out_specs=out_specs, check_vma=False)
```

profile of v0, /device:TPU:0, one launch (start us, length us, event | category | flops | bytes accessed | tf_op | source)
XLA Modules:
  0.0 1660.5 jit_solution(1379649681151618690)
XLA Ops:
  7.9 3.8 sort.45
  15.6 7.4 all-to-all-start.1
  26.7 24.1 %all-gather = f32[1,2,768]{1,0,2:T(1,128)S(1)} all-gather(f32[1,2,48]{1,0,2:T(1,128)S(1)} %copy.166), channel_id=2, replica_groups=mesh['pipe'=2,'dp'=8,'tensor'=2] {'dp','tensor'}, dimensions={2}, use_global_device_ids=true | all-gather | bytes 6528 | tf_op jit(solution)/shard_map/all_gather | solution.py:408
  50.8 3.6 all-to-all-start
  54.4 4.5 slice_reduce_fusion
  59.0 33.5 %all-gather.2 = bf16[1,384,768]{2,1,0:T(8,128)(2,1)S(1)} all-gather(bf16[1,48,768]{2,1,0:T(8,128)(2,1)S(1)} %copy-done.123), channel_id=4, replica_groups=mesh['pipe'=2,'dp'=8,'tensor'=2] {'dp'}, dimensions={1}, use_global_device_ids=true | all-gather | bytes 663552 | tf_op jit(solution)/shard_map/all_gather | solution.py:402
  93.8 3.2 sort.46
  100.5 4.0 copy.167
  114.1 4.1 all-to-all-start.3
  124.6 3.5 all-to-all-start.2
  128.0 25.5 %all-gather.3 = f32[1,768,4]{2,0,1:T(1,128)S(1)} all-gather(f32[1,48,4]{2,0,1:T(1,128)S(1)} %copy.173), channel_id=5, replica_groups=mesh['pipe'=2,'dp'=8,'tensor'=2] {'dp','tensor'}, dimensions={1}, use_global_device_ids=true | all-gather | bytes 13056 | tf_op jit(solution)/shard_map/all_gather | solution.py:409
  158.2 3.6 all-to-all-start.5
  182.8 86.5 %all-gather.12.cloned.1.call-done = bf16[1,4,768,1536]{3,2,1,0:T(8,128)(2,1)} async-done(((bf16[1,4,96,1536]{3,2,1,0:T(8,128)(2,1)}), bf16[1,4,768,1536]{3,2,1,0:T(8,128)(2,1)}) %all-gather.12.cloned.1.call-update) | async-done | bytes 9437200 | tf_op jit(solution)/shard_map/all_gather | solution.py:403
  269.3 6.7 fusion.25
  276.0 131.8 %all-gather.14.cloned.1.call-done = bf16[1,4,1536,768]{3,2,1,0:T(8,128)(2,1)} async-done(((bf16[1,4,192,768]{3,2,1,0:T(8,128)(2,1)}), bf16[1,4,1536,768]{3,2,1,0:T(8,128)(2,1)}) %all-gather.14.cloned.1.call-update) | async-done | bytes 9437200 | tf_op jit(solution)/shard_map/all_gather | solution.py:404
  407.9 6.0 fusion.13
  425.5 3.6 collective-permute-start
  430.3 3.4 collective-permute-done
  444.9 6.1 reduce-scatter.27.cloned.1.call-done
  458.7 5.5 fusion.23
  464.2 6.1 fusion.11
  474.6 3.9 all_gather.78
  479.5 4.2 reduce-scatter.29.cloned.1.call-done
  484.6 3.6 collective-permute-start.1
  506.0 6.3 reduce-scatter.31.cloned.1.call-done
  519.9 5.5 fusion.21
  525.4 6.1 fusion.9
  538.5 2.9 pad_maximum_fusion
  541.5 9.3 fusion.33
  550.8 2.9 fusion.19
  556.0 2.8 fusion.114
  564.3 3.6 reduce-scatter.35.cloned.1.call-done
  579.2 3.5 fusion.132
  582.7 3.5 fusion.129
  586.2 3.0 convolution_convert_fusion.5
  591.9 6.4 reduce-scatter.37.cloned.1.call-done
  603.2 7.5 collective-permute-done.2
  616.9 7.3 fusion.40
  624.3 2.9 fusion.17
  634.9 3.4 reduce-scatter.39.cloned.1.call-done
  649.0 3.5 fusion.126
  652.5 4.1 fusion.123
  656.6 3.1 convolution_convert_fusion.4
  660.5 8.3 reduce-scatter.41.cloned.1.call-done
  672.8 7.5 collective-permute-done.3
  686.6 7.3 fusion.47
  694.0 2.9 fusion.15
  703.6 4.4 reduce-scatter.43.cloned.1.call-done
  718.8 4.2 fusion.120
  723.0 4.2 fusion.117
  727.2 3.3 convolution_convert_fusion.3
  754.0 8.0 fusion.142
  762.0 12.4 convolution_add_fusion.1
  781.1 8.0 fusion.139
  789.1 12.2 convolution_add_fusion
  805.6 6.0 all-to-all-start.4
  815.1 8.6 all-to-all-done.4
  823.8 3.6 all-to-all-start.6
  827.3 3.2 sort.47
  833.8 36.0 %reduce-scatter.55.cloned.1.call-done = f32[48,2]{1,0:T(8,128)} async-done(((f32[768,2]{1,0:T(8,128)}), f32[48,2]{1,0:T(8,128)}) %reduce-scatter.55.cloned.1.call-update) | async-done | bytes 400
  873.2 63.6 %reduce-scatter.49.cloned.1.call-done = f32[48,768]{1,0:T(8,128)} async-done(((f32[384,768]{1,0:T(8,128)}), f32[48,768]{1,0:T(8,128)}) %reduce-scatter.49.cloned.1.call-update) | async-done | bytes 147472 | tf_op jit(solution)/shard_map/reduce_scatter | solution.py:474
  936.8 82.3 %reduce-scatter.47.cloned.1.call-done = f32[96,3,384]{2,0,1:T(8,128)} async-done(((f32[768,3,384]{2,0,1:T(8,128)}), f32[96,3,384]{2,0,1:T(8,128)}) %reduce-scatter.47.cloned.1.call-update) | async-done | bytes 442384 | tf_op jit(solution)/shard_map/reduce_scatter | solution.py:473
  1019.2 317.2 %reduce-scatter.51.cloned.1.call-done = f32[4,96,1536]{2,1,0:T(8,128)} async-done(((f32[4,768,1536]{2,1,0:T(8,128)}), f32[4,96,1536]{2,1,0:T(8,128)}) %reduce-scatter.51.cloned.1.call-update) | async-done | bytes 2359312 | tf_op jit(solution)/shard_map/reduce_scatter | solution.py:475
  1336.3 316.9 %reduce-scatter.53.cloned.1.call-done = f32[4,192,768]{2,1,0:T(8,128)} async-done(((f32[4,1536,768]{2,1,0:T(8,128)}), f32[4,192,768]{2,1,0:T(8,128)}) %reduce-scatter.53.cloned.1.call-update) | async-done | bytes 2359312 | tf_op jit(solution)/shard_map/reduce_scatter | solution.py:476
  (776 shorter events, 247.0 us)
Async XLA Ops:
  7.2 16.6 %copy-start = (bf16[256,768]{1,0:T(8,128)(2,1)S(1)}, bf16[256,768]{1,0:T(8,128)(2,1)}, u32[]{:S(2)}) copy-start(bf16[256,768]{1,0:T(8,128)(2,1)} %param.12) | copy-start | bytes 1179652
  7.2 93.3 %all-gather.10.cloned.1.call-start = ((), (), s32[]{:S(2)}) async-start(), calls=%async_computation.41 | async-start | bytes 1990656 | tf_op jit(solution)/shard_map/all_gather | solution.py:401
  15.6 35.2 %all-to-all-start.1 = ((s32[16,16,1]{1,2,0:T(1,128)}), s32[16,16,1]{1,2,0:T(1,128)S(1)}, u32[]{:S(2)}, u32[]{:S(2)}) async-start(s32[16,16,1]{1,2,0:T(1,128)} %bitcast.2), calls=%async_computation.1 | async-start | bytes 16384 | tf_op jit(solution)/shard_map/all_to_all | solution.py:372
  25.7 33.2 %copy-start.123 = (bf16[1,48,768]{2,1,0:T(8,128)(2,1)S(1)}, bf16[1,48,768]{2,1,0:T(8,128)(2,1)}, u32[]{:S(2)}) copy-start(bf16[1,48,768]{2,1,0:T(8,128)(2,1)} %param.19) | copy-start | bytes 221188
  50.8 46.2 %all-to-all-start = ((bf16[16,16,768]{2,1,0:T(8,128)(2,1)}), bf16[16,16,768]{2,1,0:T(8,128)(2,1)S(1)}, u32[]{:S(2)}, u32[]{:S(2)}) async-start(bf16[16,16,768]{2,1,0:T(8,128)(2,1)} %bitcast), calls=%async_computation | async-start | bytes 786432 | tf_op jit(solution)/shard_map/all_to_all | solution.py:366
  54.3 121.8 %reduce-scatter.23.cloned.1.call-start = ((), (), s32[]{:S(2)}) async-start(), calls=%async_computation.25 | async-start | bytes 589824 | tf_op jit(solution)/shard_map/reduce_scatter | solution.py:33
  92.5 480.4 %copy-start.7 = (bf16[1,384,768]{2,1,0:T(8,128)(2,1)}, bf16[1,384,768]{2,1,0:T(8,128)(2,1)S(1)}, u32[]{:S(2)}) copy-start(bf16[1,384,768]{2,1,0:T(8,128)(2,1)S(1)} %all-gather.2) | copy-start | bytes 1769476
  110.2 159.1 %all-gather.12.cloned.1.call-start = ((), (), s32[]{:S(2)}) async-start(), calls=%async_computation.42 | async-start | bytes 10616832 | tf_op jit(solution)/shard_map/all_gather | solution.py:403
  110.9 297.0 %all-gather.14.cloned.1.call-start = ((), (), s32[]{:S(2)}) async-start(), calls=%async_computation.43 | async-start | bytes 10616832 | tf_op jit(solution)/shard_map/all_gather | solution.py:404
  111.5 42.0 %copy-start.15 = (bf16[256,768]{1,0:T(8,128)(2,1)S(1)}, bf16[256,768]{1,0:T(8,128)(2,1)}, u32[]{:S(2)}) copy-start(bf16[256,768]{1,0:T(8,128)(2,1)} %param.13) | copy-start | bytes 1179652
  114.1 10.4 all-to-all-start.3
  124.6 33.6 %all-to-all-start.2 = ((s32[16,16,1]{1,2,0:T(1,128)}), s32[16,16,1]{1,2,0:T(1,128)S(1)}, u32[]{:S(2)}, u32[]{:S(2)}) async-start(s32[16,16,1]{1,2,0:T(1,128)} %bitcast.11), calls=%async_computation.3 | async-start | bytes 16384 | tf_op jit(solution)/shard_map/all_to_all | solution.py:375
  158.2 284.8 %all-to-all-start.5 = ((bf16[16,16,768]{2,1,0:T(8,128)(2,1)}), bf16[16,16,768]{2,1,0:T(8,128)(2,1)S(1)}, u32[]{:S(2)}, u32[]{:S(2)}) async-start(bf16[16,16,768]{2,1,0:T(8,128)(2,1)} %bitcast.65), calls=%async_computation.11 | async-start | bytes 786432 | tf_op jit(solution)/shard_map/all_to_all | solution.py:369
  161.8 262.5 %reduce-scatter.25.cloned.1.call-start = ((), (), s32[]{:S(2)}) async-start(), calls=%async_computation.26 | async-start | bytes 589824 | tf_op jit(solution)/shard_map/reduce_scatter | solution.py:33
  170.5 11.8 copy-start.131
  170.5 11.8 copy-start.133
  170.5 11.8 copy-start.135
  182.3 93.8 %copy-start.28 = (bf16[256,768]{1,0:T(8,128)(2,1)}, bf16[256,768]{1,0:T(8,128)(2,1)S(1)}, u32[]{:S(2)}) copy-start(bf16[256,768]{1,0:T(8,128)(2,1)S(1)} %gather_fusion.7) | copy-start | bytes 1179652
  182.8 233.2 %copy-start.128 = (f32[256]{0:T(256)}, f32[256]{0:T(256)S(1)}, u32[]{:S(2)}) copy-start(f32[256]{0:T(256)S(1)} %get-tuple-element.52) | copy-start | bytes 3076
  418.2 32.8 %reduce-scatter.27.cloned.1.call-start = ((), (), s32[]{:S(2)}) async-start(), calls=%async_computation.27 | async-start | bytes 589824 | tf_op jit(solution)/shard_map/reduce_scatter | solution.py:33
  418.4 39.6 %copy-start.126 = (pred[4,64]{1,0:T(4,128)(4,1)}, pred[4,64]{1,0:T(4,128)(4,1)S(1)}, u32[]{:S(2)}) copy-start(pred[4,64]{1,0:T(4,128)(4,1)S(1)} %broadcast_in_dim.403) | copy-start | bytes 772
  424.3 12.6 copy-start.60
  425.4 11.4 copy-start.88
  425.5 8.3 collective-permute-start
  434.5 17.6 %copy-start.18 = (bf16[128,768]{1,0:T(8,128)(2,1)}, bf16[128,768]{1,0:T(8,128)(2,1)S(1)}, u32[]{:S(2)}) copy-start(bf16[128,768]{1,0:T(8,128)(2,1)S(1)} %get-tuple-element.45) | copy-start | bytes 589828
  441.2 42.4 %reduce-scatter.29.cloned.1.call-start = ((), (), s32[]{:S(2)}) async-start(), calls=%async_computation.28 | async-start | bytes 589824 | tf_op jit(solution)/shard_map/reduce_scatter | solution.py:33
  444.2 12.4 copy-start.24
  474.5 37.7 %reduce-scatter.31.cloned.1.call-start = ((), (), s32[]{:S(2)}) async-start(), calls=%async_computation.29 | async-start | bytes 589824 | tf_op jit(solution)/shard_map/reduce_scatter | solution.py:33
  484.6 8.2 collective-permute-start.1
  493.9 19.4 %copy-start.20 = (bf16[128,768]{1,0:T(8,128)(2,1)}, bf16[128,768]{1,0:T(8,128)(2,1)S(1)}, u32[]{:S(2)}) copy-start(bf16[128,768]{1,0:T(8,128)(2,1)S(1)} %get-tuple-element.47) | copy-start | bytes 589828
  502.4 65.6 %reduce-scatter.35.cloned.1.call-start = ((), (), s32[]{:S(2)}) async-start(), calls=%async_computation.31 | async-start | bytes 589824 | tf_op jit(solution)/shard_map/reduce_scatter | solution.py:33
  538.5 12.3 slice-start
  538.5 12.3 slice-start.1
  558.8 39.4 %reduce-scatter.37.cloned.1.call-start = ((), (), s32[]{:S(2)}) async-start(), calls=%async_computation.32 | async-start | bytes 589824 | tf_op jit(solution)/shard_map/reduce_scatter | solution.py:33
  564.1 36.3 %copy-start.4 = (f32[3,128,768]{2,1,0:T(8,128)}, f32[3,128,768]{2,1,0:T(8,128)S(1)}, u32[]{:S(2)}) copy-start(f32[3,128,768]{2,1,0:T(8,128)S(1)} %pad_maximum_fusion.6) | copy-start | bytes 3538948
  589.2 49.1 %reduce-scatter.39.cloned.1.call-start = ((), (), s32[]{:S(2)}) async-start(), calls=%async_computation.33 | async-start | bytes 589824 | tf_op jit(solution)/shard_map/reduce_scatter | solution.py:33
  589.4 26.8 %copy-start.184 = (pred[4,64]{1,0:T(4,128)(4,1)}, pred[4,64]{1,0:T(4,128)(4,1)S(1)}, u32[]{:S(2)}) copy-start(pred[4,64]{1,0:T(4,128)(4,1)S(1)} %broadcast_in_dim.425) | copy-start | bytes 772
  589.4 11.1 copy-start.25
  589.4 11.1 copy-start.66
  591.9 11.3 copy-start.150
  591.9 11.3 copy-start.149
  601.8 13.1 copy-start.92
  601.8 13.0 copy-start.130
  601.8 8.9 collective-permute-start.2
  630.0 38.8 %reduce-scatter.41.cloned.1.call-start = ((), (), s32[]{:S(2)}) async-start(), calls=%async_computation.34 | async-start | bytes 589824 | tf_op jit(solution)/shard_map/reduce_scatter | solution.py:33
  656.6 13.5 copy-start.46
  659.7 13.1 copy-start.148
  659.7 13.1 copy-start.147
  659.7 20.6 %copy-start.26 = (bf16[256,768]{1,0:T(8,128)(2,1)S(1)}, bf16[256,768]{1,0:T(8,128)(2,1)}, u32[]{:S(2)}) copy-start(bf16[256,768]{1,0:T(8,128)(2,1)} %copy-done.24) | copy-start | bytes 1179652
  659.7 48.3 %reduce-scatter.43.cloned.1.call-start = ((), (), s32[]{:S(2)}) async-start(), calls=%async_computation.35 | async-start | bytes 589824 | tf_op jit(solution)/shard_map/reduce_scatter | solution.py:33
  671.5 13.1 copy-start.94
  671.5 8.9 collective-permute-start.3
  699.7 39.9 %reduce-scatter.45.cloned.1.call-start = ((), (), s32[]{:S(2)}) async-start(), calls=%async_computation.36 | async-start | bytes 589824 | tf_op jit(solution)/shard_map/reduce_scatter | solution.py:33
  730.5 71.5 %reduce-scatter.33.cloned.1.call-start = ((), (), s32[]{:S(2)}) async-start(), calls=%async_computation.30 | async-start | bytes 589824 | tf_op jit(solution)/shard_map/reduce_scatter | solution.py:33
  733.8 98.7 %reduce-scatter.57.cloned.1.call-start = ((), (), s32[]{:S(2)}) async-start(), calls=%async_computation.45 | async-start | bytes 417792
  736.8 133.1 %reduce-scatter.55.cloned.1.call-start = ((), (), s32[]{:S(2)}) async-start(), calls=%async_computation.44 | async-start | bytes 417792
  742.4 194.4 %reduce-scatter.49.cloned.1.call-start = ((), (), s32[]{:S(2)}) async-start(), calls=%async_computation.38 | async-start | bytes 1327104 | tf_op jit(solution)/shard_map/reduce_scatter | solution.py:474
  745.0 274.1 %reduce-scatter.47.cloned.1.call-start = ((), (), s32[]{:S(2)}) async-start(), calls=%async_computation.37 | async-start | bytes 3981312 | tf_op jit(solution)/shard_map/reduce_scatter | solution.py:473
  750.6 585.8 %reduce-scatter.51.cloned.1.call-start = ((), (), s32[]{:S(2)}) async-start(), calls=%async_computation.39 | async-start | bytes 21233664 | tf_op jit(solution)/shard_map/reduce_scatter | solution.py:475
  774.4 878.8 %reduce-scatter.53.cloned.1.call-start = ((), (), s32[]{:S(2)}) async-start(), calls=%async_computation.40 | async-start | bytes 21233664 | tf_op jit(solution)/shard_map/reduce_scatter | solution.py:476
  805.6 18.2 %all-to-all-start.4 = ((bf16[16,16,768]{2,1,0:T(8,128)(2,1)}), bf16[16,16,768]{2,1,0:T(8,128)(2,1)S(1)}, u32[]{:S(2)}, u32[]{:S(2)}) async-start(bf16[16,16,768]{2,1,0:T(8,128)(2,1)} %bitcast.62), calls=%async_computation.10 | async-start | bytes 786432 | tf_op jit(solution)/shard_map/all_to_all | solution.py:490
  813.2 14.2 copy-start.154
  823.8 47.5 %all-to-all-start.6 = ((bf16[16,16,768]{2,1,0:T(8,128)(2,1)}), bf16[16,16,768]{2,1,0:T(8,128)(2,1)S(1)}, u32[]{:S(2)}, u32[]{:S(2)}) async-start(bf16[16,16,768]{2,1,0:T(8,128)(2,1)} %bitcast.179), calls=%async_computation.18 | async-start | bytes 786432 | tf_op jit(solution)/shard_map/all_to_all | solution.py:493
  871.2 782.0 %copy-start.1 = (bf16[256,768]{1,0:T(8,128)(2,1)S(1)}, bf16[256,768]{1,0:T(8,128)(2,1)}, u32[]{:S(2)}) copy-start(bf16[256,768]{1,0:T(8,128)(2,1)} %param.12) | copy-start | bytes 1179652
  (166 other events, 574.0 us)
Sparse Core Ops, SparseCore 0:
  10.2 52.0 all-gather.9
  110.3 7.1 reduce-scatter.22
  119.9 149.3 all-gather.11
  271.6 136.2 all-gather.13
  418.3 5.9 reduce-scatter.24
  441.3 9.6 reduce-scatter.26
  474.6 8.9 reduce-scatter.28
  502.5 9.6 reduce-scatter.30
  559.0 8.9 reduce-scatter.34
  589.3 8.9 reduce-scatter.36
  630.1 8.1 reduce-scatter.38
  659.9 8.8 reduce-scatter.40
  699.8 8.1 reduce-scatter.42
  730.6 8.9 reduce-scatter.44
  742.3 8.9 reduce-scatter.32
  754.7 56.7 reduce-scatter.56
  815.2 54.6 reduce-scatter.54
  873.7 63.0 reduce-scatter.48
  941.0 78.0 reduce-scatter.46
  1023.5 312.8 reduce-scatter.50
  1340.8 312.3 reduce-scatter.52
where the time goes:
time: 1670 us; the launch traced here: 1660 us
  waiting for transfers between devices  1110 us (66%)
  matrix products  186 us (11%)
  blocking collectives  114 us (7%)
  local copies, waits for them, and re-layouts  99.9 us (6%)
  other arithmetic  85.7 us (5%)
  starting transfers between devices  43.1 us (3%)
  between operations  17.9 us (1%)
    reduce_scatter x1, waiting for transfers between devices, local(): lax.psum_scatter(grad_sum[2], 'dp', scatter_dimension=1, tiled=True)  317 us
    reduce_scatter x1, waiting for transfers between devices, local(): lax.psum_scatter(grad_sum[3], 'dp', scatter_dimension=1, tiled=True)  317 us
    all_gather x1, waiting for transfers between devices, fetch_weights(): lax.all_gather(expert_out_weight[0], 'dp', axis=1, tiled=True)  132 us
    all_gather x1, waiting for transfers between devices, fetch_weights(): lax.all_gather(expert_in_weight[0], 'dp', axis=1, tiled=True)  86.5 us
    reduce_scatter x1, waiting for transfers between devices, local(): lax.psum_scatter(grad_sum[0], 'dp', scatter_dimension=0, tiled=True)  82.3 us
    reduce_scatter x1, waiting for transfers between devices, local(): lax.psum_scatter(grad_sum[1], 'dp', scatter_dimension=0, tiled=True)  63.6 us
    reduce_scatter x12, waiting for transfers between devices, collect(): lax.psum_scatter(row_piece(jnp.int32(0), lax.axis_size('tensor') * row_co...  45 us
    unnamed x23, waiting for transfers between devices  38.2 us
  transfers between devices with their start and end apart: 32, of which 23 were waited for; matrix products, arithmetic and copies ran while one was open for 11% of the time, Pallas kernels for 0%

commit v1 on v0

v1 whole, which is shorter than its diff:
```python
import jax
import jax.numpy as jnp
from jax import lax
from jax.sharding import PartitionSpec as P

HEAD_DIM = 64
EPSILON = 1e-06
NEGATIVE = -1e30
EXACT = lax.Precision.HIGHEST
EXTRA = 128
BF = jnp.bfloat16
F32 = jnp.float32


def dot32(a, b):
    return jnp.dot(a, b, preferred_element_type=F32)


def dot_nt(a, b):
    return lax.dot_general(a, b, (((1,), (1,)), ((), ())), preferred_element_type=F32)


def dot_tn(a, b):
    return lax.dot_general(a, b, (((0,), (0,)), ((), ())), preferred_element_type=F32)


def round_bf(v):
    return lax.reduce_precision(v, 8, 7)


def norm_scale(x):
    return lax.rsqrt(jnp.mean(x * x, axis=-1, keepdims=True) + EPSILON)


def norm_back(x, scale, gain, grad):
    weighted = grad * gain
    grad_x = scale * weighted - x * (scale * scale * scale) * jnp.mean(
        x * weighted, axis=-1, keepdims=True
    )
    return grad_x, jnp.sum(grad * x * scale, axis=0)


def heads_of(flat, heads):
    return flat.reshape(flat.shape[0], heads, HEAD_DIM)


def probs_of(query, key, allowed):
    scores = jnp.einsum("qhd,khd->hqk", query, key, preferred_element_type=F32)
    scores = jnp.where(allowed[None], scores * HEAD_DIM ** (-0.5), NEGATIVE)
    weights = jnp.exp(scores - jnp.max(scores, axis=-1, keepdims=True))
    return weights / jnp.sum(weights, axis=-1, keepdims=True)


def attn_forward(stream, weights, plan):
    qkv_weight, out_weight, gains, router = weights
    slots, onehot, allowed = plan
    width = stream.shape[1]
    heads = width // HEAD_DIM
    x = stream.astype(F32)
    attn_in = (x * norm_scale(x) * gains[0]).astype(BF)
    proj = dot32(attn_in, qkv_weight).astype(BF)
    query, key, value = (heads_of(proj[:, i * width : (i + 1) * width], heads) for i in range(3))
    probs = probs_of(query, key, allowed).astype(BF)
    mixed = jnp.einsum("hqk,khd->qhd", probs, value, preferred_element_type=F32)
    mixed = mixed.reshape(x.shape).astype(BF)
    mid = x + dot32(mixed, out_weight)
    mlp_in = (mid * norm_scale(mid) * gains[1]).astype(BF)
    logits = jnp.dot(mlp_in.astype(F32), router, precision=EXACT)
    rel = jnp.exp(logits - jnp.max(logits, axis=-1, keepdims=True))
    router_probs = rel / jnp.sum(rel, axis=-1, keepdims=True)
    gate = jnp.sum(jnp.where(onehot, router_probs, 0.0), axis=1, keepdims=True)
    dispatched = dot32(slots, mlp_in).astype(BF)
    return mid, attn_in, proj, mixed, mlp_in, router_probs, gate, dispatched


def attn_backward(grad_out, grad_slots, expert_slots, stream, saved, weights, plan):
    mid, attn_in, proj, mixed, mlp_in, router_probs, gate, _ = saved
    qkv_weight, out_weight, gains, router = weights
    slots, onehot, allowed = plan
    width = stream.shape[1]
    heads = width // HEAD_DIM
    x = stream.astype(F32)
    g = grad_out.astype(F32)
    grad_gate = jnp.sum(g * dot_tn(slots, expert_slots), axis=1, keepdims=True)
    grad_logits = grad_gate * gate * (onehot.astype(F32) - router_probs)
    grad_mlp = dot_tn(slots, grad_slots) + jnp.dot(grad_logits, router.T, precision=EXACT)
    grad_norm, gain_two = norm_back(mid, norm_scale(mid), gains[1], grad_mlp)
    grad_mid = g + grad_norm
    grad_low = grad_mid.astype(BF)
    grad_mixed = heads_of(dot_nt(grad_low, out_weight).astype(BF), heads)
    query, key, value = (heads_of(proj[:, i * width : (i + 1) * width], heads) for i in range(3))
    probs = probs_of(query, key, allowed)
    grad_probs = jnp.einsum("qhd,khd->hqk", grad_mixed, value, preferred_element_type=F32)
    inner = jnp.sum(probs * grad_probs, axis=-1, keepdims=True)
    grad_scores = (probs * (grad_probs - inner) * HEAD_DIM ** (-0.5)).astype(BF)
    grad_query = jnp.einsum("hqk,khd->qhd", grad_scores, key, preferred_element_type=F32)
    grad_key = jnp.einsum("hqk,qhd->khd", grad_scores, query, preferred_element_type=F32)
    grad_value = jnp.einsum(
        "hqk,qhd->khd", probs.astype(BF), grad_mixed, preferred_element_type=F32
    )
    grad_proj = jnp.concatenate(
        [m.reshape(x.shape).astype(BF) for m in (grad_query, grad_key, grad_value)], axis=1
    )
    grad_norm, gain_one = norm_back(x, norm_scale(x), gains[0], dot_nt(grad_proj, qkv_weight))
    grad_stream = (grad_mid + grad_norm).astype(BF)
    grad_router = jnp.dot(mlp_in.astype(F32).T, grad_logits, precision=EXACT)
    return grad_stream, (attn_in, grad_proj, mixed, grad_low, gain_one, gain_two, grad_router)


def solution(mesh):
    shape = mesh.shape
    n_pipe, n_dp, n_t = shape["pipe"], shape["dp"], shape["tensor"]
    axes = ("pipe", "dp", "tensor")
    plane = ("dp", "tensor")
    n_dev = n_dp * n_t

    def local(
        inputs,
        cotangent,
        dealing,
        routes,
        slot_order,
        doc_lengths,
        attn_weight,
        attn_out_weight,
        expert_in_weight,
        expert_out_weight,
        norm_gains,
        router_weight,
    ):
        dev_rows, width = inputs.shape
        experts = expert_in_weight.shape[1]
        reps = n_dp // experts
        half = dev_rows // n_t
        pack = dev_rows
        cap = pack // experts
        per = dev_rows // n_dev
        pipe = lax.axis_index("pipe")
        dp = lax.axis_index("dp")
        core = lax.axis_index("tensor")
        mine = dp // reps
        rep = dp % reps

        def moved(value, rule):
            pairs = []
            for a in range(n_pipe):
                for b in range(experts):
                    for c in range(reps):
                        for d in range(n_t):
                            to = rule(a, b, c, d)
                            if to is not None:
                                flat = [
                                    ((w * experts + x) * reps + y) * n_t + z
                                    for w, x, y, z in ((a, b, c, d), to)
                                ]
                                pairs.append(tuple(flat))
            return lax.ppermute(value, axes, pairs)

        def swap_core(value):
            return moved(value, lambda a, b, c, d: (a, b, c, 1 - d))

        def pick(blocks, step):
            return lax.dynamic_index_in_dim(blocks, mine ^ step, 0, keepdims=False)

        def exchange(blocks, rule_of=None):
            parts = []
            for step in range(experts):
                block = pick(blocks, step)
                if rule_of is not None:
                    block = moved(block, rule_of(step))
                elif step:
                    block = moved(block, lambda a, b, c, d: (a, b ^ step, c, d))
                parts.append(block)
            return jnp.stack(parts)

        def unswizzle(blocks):
            return jnp.stack([pick(blocks, owner) for owner in range(experts)])

        def rep_groups():
            return [[b * reps + c for c in range(reps)] for b in range(experts)]

        def rep_gather(value):
            if reps == 2:
                other = moved(value, lambda a, b, c, d: (a, b, 1 - c, d))
                both = jnp.stack([value, other])
                return jnp.where(rep == 0, both, both[::-1])
            return lax.all_gather(value, "dp", axis_index_groups=rep_groups())

        def rep_scatter(blocks):
            if reps == 2:
                other = lax.dynamic_index_in_dim(blocks, 1 - rep, 0, keepdims=False).astype(BF)
                kept = lax.dynamic_index_in_dim(blocks, rep, 0, keepdims=False)
                return kept + moved(other, lambda a, b, c, d: (a, b, 1 - c, d)).astype(F32)
            return lax.psum_scatter(
                blocks.astype(BF), "dp", axis_index_groups=rep_groups(), scatter_dimension=0
            ).astype(F32)

        target = dealing // dev_rows
        rows_at = jnp.arange(dev_rows)
        earlier = (target[:, None] == target[None, :]) & (rows_at[None, :] < rows_at[:, None])
        send_slot = target * per + jnp.sum(earlier.astype(jnp.int32), axis=1)
        send_hot = (rows_at[:, None] == send_slot[None, :]).astype(BF)
        small = jnp.concatenate([norm_gains[0].reshape(-1), router_weight[0].reshape(-1)])
        small_high = round_bf(small)
        small_mid = round_bf(small - small_high)
        small_low = round_bf(small - small_high - small_mid)
        small_cols = 3 * small.shape[0] // per
        params = jnp.concatenate([small_high, small_mid, small_low]).astype(BF)
        params = jnp.tile(params.reshape(per, small_cols), (n_dev, 1))
        numbers = jnp.stack(
            [dealing % dev_rows, routes[:, 0], slot_order // 256, slot_order % 256], axis=1
        ).astype(BF)
        payload = jnp.concatenate([jnp.where(pipe == 0, inputs, cotangent), numbers], axis=1)
        payload = dot32(send_hot, payload).astype(BF)
        blank = jnp.zeros((dev_rows, EXTRA - 4 - small_cols), BF)
        payload = jnp.concatenate([payload, params, blank], axis=1)
        dealt = lax.all_to_all(payload, plane, split_axis=0, concat_axis=0, tiled=True)
        small_all = dealt[:, width + 4 : width + 4 + small_cols].astype(F32)
        small_all = small_all.reshape(n_dev, 3, -1)
        small_all = small_all[:, 0] + small_all[:, 1] + small_all[:, 2]
        gain_count = norm_gains.shape[1] * norm_gains.shape[2]
        gains = jnp.swapaxes(small_all[:, :gain_count].reshape(n_dev, 2, -1), 0, 1)
        gains = gains.reshape(2, width)
        router = small_all[:, gain_count:].reshape(width, experts)
        both = lax.all_gather(dealt[:, : width + 4], "tensor", axis=0, tiled=False)
        place = both[:, :, width].astype(jnp.int32)
        row_pos = jnp.arange(n_t)[:, None] * half + place % half
        row_pos = jnp.where(place // half == core, row_pos, -1).reshape(-1)
        place_hot = (jnp.arange(pack)[:, None] == row_pos[None, :]).astype(BF)
        rows = dot32(place_hot, both.reshape(n_t * dev_rows, -1)).astype(BF)
        own_rows = rows[:, :width]
        numbers = rows[:, width:].astype(jnp.int32)
        expert_ids = numbers[:, 1]
        priority = numbers[:, 2] * 256 + numbers[:, 3]

        ends = jnp.cumsum(lax.dynamic_index_in_dim(doc_lengths, core, 0, keepdims=False))
        spots = jnp.arange(pack)
        doc = jnp.sum((spots[:, None] >= ends[None, :]).astype(jnp.int32), axis=1)
        allowed = (doc[:, None] == doc[None, :]) & (spots[None, :] <= spots[:, None])
        same = expert_ids[:, None] == expert_ids[None, :]
        before = priority[None, :] < priority[:, None]
        rank = jnp.sum((same & before).astype(jnp.int32), axis=1)
        slot_of = jnp.where(rank < cap, expert_ids * cap + rank, -1)
        slots = (jnp.arange(experts * cap)[:, None] == slot_of[None, :]).astype(BF)
        onehot = expert_ids[:, None] == jnp.arange(experts)[None, :]
        plan = (slots, onehot, allowed)

        shard, qkv_half = attn_weight.shape[1], attn_weight.shape[3]
        attn_bundle = jnp.concatenate(
            [attn_weight[0].reshape(shard, 3 * qkv_half), attn_out_weight[0].reshape(shard, -1)],
            axis=1,
        )
        attn_mine = lax.all_gather(attn_bundle, "dp", axis=0, tiled=True)
        attn_other = swap_core(attn_mine)
        attn_both = jnp.stack([attn_mine, attn_other])
        attn_both = jnp.where(core == 0, attn_both, attn_both[::-1])
        qkv_weight = attn_both[:, :, : 3 * qkv_half].reshape(n_t, width, 3, qkv_half)
        qkv_weight = qkv_weight.transpose(1, 2, 0, 3).reshape(width, -1)
        out_weight = attn_both[:, :, 3 * qkv_half :].reshape(width, width)
        weights = (qkv_weight, out_weight, gains, router)

        ff_half = expert_in_weight.shape[3]
        in_rows, out_rows = expert_in_weight.shape[2], expert_out_weight.shape[2]
        blocks_in = rep_gather(unswizzle(exchange(expert_in_weight[0])))
        blocks_out = rep_gather(unswizzle(exchange(expert_out_weight[0])))
        w_in = jnp.swapaxes(blocks_in, 0, 1).reshape(width, ff_half)
        w_out = jnp.swapaxes(blocks_out, 0, 1).reshape(ff_half, width)

        def spread(blocks, rule_of=None):
            got = exchange(blocks.reshape(experts, cap, width), rule_of).reshape(-1, width)
            return got

        def with_other(got):
            return jnp.concatenate([got, swap_core(got)], axis=0)

        def folded(partial):
            count = partial.shape[0] // 2
            return (partial[:count] + swap_core(partial[count:].astype(BF)).astype(F32)).astype(BF)

        def returned(values, rule_of=None):
            parts = []
            for step in range(experts):
                block = values[step * cap : (step + 1) * cap]
                if rule_of is not None:
                    block = moved(block, rule_of(step))
                elif step:
                    block = moved(block, lambda a, b, c, d: (a, b ^ step, c, d))
                parts.append(block)
            return unswizzle(jnp.stack(parts)).reshape(-1, width)

        def up(step):
            return lambda a, b, c, d: (1, b ^ step, c, d) if a == 0 else None

        def down(step):
            return lambda a, b, c, d: (0, b ^ step, c, d) if a == 1 else None

        def expert_forward(dispatched):
            pre = dot32(dispatched, w_in)
            act = jax.nn.gelu(pre).astype(BF)
            return pre, act, folded(dot32(act, w_out))

        def expert_backward(grad_slot, pre):
            grad_act = dot_nt(grad_slot, w_out)
            grad_pre = jax.vjp(jax.nn.gelu, pre)[1](grad_act)[0].astype(BF)
            return grad_pre, folded(dot_nt(grad_pre, w_in))

        def merged(mid, gate, expert_slots):
            return (mid + gate * dot_tn(slots, expert_slots)).astype(BF)

        saved = attn_forward(own_rows, weights, plan)
        mid_low, gate_low = saved[0], saved[6]
        got = with_other(spread(saved[7]))
        _, _, expert_slots = expert_forward(got)
        from_first = returned(expert_slots, up)
        mid_up = moved(mid_low, lambda a, b, c, d: (1, b, c, d) if a == 0 else None)
        gate_up = moved(gate_low, lambda a, b, c, d: (1, b, c, d) if a == 0 else None)
        stream = jnp.where(pipe == 0, own_rows, merged(mid_up, gate_up, from_first))

        saved = attn_forward(stream, weights, plan)
        mid, gate = saved[0], saved[6]
        dispatched = with_other(spread(saved[7]))
        pre, act, expert_slots = expert_forward(dispatched)
        expert_slots = returned(expert_slots)
        layer_out = merged(mid, gate, expert_slots)

        def slotted(gate_now, grad):
            return dot32(slots, (gate_now * grad.astype(F32)).astype(BF)).astype(BF)

        grad_got = spread(slotted(gate, own_rows))
        _, grad_disp = expert_backward(with_other(grad_got), pre)
        grad_stream, _ = attn_backward(
            own_rows, returned(grad_disp), expert_slots, stream, saved, weights, plan
        )
        grad_down = moved(grad_stream, lambda a, b, c, d: (0, b, c, d) if a == 1 else None)
        got_down = spread(slotted(gate_up, grad_stream), down)

        grad_out = jnp.where(pipe == 0, grad_down, own_rows)
        grad_got = with_other(jnp.where(pipe == 0, got_down, grad_got))
        grad_pre, grad_disp = expert_backward(grad_got, pre)
        grad_w_in = dot_tn(dispatched, grad_pre)
        grad_w_out = dot_tn(act, grad_got)
        layer_grad, record = attn_backward(
            grad_out, returned(grad_disp), expert_slots, stream, saved, weights, plan
        )

        def to_owner(grad, rows_each):
            blocks = grad.reshape(experts, reps, rows_each, -1)
            summed = rep_scatter(jnp.swapaxes(blocks, 0, 1))
            own = pick(summed, 0)
            parts = [own]
            for step in range(1, experts):
                block = pick(summed, step).astype(BF)
                parts.append(moved(block, lambda a, b, c, d: (a, b ^ step, c, d)).astype(F32))
            return unswizzle(jnp.stack(parts))[None]

        grad_expert_in = to_owner(grad_w_in, in_rows)
        grad_expert_out = to_owner(grad_w_out, out_rows)

        attn_in, grad_proj, mixed, grad_low, gain_one, gain_two, grad_router = record
        grad_qkv = dot_tn(attn_in, grad_proj).reshape(n_dp, shard, 3, n_t, qkv_half)
        grad_qkv = grad_qkv.transpose(3, 0, 1, 2, 4).reshape(n_t, n_dp, shard * 3, qkv_half)
        grad_o = dot_tn(mixed, grad_low).reshape(n_t, n_dp, -1, qkv_half)
        tiny = jnp.concatenate(
            [
                jnp.stack([gain_one, gain_two]).reshape(2, n_dp, n_t, -1).transpose(2, 1, 0, 3).reshape(n_t, n_dp, -1),
                grad_router.reshape(n_dp, n_t, -1).transpose(1, 0, 2),
            ],
            axis=2,
        )
        tiny_count = tiny.shape[2]
        tiny = jnp.pad(tiny, ((0, 0), (0, 0), (0, 16 * qkv_half - tiny_count)))
        tiny = tiny.reshape(n_t, n_dp, 16, qkv_half)
        bundle = jnp.concatenate([grad_qkv, grad_o, tiny], axis=2)
        kept = lax.dynamic_index_in_dim(bundle, core, 0, keepdims=False)
        other = lax.dynamic_index_in_dim(bundle, 1 - core, 0, keepdims=False).astype(BF)
        bundle = kept + swap_core(other).astype(F32)
        bundle = bundle.reshape((experts, reps) + bundle.shape[1:])
        bundle = rep_scatter(jnp.swapaxes(bundle, 0, 1))
        total = pick(bundle, 0)
        for step in range(1, experts):
            block = pick(bundle, step).astype(BF)
            total = total + moved(block, lambda a, b, c, d: (a, b ^ step, c, d)).astype(F32)
        qkv_rows = shard * 3
        grad_attn = total[:qkv_rows].reshape(1, shard, 3, qkv_half)
        grad_attn_out = total[qkv_rows:-16].reshape(1, -1, width)
        tiny = total[-16:].reshape(-1)[:tiny_count]
        grad_gains = tiny[:gain_count].reshape(1, 2, -1)
        grad_router = tiny[gain_count:].reshape(1, -1, experts)

        def sent_back(values):
            spread_out = dot_tn(place_hot, values).astype(BF).reshape(n_t, dev_rows, width)
            own = lax.dynamic_index_in_dim(spread_out, core, 0, keepdims=False)
            other = lax.dynamic_index_in_dim(spread_out, 1 - core, 0, keepdims=False)
            full = own + swap_core(other)
            back = lax.all_to_all(full, plane, split_axis=0, concat_axis=0, tiled=True)
            return dot_tn(send_hot, back).astype(BF)[None]

        return (
            sent_back(layer_out),
            sent_back(layer_grad),
            grad_attn,
            grad_attn_out,
            grad_expert_in,
            grad_expert_out,
            grad_gains,
            grad_router,
        )

    in_specs = (
        P(("dp", "tensor"), None),
        P(("dp", "tensor"), None),
        P(("dp", "tensor")),
        P(("dp", "tensor"), None),
        P(("dp", "tensor")),
        P("dp", None),
        P("pipe", "dp", None, "tensor"),
        P("pipe", ("tensor", "dp"), None),
        P("pipe", None, "dp", "tensor"),
        P("pipe", None, ("tensor", "dp"), None),
        P("pipe", None, ("dp", "tensor")),
        P("pipe", ("dp", "tensor"), None),
    )
    out_specs = (
        P("pipe", ("dp", "tensor"), None),
        P("pipe", ("dp", "tensor"), None),
        P("pipe", "dp", None, "tensor"),
        P("pipe", ("tensor", "dp"), None),
        P("pipe", None, "dp", "tensor"),
        P("pipe", None, ("tensor", "dp"), None),
        P("pipe", None, ("dp", "tensor")),
        P("pipe", ("dp", "tensor"), None),
    )
    return jax.shard_map(local, mesh=mesh, in_specs=in_specs, out_specs=out_specs, check_vma=False)
```

time: 1670 us -> 618 us (0.37)
  waiting for transfers between devices: 1110 us -> 198 us
  blocking collectives: 114 us -> 5.18 us
  starting transfers between devices: 43.1 us -> 145 us
  matrix products: 186 us -> 116 us
  other arithmetic: 85.7 us -> 47.9 us
    reduce_scatter x16 -> x0, waiting for transfers between devices: 825 us -> none  [the longest x1 317 us: local(): lax.psum_scatter(grad_sum[2], 'dp', scatter_dimension=1, tiled=True)]
    all_gather x3 -> x1, waiting for transfers between devices: 218 us -> 0.02 us  [local(): attn_mine = lax.all_gather(attn_bundle, 'dp', axis=0, tiled=True)]
    ppermute x4 -> x61, waiting for transfers between devices: 21 us -> 198 us  [moved(): return lax.ppermute(value, axes, pairs)]
    ppermute x4 -> x61, starting transfers between devices: 9.82 us -> 129 us  [moved(): return lax.ppermute(value, axes, pairs)]
    all_gather x17 -> x1, blocking collectives: 114 us -> 5.18 us  [local(): both = lax.all_gather(dealt[:, :width + 4], 'tensor', axis=0, tiled=False)]
    dot_general x61 -> x47, matrix products: 186 us -> 108 us  [the longest x7 25.8 us: dot_nt(): lax.dot_general(a, b, (((1,), (1,)), ((), ())), preferred_element_type=F32)]
    gather x25 -> x0, local copies, waits for them, and re-layouts: 42 us -> none  [the longest x3 6.48 us: layer_forward(): token_out = jnp.where(is_kept[:, None], expert_out[where_slot], 0.0)]
    unnamed x23 -> x1, waiting for transfers between devices: 38.2 us -> 0.02 us
  transfers between devices with their start and end apart: 32 -> 65, of which waited for: 23 -> 26; matrix products, arithmetic and copies ran while one was open for 11% -> 29% of each run, Pallas kernels for 0% -> 0%
where the time goes in v1:
time: 618 us; the launch traced here: 612 us
  waiting for transfers between devices  198 us (32%)
  starting transfers between devices  145 us (23%)
  matrix products  116 us (19%)
  local copies, waits for them, and re-layouts  83.8 us (14%)
  other arithmetic  47.9 us (8%)
  between operations  16.5 us (3%)
    ppermute x61, waiting for transfers between devices, moved(): return lax.ppermute(value, axes, pairs)  198 us
    ppermute x61, starting transfers between devices, moved(): return lax.ppermute(value, axes, pairs)  129 us
    dot_general x7, matrix products, dot_nt(): lax.dot_general(a, b, (((1,), (1,)), ((), ())), preferred_element_type=F32)  25.8 us
    dot_general x13, matrix products, dot32(): return jnp.dot(a, b, preferred_element_type=F32)  17.6 us
    dot_general x12, matrix products, dot_tn(): lax.dot_general(a, b, (((0,), (0,)), ((), ())), preferred_element_type=F32)  16.9 us
    reshape x2, local copies, waits for them, and re-layouts, local(): grad_qkv = dot_tn(attn_in, grad_proj).reshape(n_dp, shard, 3, n_t, qkv_half)  16.6 us
    unnamed x188, local copies, waits for them, and re-layouts  15.8 us
    dot_general x2, matrix products, attn_backward(): jnp.einsum('hqk,qhd->khd', grad_scores, query, preferred_element_type=F32)  13.3 us
  transfers between devices with their start and end apart: 65, of which 26 were waited for; matrix products, arithmetic and copies ran while one was open for 29% of the time, Pallas kernels for 0%

profile of v1, /device:TPU:0, one launch (start us, length us, event | category | flops | bytes accessed | tf_op | source)
XLA Modules:
  0.0 612.4 jit_solution(2650212788513595906)
XLA Ops:
  16.1 7.4 %all-to-all-start = ((bf16[16,16,896]{2,1,0:T(8,128)(2,1)}), bf16[16,16,896]{2,1,0:T(8,128)(2,1)S(1)}, u32[]{:S(2)}, u32[]{:S(2)}) async-start(bf16[16,16,896]{2,1,0:T(8,128)(2,1)} %maximum_maximum_fusion), calls=%async_computation | async-start | bytes 917504 | tf_op jit(solution)/shard_map/all_to_all | solution.py:217
  24.4 3.7 collective-permute-start.13
  30.2 3.7 collective-permute-start.9
  35.0 14.6 %collective-permute-done.13 = bf16[192,768]{1,0:T(8,128)(2,1)S(1)} collective-permute-done((bf16[192,768]{1,0:T(8,128)(2,1)}, bf16[192,768]{1,0:T(8,128)(2,1)S(1)}, u32[]{:S(2)}, u32[]{:S(2)}) %collective-permute-start.13) | collective-permute-done | bytes 294944 | tf_op jit(solution)/shard_map/ppermute | solution.py:157
  49.6 32.1 %collective-permute-start.7 = (bf16[96,1536]{1,0:T(8,128)(2,1)S(1)}, bf16[96,1536]{1,0:T(8,128)(2,1)S(1)}, u32[]{:S(2)}, u32[]{:S(2)}) collective-permute-start(bf16[96,1536]{1,0:T(8,128)(2,1)S(1)} %get-tuple-element.75), channel_id=1, source_target_pairs={{0,4},{1,5},{2,6},{3,7},{4,0},{5,1},{6,2},{7,3},{8,12},{9,13},{10,... | collective-permute-start | bytes 884744 | tf_op jit(solution)/shard_map/ppermute | solution.py:157
  81.7 18.5 %collective-permute-done.12 = bf16[192,768]{1,0:T(8,128)(2,1)S(1)} collective-permute-done((bf16[192,768]{1,0:T(8,128)(2,1)}, bf16[192,768]{1,0:T(8,128)(2,1)S(1)}, u32[]{:S(2)}, u32[]{:S(2)}) %collective-permute-start.12) | collective-permute-done | bytes 294944 | tf_op jit(solution)/shard_map/ppermute | solution.py:157
  103.4 10.9 %collective-permute-done.8 = bf16[96,1536]{1,0:T(8,128)(2,1)S(1)} collective-permute-done((bf16[96,1536]{1,0:T(8,128)(2,1)S(1)}, bf16[96,1536]{1,0:T(8,128)(2,1)S(1)}, u32[]{:S(2)}, u32[]{:S(2)}) %collective-permute-start.8) | collective-permute-done | bytes 294944 | tf_op jit(solution)/shard_map/ppermute | solution.py:157
  117.6 5.2 all-gather
  125.3 29.1 %collective-permute-done.10 = bf16[4,96,1536]{2,1,0:T(8,128)(2,1)} collective-permute-done((bf16[4,96,1536]{2,1,0:T(8,128)(2,1)}, bf16[4,96,1536]{2,1,0:T(8,128)(2,1)}, u32[]{:S(2)}, u32[]{:S(2)}) %collective-permute-start.10) | collective-permute-done | bytes 1179680 | tf_op jit(solution)/shard_map/ppermute | solution.py:157
  154.3 2.9 pad_maximum_fusion.2
  163.6 5.8 copy.230
  175.2 3.8 fusion.256
  182.5 3.0 collective-permute-start.5
  189.2 3.5 collective-permute-done.4
  196.2 6.3 %fusion.44 = f32[512,768]{1,0:T(8,128)} fusion(bf16[1536,768]{1,0:T(8,128)(2,1)} %bitcast.356, bf16[768,1536]{1,0:T(8,128)(2,1)} %bitcast.352, bf16[256,768]{1,0:T(8,128)(2,1)S(1)} %collective-permute-done.6, bf16[256,768]{1,0:T(8,128)(2,1)S(1)} %bitcast.401), kind=kOutput, calls=%fused_computation.85 | convolution fusion | flops 2424569856 | bytes 7077888 | tf_op jit(solution)/shard_map/dot_general | solution.py:16
  206.6 3.4 collective-permute-start.1
  212.6 2.6 collective-permute-start.19
  219.2 5.5 collective-permute-start.2
  224.6 10.7 %collective-permute-done.16 = bf16[64,768]{1,0:T(8,128)(2,1)S(1)} collective-permute-done((bf16[64,768]{1,0:T(8,128)(2,1)S(1)}, bf16[64,768]{1,0:T(8,128)(2,1)S(1)}, u32[]{:S(2)}, u32[]{:S(2)}) %collective-permute-start.16) | collective-permute-done | bytes 98336 | tf_op jit(solution)/shard_map/ppermute | solution.py:157
  241.6 4.0 fusion.258
  255.7 2.5 collective-permute-done.22
  258.3 3.4 collective-permute-done.21
  264.4 2.9 collective-permute-start.29
  267.3 3.3 collective-permute-done.31
  270.6 3.7 collective-permute-done.30
  276.2 3.4 fusion.128
  283.4 8.5 %fusion.49 = f32[512,768]{1,0:T(8,128)} fusion(bf16[768,1536]{1,0:T(8,128)(2,1)} %bitcast.354, f32[512,1536]{1,0:T(8,128)} %copy-done.79, bf16[1536,768]{1,0:T(8,128)(2,1)} %bitcast.357, bf16[256,768]{1,0:T(8,128)(2,1)} %collective-permute-done.32, bf16[256,768]{1,0:T(8,128)(2,1)S(1)} %bitcast.370), kind=kOutput, calls=%fused_computation.89 | convolution fusion | flops 2433220608 | bytes 10223616 | tf_op jit(solution)/shard_map/dot_general | solution.py:20
  296.2 2.9 collective-permute-start.25
  303.7 2.8 collective-permute-done.26
  308.6 5.8 collective-permute-done.35
  319.9 3.4 convolution_convert_fusion.10
  325.5 6.6 %fusion.63 = bf16[12,64,256]{2,1,0:T(8,128)(2,1)} fusion(bf16[256,12,64]{0,2,1:T(8,128)(2,1)} %bitcast.395, f32[12,256,256]{1,2,0:T(8,128)} %fusion.260, f32[12,256,256]{1,2,0:T(8,128)} %get-tuple-element.161, f32[12,256]{1,0:T(8,128)} %copy-done.81), kind=kOutput, calls=%fused_computation.105 | convolution fusion | flops 106368256 | bytes 7090176 | tf_op jit(solution)/shard_map/hqk,qhd->khd/dot_general | solution.py:97
  332.1 6.6 %fusion.60 = bf16[12,64,256]{2,1,0:T(8,128)(2,1)} fusion(bf16[256,12,64]{0,2,1:T(8,128)(2,1)} %bitcast.398, f32[12,256,256]{1,2,0:T(8,128)} %fusion.260, f32[12,256,256]{1,2,0:T(8,128)} %get-tuple-element.161, f32[12,256]{1,0:T(8,128)} %copy-done.81), kind=kOutput, calls=%fused_computation.104 | convolution fusion | flops 106368256 | bytes 7090176 | tf_op jit(solution)/shard_map/hqk,khd->qhd/dot_general | solution.py:96
  339.9 4.3 fusion.94
  357.2 2.7 collective-permute-done.40
  369.4 4.4 all-to-all-start.1
  378.0 6.1 add_convert_fusion
  386.0 2.6 fusion.127
  393.4 3.4 fusion.125
  396.9 3.4 collective-permute-start.46
  404.5 4.6 collective-permute-done.45
  413.2 3.3 convolution_convert_fusion.7
  416.5 2.3 fusion.262
  418.8 6.7 %fusion.57 = bf16[12,64,256]{2,1,0:T(8,128)(2,1)} fusion(bf16[256,12,64]{0,2,1:T(8,128)(2,1)S(1)} %bitcast.396, f32[12,256,256]{1,2,0:T(8,128)} %fusion.262, f32[12,256,256]{1,2,0:T(8,128)} %get-tuple-element.161, f32[12,256]{1,0:T(8,128)S(1)} %copy-done.82), kind=kOutput, calls=%fused_computation.103 | convolution fusion | flops 106368256 | bytes 7090176 | tf_op jit(solution)/shard_map/hqk,qhd->khd/dot_general | solution.py:97
  425.5 6.5 %fusion.54 = bf16[12,64,256]{2,1,0:T(8,128)(2,1)} fusion(bf16[256,12,64]{0,2,1:T(8,128)(2,1)S(1)} %bitcast.399, f32[12,256,256]{1,2,0:T(8,128)} %fusion.262, f32[12,256,256]{1,2,0:T(8,128)} %get-tuple-element.161, f32[12,256]{1,0:T(8,128)S(1)} %copy-done.83), kind=kOutput, calls=%fused_computation.102 | convolution fusion | flops 106368256 | bytes 7090176 | tf_op jit(solution)/shard_map/hqk,khd->qhd/dot_general | solution.py:96
  433.4 3.7 fusion.97
  437.1 4.0 fusion.129
  446.7 3.0 copy.270
  449.7 9.5 %reshape.502 = f32[8,96,3,2,384]{4,3,2,1,0:T(2,128)} reshape(f32[768,2304]{1,0:T(8,128)} %fusion.129) | data formatting | bytes 14155776 | tf_op jit(solution)/shard_map/reshape | solution.py:360
  459.3 7.1 %copy.264 = f32[8,96,3,2,384]{4,0,2,1,3:T(8,128)S(1)} copy(f32[8,96,3,2,384]{4,3,2,1,0:T(2,128)} %reshape.502) | data formatting | bytes 14155776 | tf_op jit(solution)/shard_map/reshape | solution.py:360
  469.6 2.5 constant_dynamic-slice_fusion.10
  475.1 3.8 all-to-all-start.2
  478.9 2.5 bitcast_add_fusion.3
  481.5 3.8 collective-permute-start.56
  488.4 3.3 collective-permute-start.60
  491.7 5.2 collective-permute-done.56
  497.0 20.7 %collective-permute-start.59 = (bf16[192,768]{1,0:T(8,128)(2,1)S(1)}, bf16[192,768]{1,0:T(8,128)(2,1)S(1)}, u32[]{:S(2)}, u32[]{:S(2)}) collective-permute-start(bf16[192,768]{1,0:T(8,128)(2,1)S(1)} %get-tuple-element.57), channel_id=1, source_target_pairs={{0,8},{1,9},{2,10},{3,11},{4,12},{5,13},{6,14},{7,15},{8,0},{9,1},... | collective-permute-start | bytes 884744 | tf_op jit(solution)/shard_map/ppermute | solution.py:157
  517.8 12.0 %collective-permute-done.55 = bf16[96,1536]{1,0:T(8,128)(2,1)S(1)} collective-permute-done((bf16[96,1536]{1,0:T(8,128)(2,1)S(1)}, bf16[96,1536]{1,0:T(8,128)(2,1)S(1)}, u32[]{:S(2)}, u32[]{:S(2)}) %collective-permute-start.55) | collective-permute-done | bytes 294944 | tf_op jit(solution)/shard_map/ppermute | solution.py:157
  529.9 12.2 %collective-permute-done.59 = bf16[192,768]{1,0:T(8,128)(2,1)S(1)} collective-permute-done((bf16[192,768]{1,0:T(8,128)(2,1)S(1)}, bf16[192,768]{1,0:T(8,128)(2,1)S(1)}, u32[]{:S(2)}, u32[]{:S(2)}) %collective-permute-start.59) | collective-permute-done | bytes 294944 | tf_op jit(solution)/shard_map/ppermute | solution.py:157
  542.2 2.6 bitcast_add_fusion
  548.6 24.9 %collective-permute-done.49 = bf16[4,400,384]{2,1,0:T(8,128)(2,1)S(1)} collective-permute-done((bf16[4,400,384]{2,1,0:T(8,128)(2,1)S(1)}, bf16[4,400,384]{2,1,0:T(8,128)(2,1)S(1)}, u32[]{:S(2)}, u32[]{:S(2)}) %collective-permute-start.49) | collective-permute-done | bytes 1228832 | tf_op jit(solution)/shard_map/ppermute | solution.py:157
  576.2 2.9 collective-permute-start.50
  581.9 5.1 collective-permute-done.52
  587.0 13.7 %collective-permute-done.51 = bf16[400,384]{1,0:T(8,128)(2,1)S(1)} collective-permute-done((bf16[400,384]{1,0:T(8,128)(2,1)}, bf16[400,384]{1,0:T(8,128)(2,1)S(1)}, u32[]{:S(2)}, u32[]{:S(2)}) %collective-permute-start.51) | collective-permute-done | bytes 307232 | tf_op jit(solution)/shard_map/ppermute | solution.py:157
  (489 shorter events, 170.7 us)
Async XLA Ops:
  7.2 110.3 %all-gather.3.cloned.1.call-start = ((), (), s32[]{:S(2)}) async-start(), calls=%async_computation.3 | async-start | bytes 2654208 | tf_op jit(solution)/shard_map/all_gather | solution.py:253
  16.1 101.2 %all-to-all-start = ((bf16[16,16,896]{2,1,0:T(8,128)(2,1)}), bf16[16,16,896]{2,1,0:T(8,128)(2,1)S(1)}, u32[]{:S(2)}, u32[]{:S(2)}) async-start(bf16[16,16,896]{2,1,0:T(8,128)(2,1)} %maximum_maximum_fusion), calls=%async_computation | async-start | bytes 917504 | tf_op jit(solution)/shard_map/all_to_all | solution.py:217
  24.4 25.2 %collective-permute-start.13 = (bf16[192,768]{1,0:T(8,128)(2,1)}, bf16[192,768]{1,0:T(8,128)(2,1)S(1)}, u32[]{:S(2)}, u32[]{:S(2)}) collective-permute-start(bf16[192,768]{1,0:T(8,128)(2,1)} %get-tuple-element.86), channel_id=1, source_target_pairs={{0,12},{1,13},{2,14},{3,15},{4,8},{5,9},{6,10},{7,11},{8,4},{9,5},... | collective-permute-start | bytes 884744 | tf_op jit(solution)/shard_map/ppermute | solution.py:157
  28.1 72.1 %collective-permute-start.12 = (bf16[192,768]{1,0:T(8,128)(2,1)}, bf16[192,768]{1,0:T(8,128)(2,1)S(1)}, u32[]{:S(2)}, u32[]{:S(2)}) collective-permute-start(bf16[192,768]{1,0:T(8,128)(2,1)} %get-tuple-element.87), channel_id=1, source_target_pairs={{0,8},{1,9},{2,10},{3,11},{4,12},{5,13},{6,14},{7,15},{8,0},{9,1},... | collective-permute-start | bytes 884744 | tf_op jit(solution)/shard_map/ppermute | solution.py:157
  28.1 72.1 %collective-permute-start.11 = (bf16[192,768]{1,0:T(8,128)(2,1)}, bf16[192,768]{1,0:T(8,128)(2,1)S(1)}, u32[]{:S(2)}, u32[]{:S(2)}) collective-permute-start(bf16[192,768]{1,0:T(8,128)(2,1)} %get-tuple-element.85), channel_id=1, source_target_pairs={{0,4},{1,5},{2,6},{3,7},{4,0},{5,1},{6,2},{7,3},{8,12},{9,13},{10,... | collective-permute-start | bytes 884744 | tf_op jit(solution)/shard_map/ppermute | solution.py:157
  30.2 73.2 %collective-permute-start.9 = (bf16[96,1536]{1,0:T(8,128)(2,1)S(1)}, bf16[96,1536]{1,0:T(8,128)(2,1)S(1)}, u32[]{:S(2)}, u32[]{:S(2)}) collective-permute-start(bf16[96,1536]{1,0:T(8,128)(2,1)S(1)} %get-tuple-element.76), channel_id=1, source_target_pairs={{0,12},{1,13},{2,14},{3,15},{4,8},{5,9},{6,10},{7,11},{8,4},{9,5},... | collective-permute-start | bytes 884744 | tf_op jit(solution)/shard_map/ppermute | solution.py:157
  33.9 80.4 %collective-permute-start.8 = (bf16[96,1536]{1,0:T(8,128)(2,1)S(1)}, bf16[96,1536]{1,0:T(8,128)(2,1)S(1)}, u32[]{:S(2)}, u32[]{:S(2)}) collective-permute-start(bf16[96,1536]{1,0:T(8,128)(2,1)S(1)} %get-tuple-element.77), channel_id=1, source_target_pairs={{0,8},{1,9},{2,10},{3,11},{4,12},{5,13},{6,14},{7,15},{8,0},{9,1},... | collective-permute-start | bytes 884744 | tf_op jit(solution)/shard_map/ppermute | solution.py:157
  49.6 64.7 %collective-permute-start.7 = (bf16[96,1536]{1,0:T(8,128)(2,1)S(1)}, bf16[96,1536]{1,0:T(8,128)(2,1)S(1)}, u32[]{:S(2)}, u32[]{:S(2)}) collective-permute-start(bf16[96,1536]{1,0:T(8,128)(2,1)S(1)} %get-tuple-element.75), channel_id=1, source_target_pairs={{0,4},{1,5},{2,6},{3,7},{4,0},{5,1},{6,2},{7,3},{8,12},{9,13},{10,... | collective-permute-start | bytes 884744 | tf_op jit(solution)/shard_map/ppermute | solution.py:157
  102.0 90.8 %collective-permute-start.14 = (bf16[4,192,768]{2,1,0:T(8,128)(2,1)}, bf16[4,192,768]{2,1,0:T(8,128)(2,1)}, u32[]{:S(2)}, u32[]{:S(2)}) collective-permute-start(bf16[4,192,768]{2,1,0:T(8,128)(2,1)} %get-tuple-element.79), channel_id=1, source_target_pairs={{0,2},{1,3},{2,0},{3,1},{4,6},{5,7},{6,4},{7,5},{8,10},{9,11},{10,... | collective-permute-start | bytes 3538952 | tf_op jit(solution)/shard_map/ppermute | solution.py:157
  115.7 38.6 %collective-permute-start.10 = (bf16[4,96,1536]{2,1,0:T(8,128)(2,1)}, bf16[4,96,1536]{2,1,0:T(8,128)(2,1)}, u32[]{:S(2)}, u32[]{:S(2)}) collective-permute-start(bf16[4,96,1536]{2,1,0:T(8,128)(2,1)} %get-tuple-element.69), channel_id=1, source_target_pairs={{0,2},{1,3},{2,0},{3,1},{4,6},{5,7},{6,4},{7,5},{8,10},{9,11},{10,... | collective-permute-start | bytes 3538952 | tf_op jit(solution)/shard_map/ppermute | solution.py:157
  117.5 39.7 %collective-permute-start = (bf16[768,1536]{1,0:T(8,128)(2,1)}, bf16[768,1536]{1,0:T(8,128)(2,1)}, u32[]{:S(2)}, u32[]{:S(2)}) collective-permute-start(bf16[768,1536]{1,0:T(8,128)(2,1)} %all-gather.3.cloned.1.call-done), channel_id=1, source_target_pairs={{0,1},{1,0},{2,3},{3,2},{4,5},{5,4},{6,7},{7,6},{8,9},{9,8},{10,11... | collective-permute-start | bytes 7077896 | tf_op jit(solution)/shard_map/ppermute | solution.py:157
  182.5 6.7 %collective-permute-start.5 = (bf16[64,768]{1,0:T(8,128)(2,1)S(1)}, bf16[64,768]{1,0:T(8,128)(2,1)S(1)}, u32[]{:S(2)}, u32[]{:S(2)}) collective-permute-start(bf16[64,768]{1,0:T(8,128)(2,1)S(1)} %get-tuple-element.136), channel_id=1, source_target_pairs={{0,12},{1,13},{2,14},{3,15},{4,8},{5,9},{6,10},{7,11},{8,4},{9,5},... | collective-permute-start | bytes 294920 | tf_op jit(solution)/shard_map/ppermute | solution.py:157
  185.5 7.2 %collective-permute-start.4 = (bf16[64,768]{1,0:T(8,128)(2,1)S(1)}, bf16[64,768]{1,0:T(8,128)(2,1)S(1)}, u32[]{:S(2)}, u32[]{:S(2)}) collective-permute-start(bf16[64,768]{1,0:T(8,128)(2,1)S(1)} %get-tuple-element.137), channel_id=1, source_target_pairs={{0,8},{1,9},{2,10},{3,11},{4,12},{5,13},{6,14},{7,15},{8,0},{9,1},... | collective-permute-start | bytes 294920 | tf_op jit(solution)/shard_map/ppermute | solution.py:157
  185.5 7.2 %collective-permute-start.3 = (bf16[64,768]{1,0:T(8,128)(2,1)S(1)}, bf16[64,768]{1,0:T(8,128)(2,1)S(1)}, u32[]{:S(2)}, u32[]{:S(2)}) collective-permute-start(bf16[64,768]{1,0:T(8,128)(2,1)S(1)} %get-tuple-element.138), channel_id=1, source_target_pairs={{0,4},{1,5},{2,6},{3,7},{4,0},{5,1},{6,2},{7,3},{8,12},{9,13},{10,... | collective-permute-start | bytes 294920 | tf_op jit(solution)/shard_map/ppermute | solution.py:157
  203.7 7.6 %collective-permute-start.15 = (bf16[256,768]{1,0:T(8,128)(2,1)S(1)}, bf16[256,768]{1,0:T(8,128)(2,1)S(1)}, u32[]{:S(2)}, u32[]{:S(2)}) collective-permute-start(bf16[256,768]{1,0:T(8,128)(2,1)S(1)} %slice.341), channel_id=1, source_target_pairs={{0,1},{1,0},{2,3},{3,2},{4,5},{5,4},{6,7},{7,6},{8,9},{9,8},{10,11... | collective-permute-start | bytes 1179656 | tf_op jit(solution)/shard_map/ppermute | solution.py:157
  206.6 28.9 %collective-permute-start.1 = (f32[256,768]{0,1:T(8,128)S(1)}, f32[256,768]{0,1:T(8,128)S(1)}, u32[]{:S(2)}, u32[]{:S(2)}) collective-permute-start(f32[256,768]{0,1:T(8,128)S(1)} %get-tuple-element.155), channel_id=1, source_target_pairs={{0,16},{1,17},{2,18},{3,19},{4,20},{5,21},{6,22},{7,23},{8,24},{9,... | collective-permute-start | bytes 2359304 | tf_op jit(solution)/shard_map/ppermute | solution.py:157
  212.6 6.6 %collective-permute-start.19 = (bf16[64,768]{1,0:T(8,128)(2,1)S(1)}, bf16[64,768]{1,0:T(8,128)(2,1)S(1)}, u32[]{:S(2)}, u32[]{:S(2)}) collective-permute-start(bf16[64,768]{1,0:T(8,128)(2,1)S(1)} %get-tuple-element.132), channel_id=1, source_target_pairs={{0,28},{1,29},{2,30},{3,31},{4,24},{5,25},{6,26},{7,27},{8,20},{9,... | collective-permute-start | bytes 294920 | tf_op jit(solution)/shard_map/ppermute | solution.py:157
  215.2 9.4 %collective-permute-start.18 = (bf16[64,768]{1,0:T(8,128)(2,1)S(1)}, bf16[64,768]{1,0:T(8,128)(2,1)S(1)}, u32[]{:S(2)}, u32[]{:S(2)}) collective-permute-start(bf16[64,768]{1,0:T(8,128)(2,1)S(1)} %get-tuple-element.133), channel_id=1, source_target_pairs={{0,24},{1,25},{2,26},{3,27},{4,28},{5,29},{6,30},{7,31},{8,16},{9,... | collective-permute-start | bytes 294920 | tf_op jit(solution)/shard_map/ppermute | solution.py:157
  216.5 8.1 %collective-permute-start.17 = (bf16[64,768]{1,0:T(8,128)(2,1)S(1)}, bf16[64,768]{1,0:T(8,128)(2,1)S(1)}, u32[]{:S(2)}, u32[]{:S(2)}) collective-permute-start(bf16[64,768]{1,0:T(8,128)(2,1)S(1)} %get-tuple-element.134), channel_id=1, source_target_pairs={{0,20},{1,21},{2,22},{3,23},{4,16},{5,17},{6,18},{7,19},{8,28},{9,... | collective-permute-start | bytes 294920 | tf_op jit(solution)/shard_map/ppermute | solution.py:157
  217.8 17.5 %collective-permute-start.16 = (bf16[64,768]{1,0:T(8,128)(2,1)S(1)}, bf16[64,768]{1,0:T(8,128)(2,1)S(1)}, u32[]{:S(2)}, u32[]{:S(2)}) collective-permute-start(bf16[64,768]{1,0:T(8,128)(2,1)S(1)} %get-tuple-element.131), channel_id=1, source_target_pairs={{0,16},{1,17},{2,18},{3,19},{4,20},{5,21},{6,22},{7,23},{8,24},{9,... | collective-permute-start | bytes 294920 | tf_op jit(solution)/shard_map/ppermute | solution.py:157
  219.2 16.4 %collective-permute-start.2 = (f32[256,1]{0,1:T(1,128)S(1)}, f32[256,1]{0,1:T(1,128)S(1)}, u32[]{:S(2)}, u32[]{:S(2)}) collective-permute-start(f32[256,1]{0,1:T(1,128)S(1)} %bitcast.451), channel_id=1, source_target_pairs={{0,16},{1,17},{2,18},{3,19},{4,20},{5,21},{6,22},{7,23},{8,24},{9,... | collective-permute-start | bytes 3080 | tf_op jit(solution)/shard_map/ppermute | solution.py:157
  250.6 7.6 %collective-permute-start.22 = (bf16[64,768]{1,0:T(8,128)(2,1)S(1)}, bf16[64,768]{1,0:T(8,128)(2,1)S(1)}, u32[]{:S(2)}, u32[]{:S(2)}) collective-permute-start(bf16[64,768]{1,0:T(8,128)(2,1)S(1)} %get-tuple-element.124), channel_id=1, source_target_pairs={{0,12},{1,13},{2,14},{3,15},{4,8},{5,9},{6,10},{7,11},{8,4},{9,5},... | collective-permute-start | bytes 294920 | tf_op jit(solution)/shard_map/ppermute | solution.py:157
  252.4 9.3 %collective-permute-start.21 = (bf16[64,768]{1,0:T(8,128)(2,1)S(1)}, bf16[64,768]{1,0:T(8,128)(2,1)S(1)}, u32[]{:S(2)}, u32[]{:S(2)}) collective-permute-start(bf16[64,768]{1,0:T(8,128)(2,1)S(1)} %get-tuple-element.125), channel_id=1, source_target_pairs={{0,8},{1,9},{2,10},{3,11},{4,12},{5,13},{6,14},{7,15},{8,0},{9,1},... | collective-permute-start | bytes 294920 | tf_op jit(solution)/shard_map/ppermute | solution.py:157
  252.9 8.8 %collective-permute-start.20 = (bf16[64,768]{1,0:T(8,128)(2,1)S(1)}, bf16[64,768]{1,0:T(8,128)(2,1)S(1)}, u32[]{:S(2)}, u32[]{:S(2)}) collective-permute-start(bf16[64,768]{1,0:T(8,128)(2,1)S(1)} %get-tuple-element.126), channel_id=1, source_target_pairs={{0,4},{1,5},{2,6},{3,7},{4,0},{5,1},{6,2},{7,3},{8,12},{9,13},{10,... | collective-permute-start | bytes 294920 | tf_op jit(solution)/shard_map/ppermute | solution.py:157
  261.7 14.4 %collective-permute-start.23 = (bf16[256,768]{1,0:T(8,128)(2,1)S(1)}, bf16[256,768]{1,0:T(8,128)(2,1)}, u32[]{:S(2)}, u32[]{:S(2)}) collective-permute-start(bf16[256,768]{1,0:T(8,128)(2,1)S(1)} %bitcast.366), channel_id=1, source_target_pairs={{0,1},{1,0},{2,3},{3,2},{4,5},{5,4},{6,7},{7,6},{8,9},{9,8},{10,11... | collective-permute-start | bytes 1179656 | tf_op jit(solution)/shard_map/ppermute | solution.py:157
  262.9 7.7 %collective-permute-start.31 = (bf16[64,768]{1,0:T(8,128)(2,1)}, bf16[64,768]{1,0:T(8,128)(2,1)S(1)}, u32[]{:S(2)}, u32[]{:S(2)}) collective-permute-start(bf16[64,768]{1,0:T(8,128)(2,1)} %get-tuple-element.112), channel_id=1, source_target_pairs={{0,12},{1,13},{2,14},{3,15},{4,8},{5,9},{6,10},{7,11},{8,4},{9,5},... | collective-permute-start | bytes 294920 | tf_op jit(solution)/shard_map/ppermute | solution.py:157
  264.4 9.9 %collective-permute-start.30 = (bf16[64,768]{1,0:T(8,128)(2,1)S(1)}, bf16[64,768]{1,0:T(8,128)(2,1)S(1)}, u32[]{:S(2)}, u32[]{:S(2)}) collective-permute-start(bf16[64,768]{1,0:T(8,128)(2,1)S(1)} %get-tuple-element.113), channel_id=1, source_target_pairs={{0,8},{1,9},{2,10},{3,11},{4,12},{5,13},{6,14},{7,15},{8,0},{9,1},... | collective-permute-start | bytes 294920 | tf_op jit(solution)/shard_map/ppermute | solution.py:157
  264.4 9.9 %collective-permute-start.29 = (bf16[64,768]{1,0:T(8,128)(2,1)S(1)}, bf16[64,768]{1,0:T(8,128)(2,1)}, u32[]{:S(2)}, u32[]{:S(2)}) collective-permute-start(bf16[64,768]{1,0:T(8,128)(2,1)S(1)} %get-tuple-element.114), channel_id=1, source_target_pairs={{0,4},{1,5},{2,6},{3,7},{4,0},{5,1},{6,2},{7,3},{8,12},{9,13},{10,... | collective-permute-start | bytes 294920 | tf_op jit(solution)/shard_map/ppermute | solution.py:157
  276.1 7.3 %collective-permute-start.32 = (bf16[256,768]{1,0:T(8,128)(2,1)S(1)}, bf16[256,768]{1,0:T(8,128)(2,1)}, u32[]{:S(2)}, u32[]{:S(2)}) collective-permute-start(bf16[256,768]{1,0:T(8,128)(2,1)S(1)} %bitcast.369), channel_id=1, source_target_pairs={{0,1},{1,0},{2,3},{3,2},{4,5},{5,4},{6,7},{7,6},{8,9},{9,8},{10,11... | collective-permute-start | bytes 1179656 | tf_op jit(solution)/shard_map/ppermute | solution.py:157
  282.8 10.5 %collective-permute-start.24 = (bf16[256,768]{1,0:T(8,128)(2,1)S(1)}, bf16[256,768]{1,0:T(8,128)(2,1)}, u32[]{:S(2)}, u32[]{:S(2)}) collective-permute-start(bf16[256,768]{1,0:T(8,128)(2,1)S(1)} %slice.340), channel_id=1, source_target_pairs={{0,1},{1,0},{2,3},{3,2},{4,5},{5,4},{6,7},{7,6},{8,9},{9,8},{10,11... | collective-permute-start | bytes 1179656 | tf_op jit(solution)/shard_map/ppermute | solution.py:157
  293.2 5.9 collective-permute-start.33
  294.7 7.6 %collective-permute-start.27 = (bf16[64,768]{1,0:T(8,128)(2,1)S(1)}, bf16[64,768]{1,0:T(8,128)(2,1)S(1)}, u32[]{:S(2)}, u32[]{:S(2)}) collective-permute-start(bf16[64,768]{1,0:T(8,128)(2,1)S(1)} %get-tuple-element.120), channel_id=1, source_target_pairs={{0,12},{1,13},{2,14},{3,15},{4,8},{5,9},{6,10},{7,11},{8,4},{9,5},... | collective-permute-start | bytes 294920 | tf_op jit(solution)/shard_map/ppermute | solution.py:157
  296.2 10.3 %collective-permute-start.26 = (bf16[64,768]{1,0:T(8,128)(2,1)S(1)}, bf16[64,768]{1,0:T(8,128)(2,1)S(1)}, u32[]{:S(2)}, u32[]{:S(2)}) collective-permute-start(bf16[64,768]{1,0:T(8,128)(2,1)S(1)} %get-tuple-element.121), channel_id=1, source_target_pairs={{0,8},{1,9},{2,10},{3,11},{4,12},{5,13},{6,14},{7,15},{8,0},{9,1},... | collective-permute-start | bytes 294920 | tf_op jit(solution)/shard_map/ppermute | solution.py:157
  296.2 10.3 %collective-permute-start.25 = (bf16[64,768]{1,0:T(8,128)(2,1)S(1)}, bf16[64,768]{1,0:T(8,128)(2,1)S(1)}, u32[]{:S(2)}, u32[]{:S(2)}) collective-permute-start(bf16[64,768]{1,0:T(8,128)(2,1)S(1)} %get-tuple-element.122), channel_id=1, source_target_pairs={{0,4},{1,5},{2,6},{3,7},{4,0},{5,1},{6,2},{7,3},{8,12},{9,13},{10,... | collective-permute-start | bytes 294920 | tf_op jit(solution)/shard_map/ppermute | solution.py:157
  299.2 9.3 %collective-permute-start.36 = (bf16[64,768]{1,0:T(8,128)(2,1)S(1)}, bf16[64,768]{1,0:T(8,128)(2,1)S(1)}, u32[]{:S(2)}, u32[]{:S(2)}) collective-permute-start(bf16[64,768]{1,0:T(8,128)(2,1)S(1)} %get-tuple-element.108), channel_id=1, source_target_pairs={{0,12},{1,13},{2,14},{3,15},{4,8},{5,9},{6,10},{7,11},{8,4},{9,5},... | collective-permute-start | bytes 294920 | tf_op jit(solution)/shard_map/ppermute | solution.py:157
  300.8 13.6 %collective-permute-start.35 = (bf16[64,768]{1,0:T(8,128)(2,1)S(1)}, bf16[64,768]{1,0:T(8,128)(2,1)S(1)}, u32[]{:S(2)}, u32[]{:S(2)}) collective-permute-start(bf16[64,768]{1,0:T(8,128)(2,1)S(1)} %get-tuple-element.109), channel_id=1, source_target_pairs={{0,8},{1,9},{2,10},{3,11},{4,12},{5,13},{6,14},{7,15},{8,0},{9,1},... | collective-permute-start | bytes 294920 | tf_op jit(solution)/shard_map/ppermute | solution.py:157
  302.2 12.2 %collective-permute-start.34 = (bf16[64,768]{1,0:T(8,128)(2,1)S(1)}, bf16[64,768]{1,0:T(8,128)(2,1)S(1)}, u32[]{:S(2)}, u32[]{:S(2)}) collective-permute-start(bf16[64,768]{1,0:T(8,128)(2,1)S(1)} %get-tuple-element.110), channel_id=1, source_target_pairs={{0,4},{1,5},{2,6},{3,7},{4,0},{5,1},{6,2},{7,3},{8,12},{9,13},{10,... | collective-permute-start | bytes 294920 | tf_op jit(solution)/shard_map/ppermute | solution.py:157
  346.0 9.9 %collective-permute-start.41 = (bf16[64,768]{1,0:T(8,128)(2,1)}, bf16[64,768]{1,0:T(8,128)(2,1)}, u32[]{:S(2)}, u32[]{:S(2)}) collective-permute-start(bf16[64,768]{1,0:T(8,128)(2,1)} %get-tuple-element.100), channel_id=1, source_target_pairs={{16,12},{17,13},{18,14},{19,15},{20,8},{21,9},{22,10},{23,11},{24,... | collective-permute-start | bytes 294920 | tf_op jit(solution)/shard_map/ppermute | solution.py:157
  347.3 12.7 %collective-permute-start.40 = (bf16[64,768]{1,0:T(8,128)(2,1)}, bf16[64,768]{1,0:T(8,128)(2,1)}, u32[]{:S(2)}, u32[]{:S(2)}) collective-permute-start(bf16[64,768]{1,0:T(8,128)(2,1)} %get-tuple-element.101), channel_id=1, source_target_pairs={{16,8},{17,9},{18,10},{19,11},{20,12},{21,13},{22,14},{23,15},{24,... | collective-permute-start | bytes 294920 | tf_op jit(solution)/shard_map/ppermute | solution.py:157
  348.6 11.4 %collective-permute-start.39 = (bf16[64,768]{1,0:T(8,128)(2,1)}, bf16[64,768]{1,0:T(8,128)(2,1)}, u32[]{:S(2)}, u32[]{:S(2)}) collective-permute-start(bf16[64,768]{1,0:T(8,128)(2,1)} %get-tuple-element.102), channel_id=1, source_target_pairs={{16,4},{17,5},{18,6},{19,7},{20,0},{21,1},{22,2},{23,3},{24,12},{2... | collective-permute-start | bytes 294920 | tf_op jit(solution)/shard_map/ppermute | solution.py:157
  349.9 12.1 %collective-permute-start.38 = (bf16[64,768]{1,0:T(8,128)(2,1)}, bf16[64,768]{1,0:T(8,128)(2,1)}, u32[]{:S(2)}, u32[]{:S(2)}) collective-permute-start(bf16[64,768]{1,0:T(8,128)(2,1)} %get-tuple-element.99), channel_id=1, source_target_pairs={{16,0},{17,1},{18,2},{19,3},{20,4},{21,5},{22,6},{23,7},{24,8},{25... | collective-permute-start | bytes 294920 | tf_op jit(solution)/shard_map/ppermute | solution.py:157
  352.0 15.5 %collective-permute-start.28 = (bf16[256,768]{1,0:T(8,128)(2,1)}, bf16[256,768]{1,0:T(8,128)(2,1)}, u32[]{:S(2)}, u32[]{:S(2)}) collective-permute-start(bf16[256,768]{1,0:T(8,128)(2,1)} %dynamic-slice_bitcast_fusion.1), channel_id=1, source_target_pairs={{0,1},{1,0},{2,3},{3,2},{4,5},{5,4},{6,7},{7,6},{8,9},{9,8},{10,11... | collective-permute-start | bytes 1179656 | tf_op jit(solution)/shard_map/ppermute | solution.py:157
  356.0 17.9 %collective-permute-start.37 = (bf16[256,768]{0,1:T(8,128)(2,1)}, bf16[256,768]{0,1:T(8,128)(2,1)}, u32[]{:S(2)}, u32[]{:S(2)}) collective-permute-start(bf16[256,768]{0,1:T(8,128)(2,1)} %copy-done.29), channel_id=1, source_target_pairs={{16,0},{17,1},{18,2},{19,3},{20,4},{21,5},{22,6},{23,7},{24,8},{25... | collective-permute-start | bytes 1179656 | tf_op jit(solution)/shard_map/ppermute | solution.py:157
  367.5 10.5 %collective-permute-start.42 = (bf16[256,768]{0,1:T(8,128)(2,1)}, bf16[256,768]{0,1:T(8,128)(2,1)}, u32[]{:S(2)}, u32[]{:S(2)}) collective-permute-start(bf16[256,768]{0,1:T(8,128)(2,1)} %broadcast_select_fusion), channel_id=1, source_target_pairs={{0,1},{1,0},{2,3},{3,2},{4,5},{5,4},{6,7},{7,6},{8,9},{9,8},{10,11... | collective-permute-start | bytes 1179656 | tf_op jit(solution)/shard_map/ppermute | solution.py:157
  369.4 102.8 %all-to-all-start.1 = ((bf16[16,16,768]{2,1,0:T(8,128)(2,1)}), bf16[16,16,768]{2,1,0:T(8,128)(2,1)}, u32[]{:S(2)}, u32[]{:S(2)}) async-start(bf16[16,16,768]{2,1,0:T(8,128)(2,1)} %bitcast.376), calls=%async_computation.1 | async-start | bytes 786432 | tf_op jit(solution)/shard_map/all_to_all | solution.py:395
  385.6 11.2 %collective-permute-start.43 = (bf16[256,768]{1,0:T(8,128)(2,1)S(1)}, bf16[256,768]{1,0:T(8,128)(2,1)S(1)}, u32[]{:S(2)}, u32[]{:S(2)}) collective-permute-start(bf16[256,768]{1,0:T(8,128)(2,1)S(1)} %slice.338), channel_id=1, source_target_pairs={{0,1},{1,0},{2,3},{3,2},{4,5},{5,4},{6,7},{7,6},{8,9},{9,8},{10,11... | collective-permute-start | bytes 1179656 | tf_op jit(solution)/shard_map/ppermute | solution.py:157
  391.9 87.0 %collective-permute-start.53 = (bf16[4,96,1536]{2,1,0:T(8,128)(2,1)}, bf16[4,96,1536]{2,1,0:T(8,128)(2,1)}, u32[]{:S(2)}, u32[]{:S(2)}) collective-permute-start(bf16[4,96,1536]{2,1,0:T(8,128)(2,1)} %fusion.70), channel_id=1, source_target_pairs={{0,2},{1,3},{2,0},{3,1},{4,6},{5,7},{6,4},{7,5},{8,10},{9,11},{10,... | collective-permute-start | bytes 3538952 | tf_op jit(solution)/shard_map/ppermute | solution.py:157
  396.9 7.6 %collective-permute-start.46 = (bf16[64,768]{1,0:T(8,128)(2,1)S(1)}, bf16[64,768]{1,0:T(8,128)(2,1)S(1)}, u32[]{:S(2)}, u32[]{:S(2)}) collective-permute-start(bf16[64,768]{1,0:T(8,128)(2,1)S(1)} %get-tuple-element.96), channel_id=1, source_target_pairs={{0,12},{1,13},{2,14},{3,15},{4,8},{5,9},{6,10},{7,11},{8,4},{9,5},... | collective-permute-start | bytes 294920 | tf_op jit(solution)/shard_map/ppermute | solution.py:157
  400.3 8.8 %collective-permute-start.45 = (bf16[64,768]{1,0:T(8,128)(2,1)S(1)}, bf16[64,768]{1,0:T(8,128)(2,1)S(1)}, u32[]{:S(2)}, u32[]{:S(2)}) collective-permute-start(bf16[64,768]{1,0:T(8,128)(2,1)S(1)} %get-tuple-element.97), channel_id=1, source_target_pairs={{0,8},{1,9},{2,10},{3,11},{4,12},{5,13},{6,14},{7,15},{8,0},{9,1},... | collective-permute-start | bytes 294920 | tf_op jit(solution)/shard_map/ppermute | solution.py:157
  400.3 8.8 %collective-permute-start.44 = (bf16[64,768]{1,0:T(8,128)(2,1)S(1)}, bf16[64,768]{1,0:T(8,128)(2,1)S(1)}, u32[]{:S(2)}, u32[]{:S(2)}) collective-permute-start(bf16[64,768]{1,0:T(8,128)(2,1)S(1)} %get-tuple-element.98), channel_id=1, source_target_pairs={{0,4},{1,5},{2,6},{3,7},{4,0},{5,1},{6,2},{7,3},{8,12},{9,13},{10,... | collective-permute-start | bytes 294920 | tf_op jit(solution)/shard_map/ppermute | solution.py:157
  402.5 82.8 %collective-permute-start.57 = (bf16[4,192,768]{2,1,0:T(8,128)(2,1)}, bf16[4,192,768]{2,1,0:T(8,128)(2,1)}, u32[]{:S(2)}, u32[]{:S(2)}) collective-permute-start(bf16[4,192,768]{2,1,0:T(8,128)(2,1)} %fusion.71), channel_id=1, source_target_pairs={{0,2},{1,3},{2,0},{3,1},{4,6},{5,7},{6,4},{7,5},{8,10},{9,11},{10,... | collective-permute-start | bytes 3538952 | tf_op jit(solution)/shard_map/ppermute | solution.py:157
  443.4 30.9 %collective-permute-start.47 = (bf16[256,768]{1,0:T(8,128)(2,1)}, bf16[256,768]{1,0:T(8,128)(2,1)S(1)}, u32[]{:S(2)}, u32[]{:S(2)}) collective-permute-start(bf16[256,768]{1,0:T(8,128)(2,1)} %dynamic-slice_bitcast_fusion), channel_id=1, source_target_pairs={{0,1},{1,0},{2,3},{3,2},{4,5},{5,4},{6,7},{7,6},{8,9},{9,8},{10,11... | collective-permute-start | bytes 1179656 | tf_op jit(solution)/shard_map/ppermute | solution.py:157
  469.1 73.0 %collective-permute-start.48 = (bf16[8,400,384]{2,1,0:T(8,128)(2,1)}, bf16[8,400,384]{2,1,0:T(8,128)(2,1)}, u32[]{:S(2)}, u32[]{:S(2)}) collective-permute-start(bf16[8,400,384]{2,1,0:T(8,128)(2,1)} %bitcast.325), channel_id=1, source_target_pairs={{0,1},{1,0},{2,3},{3,2},{4,5},{5,4},{6,7},{7,6},{8,9},{9,8},{10,11... | collective-permute-start | bytes 7372808 | tf_op jit(solution)/shard_map/ppermute | solution.py:157
  475.1 105.7 %all-to-all-start.2 = ((bf16[16,16,768]{2,1,0:T(8,128)(2,1)}), bf16[16,16,768]{2,1,0:T(8,128)(2,1)S(1)}, u32[]{:S(2)}, u32[]{:S(2)}) async-start(bf16[16,16,768]{2,1,0:T(8,128)(2,1)} %bitcast.128), calls=%async_computation.2 | async-start | bytes 786432 | tf_op jit(solution)/shard_map/all_to_all | solution.py:395
  481.5 15.5 %collective-permute-start.56 = (bf16[96,1536]{1,0:T(8,128)(2,1)S(1)}, bf16[96,1536]{1,0:T(8,128)(2,1)S(1)}, u32[]{:S(2)}, u32[]{:S(2)}) collective-permute-start(bf16[96,1536]{1,0:T(8,128)(2,1)S(1)} %get-tuple-element.63), channel_id=1, source_target_pairs={{0,12},{1,13},{2,14},{3,15},{4,8},{5,9},{6,10},{7,11},{8,4},{9,5},... | collective-permute-start | bytes 884744 | tf_op jit(solution)/shard_map/ppermute | solution.py:157
  487.2 42.5 %collective-permute-start.55 = (bf16[96,1536]{1,0:T(8,128)(2,1)S(1)}, bf16[96,1536]{1,0:T(8,128)(2,1)S(1)}, u32[]{:S(2)}, u32[]{:S(2)}) collective-permute-start(bf16[96,1536]{1,0:T(8,128)(2,1)S(1)} %get-tuple-element.64), channel_id=1, source_target_pairs={{0,8},{1,9},{2,10},{3,11},{4,12},{5,13},{6,14},{7,15},{8,0},{9,1},... | collective-permute-start | bytes 884744 | tf_op jit(solution)/shard_map/ppermute | solution.py:157
  487.3 54.7 %collective-permute-start.54 = (bf16[96,1536]{1,0:T(8,128)(2,1)S(1)}, bf16[96,1536]{1,0:T(8,128)(2,1)S(1)}, u32[]{:S(2)}, u32[]{:S(2)}) collective-permute-start(bf16[96,1536]{1,0:T(8,128)(2,1)S(1)} %get-tuple-element.62), channel_id=1, source_target_pairs={{0,4},{1,5},{2,6},{3,7},{4,0},{5,1},{6,2},{7,3},{8,12},{9,13},{10,... | collective-permute-start | bytes 884744 | tf_op jit(solution)/shard_map/ppermute | solution.py:157
  488.4 41.4 %collective-permute-start.60 = (bf16[192,768]{1,0:T(8,128)(2,1)S(1)}, bf16[192,768]{1,0:T(8,128)(2,1)S(1)}, u32[]{:S(2)}, u32[]{:S(2)}) collective-permute-start(bf16[192,768]{1,0:T(8,128)(2,1)S(1)} %get-tuple-element.56), channel_id=1, source_target_pairs={{0,12},{1,13},{2,14},{3,15},{4,8},{5,9},{6,10},{7,11},{8,4},{9,5},... | collective-permute-start | bytes 884744 | tf_op jit(solution)/shard_map/ppermute | solution.py:157
  497.0 45.0 %collective-permute-start.59 = (bf16[192,768]{1,0:T(8,128)(2,1)S(1)}, bf16[192,768]{1,0:T(8,128)(2,1)S(1)}, u32[]{:S(2)}, u32[]{:S(2)}) collective-permute-start(bf16[192,768]{1,0:T(8,128)(2,1)S(1)} %get-tuple-element.57), channel_id=1, source_target_pairs={{0,8},{1,9},{2,10},{3,11},{4,12},{5,13},{6,14},{7,15},{8,0},{9,1},... | collective-permute-start | bytes 884744 | tf_op jit(solution)/shard_map/ppermute | solution.py:157
  529.7 16.8 %collective-permute-start.58 = (bf16[192,768]{1,0:T(8,128)(2,1)S(1)}, bf16[192,768]{1,0:T(8,128)(2,1)S(1)}, u32[]{:S(2)}, u32[]{:S(2)}) collective-permute-start(bf16[192,768]{1,0:T(8,128)(2,1)S(1)} %get-tuple-element.55), channel_id=1, source_target_pairs={{0,4},{1,5},{2,6},{3,7},{4,0},{5,1},{6,2},{7,3},{8,12},{9,13},{10,... | collective-permute-start | bytes 884744 | tf_op jit(solution)/shard_map/ppermute | solution.py:157
  545.0 28.6 %collective-permute-start.49 = (bf16[4,400,384]{2,1,0:T(8,128)(2,1)S(1)}, bf16[4,400,384]{2,1,0:T(8,128)(2,1)S(1)}, u32[]{:S(2)}, u32[]{:S(2)}) collective-permute-start(bf16[4,400,384]{2,1,0:T(8,128)(2,1)S(1)} %fusion.66), channel_id=1, source_target_pairs={{0,2},{1,3},{2,0},{3,1},{4,6},{5,7},{6,4},{7,5},{8,10},{9,11},{10,... | collective-permute-start | bytes 3686408 | tf_op jit(solution)/shard_map/ppermute | solution.py:157
  574.7 12.3 %collective-permute-start.52 = (bf16[400,384]{1,0:T(8,128)(2,1)}, bf16[400,384]{1,0:T(8,128)(2,1)S(1)}, u32[]{:S(2)}, u32[]{:S(2)}) collective-permute-start(bf16[400,384]{1,0:T(8,128)(2,1)} %get-tuple-element.49), channel_id=1, source_target_pairs={{0,12},{1,13},{2,14},{3,15},{4,8},{5,9},{6,10},{7,11},{8,4},{9,5},... | collective-permute-start | bytes 921608 | tf_op jit(solution)/shard_map/ppermute | solution.py:157
  576.2 24.5 %collective-permute-start.51 = (bf16[400,384]{1,0:T(8,128)(2,1)}, bf16[400,384]{1,0:T(8,128)(2,1)S(1)}, u32[]{:S(2)}, u32[]{:S(2)}) collective-permute-start(bf16[400,384]{1,0:T(8,128)(2,1)} %get-tuple-element.50), channel_id=1, source_target_pairs={{0,8},{1,9},{2,10},{3,11},{4,12},{5,13},{6,14},{7,15},{8,0},{9,1},... | collective-permute-start | bytes 921608 | tf_op jit(solution)/shard_map/ppermute | solution.py:157
  576.2 24.5 %collective-permute-start.50 = (bf16[400,384]{1,0:T(8,128)(2,1)}, bf16[400,384]{1,0:T(8,128)(2,1)}, u32[]{:S(2)}, u32[]{:S(2)}) collective-permute-start(bf16[400,384]{1,0:T(8,128)(2,1)} %get-tuple-element.48), channel_id=1, source_target_pairs={{0,4},{1,5},{2,6},{3,7},{4,0},{5,1},{6,2},{7,3},{8,12},{9,13},{10,... | collective-permute-start | bytes 921608 | tf_op jit(solution)/shard_map/ppermute | solution.py:157
  (90 other events, 623.8 us)
Sparse Core Ops, SparseCore 0:
  10.8 93.0 all-gather.2

commit v2 on v1

v2 whole, which is shorter than its diff:
```python
import functools

import jax
import jax.numpy as jnp
from jax import lax
from jax.experimental import pallas as pl
from jax.experimental.pallas import tpu as pltpu
from jax.sharding import PartitionSpec as P

HEAD_DIM = 64
EPSILON = 1e-06
NEGATIVE = -1e30
EXACT = lax.Precision.HIGHEST
EXTRA = 128
BF = jnp.bfloat16
F32 = jnp.float32
VM = pl.BlockSpec(memory_space=pltpu.VMEM)
SM = pl.BlockSpec(memory_space=pltpu.SMEM)
HB = pl.BlockSpec(memory_space=pl.ANY)
PIPE, MINE, REP, CORE, SPLIT = range(5)


def dot32(a, b):
    return jnp.dot(a, b, preferred_element_type=F32)


def dot_nt(a, b):
    return lax.dot_general(a, b, (((1,), (1,)), ((), ())), preferred_element_type=F32)


def dot_tn(a, b):
    return lax.dot_general(a, b, (((0,), (0,)), ((), ())), preferred_element_type=F32)


def norm_scale(x):
    return lax.rsqrt(jnp.mean(x * x, axis=-1, keepdims=True) + EPSILON)


def norm_back(x, scale, gain, grad):
    weighted = grad * gain
    grad_x = scale * weighted - x * (scale * scale * scale) * jnp.mean(
        x * weighted, axis=-1, keepdims=True
    )
    return grad_x, jnp.sum(grad * (x * scale), axis=0, keepdims=True)


def kernel_call(body, name, outs, ins, specs, scratch=(), flops=0, size=0, exps=0):
    return pl.pallas_call(
        body,
        name=name,
        out_shape=[jax.ShapeDtypeStruct(shape, kind) for shape, kind in outs],
        in_specs=specs,
        out_specs=[VM] * len(outs),
        scratch_shapes=list(scratch),
        compiler_params=pltpu.CompilerParams(vmem_limit_bytes=50 << 20),
        cost_estimate=pl.CostEstimate(flops=flops, bytes_accessed=size, transcendentals=exps),
    )(*ins)


def deal_kernel(facts, both, own_rows, slots, onehot, place):
    width = own_rows.shape[1]
    pack = own_rows.shape[0]
    total = both.shape[0]
    half = pack // 2
    core = facts[CORE].astype(F32)
    numbers = both[:, width:]
    spot = numbers[:, 0:1].astype(F32)
    source = (lax.broadcasted_iota(jnp.int32, (total, 1), 0) >= pack).astype(F32)
    upper = (spot >= half).astype(F32)
    where = jnp.where(upper == core, source * half + spot - upper * half, -1.0)
    spots = lax.broadcasted_iota(jnp.int32, (total, pack), 1).astype(F32)
    hot = (spots == where).astype(F32).astype(BF)
    place[...] = hot
    own_rows[...] = dot_tn(hot, both[:, :width]).astype(BF)
    mine = dot_tn(hot, numbers)
    lanes = lax.broadcasted_iota(jnp.int32, (EXTRA, EXTRA), 0)
    eye = (lanes == lax.broadcasted_iota(jnp.int32, (EXTRA, EXTRA), 1)).astype(F32).astype(BF)
    across = dot_nt(eye, mine.astype(BF))
    expert_col, expert_row = mine[:, 1:2], across[1:2, :]
    order_col = mine[:, 2:3] * 256.0 + mine[:, 3:4]
    order_row = across[2:3, :] * 256.0 + across[3:4, :]
    ahead = (expert_col == expert_row) & (order_col < order_row)
    rank = jnp.sum(ahead.astype(F32), axis=0, keepdims=True).astype(jnp.int32)
    experts = 4
    cap = pack // experts
    block = jnp.bitwise_xor(expert_row.astype(jnp.int32), facts[MINE])
    slot = jnp.where(rank < cap, block * cap + rank, -1)
    slots[...] = (lax.broadcasted_iota(jnp.int32, (pack, pack), 0) == slot).astype(F32).astype(BF)
    onehot[...] = (
        lax.broadcasted_iota(jnp.int32, (pack, EXTRA), 1) == expert_col.astype(jnp.int32)
    ).astype(F32)


def mask_of(facts, pack):
    query = lax.broadcasted_iota(jnp.int32, (pack, pack), 0)
    key = lax.broadcasted_iota(jnp.int32, (pack, pack), 1)
    split = facts[SPLIT]
    return ((query < split) == (key < split)) & (key <= query)


def stacked(refs):
    return jnp.concatenate([ref[...] for ref in refs], axis=0)


def attn_kernel(second, facts, *refs):
    refs = list(refs)
    own_rows = refs.pop(0)
    if second:
        up = refs.pop(0)
        slots_in = [refs.pop(0) for _ in range(4)]
    attn_own, attn_other, gains, router, slots, onehot = (refs.pop(0) for _ in range(6))
    mid, attn_in, proj, mixed, mlp_in, probs = (refs.pop(0) for _ in range(6))
    blocks = [refs.pop(0) for _ in range(4)]
    pack, width = own_rows.shape
    cols = attn_own.shape[1]
    cap = pack // 4
    hot = slots[...]
    if second:
        stream = refs.pop(0)
        grads = [refs.pop(0) for _ in range(4)]
        came = up[:, :width] + up[:, width : width + 1] * dot_tn(hot, stacked(slots_in))
        rows = jnp.where(facts[PIPE] == 0, own_rows[...], came.astype(BF))
        stream[...] = rows
    else:
        rows = own_rows[...]
    x = rows.astype(F32)
    normed = (x * norm_scale(x) * gains[0:1, :]).astype(BF)
    attn_in[...] = normed
    allowed = mask_of(facts, pack)
    for at, weight in ((0, attn_own), (1, attn_other)):
        for part in range(3):
            proj[at, part] = dot32(normed, weight[part * width : (part + 1) * width, :]).astype(BF)
        for head in range(cols // HEAD_DIM):
            lanes = slice(head * HEAD_DIM, (head + 1) * HEAD_DIM)
            scores = dot_nt(proj[at, 0, :, lanes], proj[at, 1, :, lanes]) * HEAD_DIM ** (-0.5)
            scores = jnp.where(allowed, scores, NEGATIVE)
            weights = jnp.exp(scores - jnp.max(scores, axis=-1, keepdims=True))
            share = (weights * (1.0 / jnp.sum(weights, axis=-1, keepdims=True))).astype(BF)
            spot = at * cols + head * HEAD_DIM
            mixed[:, spot : spot + HEAD_DIM] = dot32(share, proj[at, 2, :, lanes]).astype(BF)
    base = 3 * width
    for side in range(2):
        rows_at = slice(base + side * cols, base + (side + 1) * cols)
        lanes = slice(side * cols, (side + 1) * cols)
        mid[:, lanes] = (
            x[:, lanes]
            + dot32(mixed[:, :cols], attn_own[rows_at, :])
            + dot32(mixed[:, cols:], attn_other[rows_at, :])
        )
    m = mid[:, :width]
    low = (m * norm_scale(m) * gains[1:2, :]).astype(BF)
    mlp_in[...] = low
    logits = dot32(low, router[...])
    lane = lax.broadcasted_iota(jnp.int32, logits.shape, 1)
    logits = logits + pltpu.roll(logits, EXTRA - 4, 1) + pltpu.roll(logits, EXTRA - 8, 1)
    logits = jnp.where(lane < 4, logits, NEGATIVE)
    rel = jnp.exp(logits - jnp.max(logits, axis=-1, keepdims=True))
    share = rel / jnp.sum(rel, axis=-1, keepdims=True)
    probs[...] = share
    gate = jnp.sum(share * onehot[...], axis=-1, keepdims=True)
    mid[:, width:] = jnp.broadcast_to(gate, (pack, EXTRA))
    for step in range(4):
        blocks[step][...] = dot32(hot[step * cap : (step + 1) * cap, :], low).astype(BF)
    if second:
        weighted = (gate * own_rows[...].astype(F32)).astype(BF)
        for step in range(4):
            grads[step][...] = dot32(hot[step * cap : (step + 1) * cap, :], weighted).astype(BF)


def attn_forward(facts, own_rows, weights, plan, came=None):
    attn_own, attn_other, gains, router3, _ = weights
    slots, onehot = plan
    pack, width = own_rows.shape
    cols = attn_own.shape[1]
    cap = pack // 4
    second = came is not None
    ins = [facts, own_rows] + (list(came) if second else [])
    ins += [attn_own, attn_other, gains, router3, slots, onehot]
    outs = [
        ((pack, width + EXTRA), F32),
        ((pack, width), BF),
        ((2, 3, pack, cols), BF),
        ((pack, width), BF),
        ((pack, width), BF),
        ((pack, EXTRA), F32),
    ]
    outs += [((cap, width), BF)] * 4
    if second:
        outs += [((pack, width), BF)] + [((cap, width), BF)] * 4
    return kernel_call(
        functools.partial(attn_kernel, second),
        "attn_second" if second else "attn_first",
        outs,
        ins,
        [SM] + [VM] * (len(ins) - 1),
        flops=2 * pack * width * width * 5,
        size=8 * width * width,
        exps=pack * pack * 12,
    )


def attn_back_kernel(first, facts, *refs):
    refs = list(refs)
    grad_out = refs.pop(0)
    if first:
        up = refs.pop(0)
    else:
        own_rows = refs.pop(0)
    grad_slots = [refs.pop(0) for _ in range(4)]
    expert_slots = [refs.pop(0) for _ in range(4)]
    stream, mid, proj, mlp_in, probs = (refs.pop(0) for _ in range(5))
    attn_own, attn_other, gains, router, slots, onehot = (refs.pop(0) for _ in range(6))
    grad_stream = refs.pop(0)
    if first:
        blocks = [refs.pop(0) for _ in range(4)]
        grad_proj = refs.pop(0)
    else:
        grad_proj, grad_low, grad_gains, grad_router = (refs.pop(0) for _ in range(4))
    pack, width = stream.shape
    cols = attn_own.shape[1]
    cap = pack // 4
    hot = slots[...]
    rows = grad_out[...]
    if not first:
        rows = jnp.where(facts[PIPE] == 0, rows, own_rows[...])
    g = rows.astype(F32)
    grad_gate = jnp.sum(g * dot_tn(hot, stacked(expert_slots)), axis=-1, keepdims=True)
    gate = mid[:, width : width + 1]
    grad_logits = grad_gate * gate * (onehot[...] - probs[...])
    m = mid[:, :width]
    grad_mlp = dot_tn(hot, stacked(grad_slots)) + jnp.dot(
        grad_logits, router[...], preferred_element_type=F32, precision=EXACT
    )
    grad_norm, gain_two = norm_back(m, norm_scale(m), gains[1:2, :], grad_mlp)
    grad_mid = g + grad_norm
    low = grad_mid.astype(BF)
    allowed = mask_of(facts, pack)
    grad_in = jnp.zeros((pack, width), F32)
    base = 3 * width
    for at, weight in ((0, attn_own), (1, attn_other)):
        grad_mixed = (
            dot_nt(low[:, :cols], weight[base : base + cols, :])
            + dot_nt(low[:, cols:], weight[base + cols : base + 2 * cols, :])
        ).astype(BF)
        for head in range(cols // HEAD_DIM):
            lanes = slice(head * HEAD_DIM, (head + 1) * HEAD_DIM)
            query, key, value = (proj[at, part, :, lanes] for part in range(3))
            grad_head = grad_mixed[:, lanes]
            scores = dot_nt(query, key) * HEAD_DIM ** (-0.5)
            scores = jnp.where(allowed, scores, NEGATIVE)
            share = jnp.exp(scores - jnp.max(scores, axis=-1, keepdims=True))
            share = share * (1.0 / jnp.sum(share, axis=-1, keepdims=True))
            grad_share = dot_nt(grad_head, value)
            pulled = share * grad_share
            inner = jnp.sum(pulled, axis=-1, keepdims=True)
            grad_scores = ((pulled - share * inner) * HEAD_DIM ** (-0.5)).astype(BF)
            grad_proj[at, 0, :, lanes] = dot32(grad_scores, key).astype(BF)
            grad_proj[at, 1, :, lanes] = dot_tn(grad_scores, query).astype(BF)
            grad_proj[at, 2, :, lanes] = dot_tn(share.astype(BF), grad_head).astype(BF)
        for part in range(3):
            grad_in += dot_nt(grad_proj[at, part], weight[part * width : (part + 1) * width, :])
    x = stream[...].astype(F32)
    grad_norm, gain_one = norm_back(x, norm_scale(x), gains[0:1, :], grad_in)
    result = (grad_mid + grad_norm).astype(BF)
    grad_stream[...] = result
    if first:
        weighted = (up[:, width : width + 1] * result.astype(F32)).astype(BF)
        for step in range(4):
            blocks[step][...] = dot32(hot[step * cap : (step + 1) * cap, :], weighted).astype(BF)
    else:
        grad_low[...] = low
        grad_gains[0:1, :] = gain_one
        grad_gains[1:2, :] = gain_two
        high = grad_logits.astype(BF)
        rest = (grad_logits - high.astype(F32)).astype(BF)
        grad_router[...] = dot_tn(mlp_in[...], high) + dot_tn(mlp_in[...], rest)


def attn_backward(facts, grad_out, extra, grad_slots, expert_slots, saved, weights, plan, first):
    attn_own, attn_other, gains, _, router = weights
    slots, onehot = plan
    stream, mid, proj, mlp_in, probs = saved
    pack, width = stream.shape
    cols = attn_own.shape[1]
    cap = pack // 4
    ins = [facts, grad_out, extra, *grad_slots, *expert_slots, stream, mid, proj, mlp_in, probs]
    ins += [attn_own, attn_other, gains, router, slots, onehot]
    outs = [((pack, width), BF)]
    if first:
        outs += [((cap, width), BF)] * 4
    outs += [((2, 3, pack, cols), BF)]
    if not first:
        outs += [((pack, width), BF), ((2, width), F32), ((width, EXTRA), F32)]
    return kernel_call(
        functools.partial(attn_back_kernel, first),
        "attn_back_first" if first else "attn_back_second",
        outs,
        ins,
        [SM] + [VM] * (len(ins) - 1),
        flops=2 * pack * width * width * 8,
        size=8 * width * width,
        exps=pack * pack * 12,
    )


def gelu_parts(u):
    inner = 0.7978845608028654 * (u + 0.044715 * (u * u * u))
    t = jnp.tanh(inner)
    return t, 0.5 * u * (1.0 + t)


def gelu_slope(u):
    t, _ = gelu_parts(u)
    slope = 0.7978845608028654 * (1.0 + 3.0 * 0.044715 * (u * u))
    return 0.5 * (1.0 + t) + 0.5 * u * (1.0 - t * t) * slope


def bring(facts, pieces, places, scratch, sems):
    copies = []
    for piece, spots in zip(pieces, places, strict=True):
        for source, target, rows, column, columns in spots(facts):
            copies.append(
                pltpu.make_async_copy(
                    piece.at[pl.ds(source, rows), pl.ds(0, columns)],
                    scratch.at[pl.ds(target, rows), pl.ds(column, columns)],
                    sems.at[len(copies)],
                )
            )
    for copy in copies:
        copy.start()
    return copies


TILE = 256


def expert_kernel(places_in, places_out, facts, *refs):
    refs = list(refs)
    blocks = [refs.pop(0) for _ in range(8)]
    pieces = [refs.pop(0) for _ in range(len(places_in))]
    pre, act, own, other = (refs.pop(0) for _ in range(4))
    w_in, w_out, rows, sems_in, sems_out = refs
    arriving = bring(facts, pieces, places_in, w_in, sems_in)
    later = bring(facts, pieces, places_out, w_out, sems_out)
    cap = blocks[0].shape[0]
    for at, block in enumerate(blocks):
        rows[at * cap : (at + 1) * cap, :] = block[...]
    for copy in arriving:
        copy.wait()
    ff = w_in.shape[1]
    width = w_in.shape[0]

    @pl.loop(0, ff // TILE)
    def _(tile):
        lanes = pl.ds(pl.multiple_of(tile * TILE, TILE), TILE)
        value = dot32(rows[...], w_in[:, lanes])
        pre[:, lanes] = value
        act[:, lanes] = gelu_parts(value)[1].astype(BF)

    for copy in later:
        copy.wait()
    count = 4 * cap

    @pl.loop(0, width // TILE)
    def _(tile):
        lanes = pl.ds(pl.multiple_of(tile * TILE, TILE), TILE)
        value = dot32(act[...], w_out[:, lanes])
        own[:, lanes] = value[:count]
        other[:, lanes] = value[count:].astype(BF)


def expert_back_kernel(places_in, places_out, facts, *refs):
    refs = list(refs)
    blocks = [refs.pop(0) for _ in range(8)]
    pre = refs.pop(0)
    pieces = [refs.pop(0) for _ in range(len(places_in))]
    grad_pre, own, other = (refs.pop(0) for _ in range(3))
    w_in, w_out, rows, sems_in, sems_out = refs
    arriving = bring(facts, pieces, places_out, w_out, sems_out)
    later = bring(facts, pieces, places_in, w_in, sems_in)
    cap = blocks[0].shape[0]
    for at, block in enumerate(blocks):
        rows[at * cap : (at + 1) * cap, :] = block[...]
    for copy in arriving:
        copy.wait()
    ff = w_in.shape[1]
    width = w_in.shape[0]

    @pl.loop(0, ff // TILE)
    def _(tile):
        lanes = pl.ds(pl.multiple_of(tile * TILE, TILE), TILE)
        value = dot_nt(rows[...], w_out[lanes, :])
        grad_pre[:, lanes] = (value * gelu_slope(pre[:, lanes])).astype(BF)

    for copy in later:
        copy.wait()
    count = 4 * cap

    @pl.loop(0, width // TILE)
    def _(tile):
        lanes = pl.ds(pl.multiple_of(tile * TILE, TILE), TILE)
        value = dot_nt(grad_pre[...], w_in[lanes, :])
        own[:, lanes] = value[:count]
        other[:, lanes] = value[count:].astype(BF)


def expert_call(body, name, facts, blocks, pre, pieces, places, width, ff):
    places_in, places_out = places
    cap = blocks[0].shape[0]
    count = 4 * cap
    back = pre is not None
    ins = [facts, *blocks] + ([pre] if back else []) + list(pieces)
    outs = [((2 * count, ff), BF)] if back else [((2 * count, ff), F32), ((2 * count, ff), BF)]
    outs += [((count, width), F32), ((count, width), BF)]
    numbers = jnp.zeros((8,), jnp.int32)
    sizes = [sum(len(spots(numbers)) for spots in each) for each in places]
    scratch = [
        pltpu.VMEM((width, ff), BF),
        pltpu.VMEM((ff, width), BF),
        pltpu.VMEM((2 * count, width), BF),
        pltpu.SemaphoreType.DMA((sizes[0],)),
        pltpu.SemaphoreType.DMA((sizes[1],)),
    ]
    specs = [SM] + [VM] * (len(ins) - 1 - len(pieces)) + [HB] * len(pieces)
    return kernel_call(
        functools.partial(body, places_in, places_out),
        name,
        outs,
        ins,
        specs,
        scratch,
        flops=8 * count * width * ff,
        size=6 * width * ff,
        exps=2 * count * ff,
    )


def fold_kernel(own, other, *blocks):
    cap = blocks[0].shape[0]
    for step, block in enumerate(blocks):
        rows = slice(step * cap, (step + 1) * cap)
        block[...] = (own[rows, :] + other[rows, :].astype(F32)).astype(BF)


def fold(own, other, name):
    count, width = own.shape
    cap = count // 4
    return kernel_call(
        fold_kernel, name, [((cap, width), BF)] * 4, [own, other], [VM, VM], size=8 * count * width
    )


def return_kernel(merge, *refs):
    refs = list(refs)
    rows = refs.pop(0)
    if merge:
        hot = refs.pop(0)
        slots_in = [refs.pop(0) for _ in range(4)]
        width = slots_in[0].shape[1]
        values = rows[:, :width] + rows[:, width : width + 1] * dot_tn(hot[...], stacked(slots_in))
        values = values.astype(BF)
    else:
        values = rows[...]
    place, own, other, facts = refs[0], refs[2], refs[3], refs[1]
    pack = own.shape[0]
    core = facts[CORE]
    own[...] = dot32(place[pl.ds(pl.multiple_of(core * pack, pack), pack), :], values).astype(BF)
    other[...] = dot32(
        place[pl.ds(pl.multiple_of((1 - core) * pack, pack), pack), :], values
    ).astype(BF)


def sent_rows(facts, merge, rows, extra, place, width):
    pack = place.shape[1]
    ins = [rows, *extra, place, facts]
    outs = [((pack, width), BF)] * 2
    return kernel_call(
        functools.partial(return_kernel, merge),
        "return_merged" if merge else "return_rows",
        outs,
        ins,
        [VM] * (len(ins) - 1) + [SM],
        flops=4 * pack * pack * width,
        size=8 * pack * width,
    )


def gather_kernel(places, facts, *refs):
    pieces, out, sems = refs[:-2], refs[-2], refs[-1]
    for copy in bring(facts, pieces, places, out, sems):
        copy.wait()


def gather_pieces(facts, pieces, places, shape):
    numbers = jnp.zeros((8,), jnp.int32)
    count = sum(len(spots(numbers)) for spots in places)
    return pl.pallas_call(
        functools.partial(gather_kernel, places),
        name="gather_pieces",
        out_shape=jax.ShapeDtypeStruct(shape, BF),
        in_specs=[SM] + [HB] * len(pieces),
        out_specs=HB,
        scratch_shapes=[pltpu.SemaphoreType.DMA((count,))],
        compiler_params=pltpu.CompilerParams(vmem_limit_bytes=16 << 20),
        cost_estimate=pl.CostEstimate(
            flops=0, bytes_accessed=4 * shape[0] * shape[1], transcendentals=0
        ),
    )(facts, *pieces)


def expert_grad_kernel(split, facts, *refs):
    refs = list(refs)
    blocks = [refs.pop(0) for _ in range(8)]
    grads = [refs.pop(0) for _ in range(8)]
    act, grad_pre = refs.pop(0), refs.pop(0)
    if split:
        sends = [refs.pop(0) for _ in range(4)]
        keeps = [refs.pop(0) for _ in range(4)]
        grad_in, grad_out, rows, grad_rows = refs
    else:
        grad_in, grad_out, rows, grad_rows = refs
    cap = blocks[0].shape[0]
    for at in range(8):
        rows[at * cap : (at + 1) * cap, :] = blocks[at][...]
        grad_rows[at * cap : (at + 1) * cap, :] = grads[at][...]
    ff = act.shape[1]
    width = rows.shape[1]

    @pl.loop(0, ff // TILE)
    def _(tile):
        lanes = pl.ds(pl.multiple_of(tile * TILE, TILE), TILE)
        grad_in[:, lanes] = dot_tn(rows[...], grad_pre[:, lanes])
        grad_out[lanes, :] = dot_tn(act[:, lanes], grad_rows[...])

    if split:
        shard, out_shard = width // 8, ff // 8
        for step in range(4):
            owner = jnp.bitwise_xor(facts[MINE], step) * 2
            for rep, target in ((1 - facts[REP], sends[step]), (facts[REP], keeps[step])):
                spot = pl.ds(pl.multiple_of((owner + rep) * shard, shard), shard)
                target[0:shard, :] = grad_in[spot, :width].astype(BF)
                target[shard : 2 * shard, :] = grad_in[spot, width:].astype(BF)
                spot = pl.ds(pl.multiple_of((owner + rep) * out_shard, out_shard), out_shard)
                target[2 * shard :, :] = grad_out[spot, :].astype(BF)


def expert_grads(facts, blocks, grads, act, grad_pre, split):
    cap, width = blocks[0].shape
    ff = act.shape[1]
    ins = [facts, *blocks, *grads, act, grad_pre]
    full = [((width, ff), F32), ((ff, width), F32)]
    rows = [pltpu.VMEM((8 * cap, width), BF)] * 2
    if split:
        outs = [((width // 2, width), BF)] * 8
        scratch = [pltpu.VMEM(*each) for each in full] + rows
    else:
        outs, scratch = full, rows
    return kernel_call(
        functools.partial(expert_grad_kernel, split),
        "expert_grads",
        outs,
        ins,
        [SM] + [VM] * (len(ins) - 1),
        scratch,
        flops=32 * cap * width * ff,
        size=8 * width * ff,
    )


def owner_kernel(facts, *refs):
    pieces, grad_in, grad_out = refs[:-2], refs[-2], refs[-1]
    shard = grad_in.shape[1]
    width = grad_out.shape[2]
    for step, piece in enumerate(pieces):
        at = jnp.bitwise_xor(facts[MINE], step)
        grad_in[at, :, :width] = piece[:shard, :].astype(F32)
        grad_in[at, :, width:] = piece[shard : 2 * shard, :].astype(F32)
        grad_out[at] = piece[2 * shard :, :].astype(F32)


def owner_grads(facts, pieces, in_shape, out_shape):
    return kernel_call(
        owner_kernel,
        "owner_grads",
        [(in_shape, F32), (out_shape, F32)],
        [facts, *pieces],
        [SM] + [VM] * len(pieces),
        size=24 * pieces[0].size,
    )


def attn_grad_kernel(attn_in, grad_proj, mixed, low, own, other):
    width = attn_in.shape[1]
    cols = own.shape[1]
    for at, target in ((0, own), (1, other)):
        for part in range(3):
            target[part * width : (part + 1) * width, :] = dot_tn(
                attn_in[...], grad_proj[at, part]
            ).astype(BF)
        for side in range(2):
            spot = 3 * width + side * cols
            target[spot : spot + cols, :] = dot_tn(
                mixed[:, at * cols : (at + 1) * cols], low[:, side * cols : (side + 1) * cols]
            ).astype(BF)


def attn_grads(attn_in, grad_proj, mixed, low):
    pack, width = attn_in.shape
    cols = grad_proj.shape[3]
    return kernel_call(
        attn_grad_kernel,
        "attn_grads",
        [((3 * width + 2 * cols, cols), BF)] * 2,
        [attn_in, grad_proj, mixed, low],
        [VM] * 4,
        flops=8 * pack * width * width,
        size=8 * width * width,
    )


def attn_split_kernel(facts, own, came, *refs):
    sends, keeps = refs[:4], refs[4:]
    cols = own.shape[1]
    width = 2 * cols
    shard = width // 8
    for step in range(4):
        owner = jnp.bitwise_xor(facts[MINE], step) * 2
        for rep, target in ((1 - facts[REP], sends[step]), (facts[REP], keeps[step])):
            at = owner + rep
            for source, rows, spot in attn_rows(width, shard):
                where = pl.ds(pl.multiple_of(source + at * rows, rows), rows)
                target[spot : spot + rows, :] = (
                    own[where, :].astype(F32) + came[where, :].astype(F32)
                ).astype(BF)


def attn_rows(width, shard):
    out = shard // 2
    return (
        (0, shard, 0),
        (width, shard, shard),
        (2 * width, shard, 2 * shard),
        (3 * width, out, 3 * shard),
        (3 * width + width // 2, out, 3 * shard + out),
    )


def attn_split(facts, own, came):
    rows, cols = own.shape
    return kernel_call(
        attn_split_kernel,
        "attn_split",
        [((rows // 8, cols), BF)] * 8,
        [facts, own, came],
        [SM, VM, VM],
        size=6 * rows * cols,
    )


def solution(mesh):
    shape = mesh.shape
    n_pipe, n_dp, n_t = shape["pipe"], shape["dp"], shape["tensor"]
    axes = ("pipe", "dp", "tensor")
    plane = ("dp", "tensor")
    n_dev = n_dp * n_t

    def local(
        inputs,
        cotangent,
        dealing,
        routes,
        slot_order,
        doc_lengths,
        attn_weight,
        attn_out_weight,
        expert_in_weight,
        expert_out_weight,
        norm_gains,
        router_weight,
    ):
        dev_rows, width = inputs.shape
        experts = expert_in_weight.shape[1]
        reps = n_dp // experts
        paired = reps == 2
        pack = dev_rows
        cap = pack // experts
        per = dev_rows // n_dev
        shard, cols = attn_weight.shape[1], attn_weight.shape[3]
        ff = expert_in_weight.shape[3]
        in_rows, out_rows = expert_in_weight.shape[2], expert_out_weight.shape[2]
        pipe = lax.axis_index("pipe")
        dp = lax.axis_index("dp")
        core = lax.axis_index("tensor")
        mine = dp // reps
        rep = dp % reps
        lengths = lax.dynamic_index_in_dim(doc_lengths, core, 0, keepdims=False)
        zero = jnp.int32(0)
        facts = jnp.stack([pipe, mine, rep, core, lengths[0], zero, zero, zero]).astype(jnp.int32)

        def moved(value, rule):
            pairs = []
            for a in range(n_pipe):
                for b in range(experts):
                    for c in range(reps):
                        for d in range(n_t):
                            to = rule(a, b, c, d)
                            if to is not None:
                                flat = [
                                    ((w * experts + x) * reps + y) * n_t + z
                                    for w, x, y, z in ((a, b, c, d), to)
                                ]
                                pairs.append(tuple(flat))
            return lax.ppermute(value, axes, pairs)

        def swap_core(value):
            return moved(value, lambda a, b, c, d: (a, b, c, 1 - d))

        def swap_rep(value):
            return moved(value, lambda a, b, c, d: (a, b, 1 - c, d))

        def across(step):
            return lambda a, b, c, d: (a, b ^ step, c, d)

        def up(step):
            return lambda a, b, c, d: (1, b ^ step, c, d) if a == 0 else None

        def down(step):
            return lambda a, b, c, d: (0, b ^ step, c, d) if a == 1 else None

        order = (2, 3, 1)

        def exchange(blocks):
            out = {0: blocks[0]}
            for step in order:
                out[step] = moved(blocks[step], across(step))
            return [out[step] for step in range(experts)]

        def crossed(blocks, way):
            out = {}
            for step in (*order, 0):
                out[step] = moved(blocks[step], way(step))
            return [out[step] for step in range(experts)]

        def with_other(blocks):
            out = {}
            for step in (0, 1, 2, 3):
                out[step] = swap_core(blocks[step])
            return list(blocks) + [out[step] for step in range(experts)]

        def pick(blocks, step):
            return lax.dynamic_index_in_dim(blocks, mine ^ step, 0, keepdims=False)

        rep_groups = [[b * reps + c for c in range(reps)] for b in range(experts)]

        target = dealing // dev_rows
        rows_at = jnp.arange(dev_rows)
        earlier = (target[:, None] == target[None, :]) & (rows_at[None, :] < rows_at[:, None])
        send_slot = target * per + jnp.sum(earlier.astype(jnp.int32), axis=1)
        send_hot = (rows_at[:, None] == send_slot[None, :]).astype(BF)
        small = jnp.concatenate([norm_gains[0].reshape(-1), router_weight[0].reshape(-1)])
        small_high = lax.reduce_precision(small, 8, 7)
        small_mid = lax.reduce_precision(small - small_high, 8, 7)
        small_low = lax.reduce_precision(small - small_high - small_mid, 8, 7)
        small_cols = 3 * small.shape[0] // per
        params = jnp.concatenate([small_high, small_mid, small_low]).astype(BF)
        params = jnp.tile(params.reshape(per, small_cols), (n_dev, 1))
        numbers = jnp.stack(
            [dealing % dev_rows, routes[:, 0], slot_order // 256, slot_order % 256], axis=1
        ).astype(BF)
        payload = jnp.concatenate([jnp.where(pipe == 0, inputs, cotangent), numbers], axis=1)
        payload = dot32(send_hot, payload).astype(BF)
        blank = jnp.zeros((dev_rows, EXTRA - 4 - small_cols), BF)
        payload = jnp.concatenate([payload, params, blank], axis=1)
        dealt = lax.all_to_all(payload, plane, split_axis=0, concat_axis=0, tiled=True)
        parts = dealt[:, width + 4 : width + 4 + small_cols].reshape(n_dev, 3, -1)
        gain_count = norm_gains.shape[1] * norm_gains.shape[2]
        gains = jnp.sum(parts[:, :, :gain_count].astype(F32), axis=1)
        gains = jnp.swapaxes(gains.reshape(n_dev, 2, -1), 0, 1).reshape(2, width)
        router = parts[:, :, gain_count:].reshape(n_dev, 3, -1, experts)
        router3 = jnp.swapaxes(router, 1, 2).reshape(width, 3 * experts)
        router3 = jnp.pad(router3, ((0, 0), (0, EXTRA - 3 * experts)))
        router = jnp.sum(router.astype(F32), axis=1).reshape(width, experts)
        router = jnp.pad(router.T, ((0, EXTRA - experts), (0, 0)))
        both = lax.all_gather(dealt, "tensor", axis=0, tiled=True)
        own_rows, slots, onehot, place = kernel_call(
            deal_kernel,
            "deal",
            [((pack, width), BF), ((pack, pack), BF), ((pack, EXTRA), F32), ((2 * pack, pack), BF)],
            [facts, both],
            [SM, VM],
            flops=4 * pack * pack * width,
            size=4 * pack * width,
        )
        plan = (slots, onehot)

        out_shard = attn_out_weight[0]
        attn_bundle = jnp.concatenate(
            [attn_weight[0, :, part] for part in range(3)] + [out_shard[:, :cols], out_shard[:, cols:]],
            axis=0,
        )
        attn_shape = (4 * width, cols)

        def attn_places(way, step):
            def spots(numbers):
                owner = jnp.bitwise_xor(numbers[MINE], step) * 2
                owner = owner + (numbers[REP] if way == 0 else 1 - numbers[REP])
                return [
                    (spot, pl.multiple_of(source + owner * rows, rows), rows, 0, cols)
                    for source, rows, spot in attn_rows(width, shard)
                ]

            return spots

        def expert_places(way, step):
            def owner_of(numbers):
                owner = jnp.bitwise_xor(numbers[MINE], step) * 2
                return owner + (numbers[REP] if way == 0 else 1 - numbers[REP])

            def spots_in(numbers):
                at = pl.multiple_of(owner_of(numbers) * in_rows, in_rows)
                return [(0, at, in_rows, 0, width), (in_rows, at, in_rows, width, width)]

            def spots_out(numbers):
                at = pl.multiple_of(owner_of(numbers) * out_rows, out_rows)
                return [(2 * in_rows, at, out_rows, 0, width)]

            return spots_in, spots_out

        if paired:
            attn_near = exchange([attn_bundle] * experts)
            w_in_raw = expert_in_weight[0]
            w_out_raw = expert_out_weight[0]
            bundles = []
            for step in range(experts):
                piece = pick(w_in_raw, step)
                bundles.append(
                    jnp.concatenate(
                        [piece[:, :width], piece[:, width:], pick(w_out_raw, step)], axis=0
                    )
                )
            attn_far = [swap_rep(piece) for piece in attn_near]
            attn_own = gather_pieces(
                facts,
                attn_near + attn_far,
                [attn_places(way, step) for way in range(2) for step in range(experts)],
                attn_shape,
            )
            near = exchange(bundles)
            far = {}
            for step in (0, 1, 2, 3):
                far[step] = swap_rep(near[step])
            pieces = near + [far[step] for step in range(experts)]
            both_places = [
                expert_places(way, step) for way in range(2) for step in range(experts)
            ]
            places = ([each[0] for each in both_places], [each[1] for each in both_places])
        else:
            every = lax.all_gather(attn_bundle, "dp", axis=0)
            attn_own = jnp.concatenate(
                [
                    every[:, spot : spot + rows].reshape(-1, cols)
                    for _, rows, spot in attn_rows(width, shard)
                ],
                axis=0,
            )

            def assembled(blocks):
                got = exchange([pick(blocks, step) for step in range(experts)])
                got = jnp.stack(got)
                got = jnp.stack([pick(got, owner) for owner in range(experts)])
                got = lax.all_gather(got, "dp", axis_index_groups=rep_groups)
                return jnp.swapaxes(got, 0, 1)

            pieces = [
                assembled(expert_in_weight[0]).reshape(width, ff),
                assembled(expert_out_weight[0]).reshape(ff, width),
            ]
            places = (
                [lambda numbers: [(0, 0, width, 0, ff)], lambda numbers: []],
                [lambda numbers: [], lambda numbers: [(0, 0, ff, 0, width)]],
            )
        attn_other = swap_core(attn_own)
        weights = (attn_own, attn_other, gains, router3, router)

        def expert_forward(blocks, name):
            pre, act, own, other = expert_call(
                expert_kernel, name, facts, blocks, None, pieces, places, width, ff
            )
            return pre, act, fold(own, swap_core(other), "fold_" + name)

        def expert_backward(blocks, pre, name):
            grad_pre, own, other = expert_call(
                expert_back_kernel, name, facts, blocks, pre, pieces, places, width, ff
            )
            return grad_pre, fold(own, swap_core(other), "fold_" + name)

        out = attn_forward(facts, own_rows, weights, plan)
        mid_up = moved(out[0], lambda a, b, c, d: (1, b, c, d) if a == 0 else None)
        blocks = with_other(exchange(out[6:10]))
        _, _, expert_slots = expert_forward(blocks, "expert_first")
        from_first = crossed(expert_slots, up)

        out = attn_forward(facts, own_rows, weights, plan, (mid_up, *from_first))
        mid, attn_in, proj, mixed, mlp_in, probs = out[:6]
        stream = out[10]
        blocks = with_other(exchange(out[6:10]))
        grads = exchange(out[11:15])
        pre, act, expert_slots = expert_forward(blocks, "expert_second")
        expert_slots = exchange(expert_slots)

        saved = (stream, mid, proj, mlp_in, probs)
        _, grad_slots = expert_backward(with_other(grads), pre, "expert_back_first")
        back = attn_backward(
            facts, own_rows, mid_up, exchange(grad_slots), expert_slots, saved, weights, plan, True
        )
        grad_down = moved(back[0], lambda a, b, c, d: (0, b, c, d) if a == 1 else None)
        got_down = crossed(back[1:5], down)

        grads = with_other(
            [jnp.where(pipe == 0, came, kept) for came, kept in zip(got_down, grads)]
        )
        grad_pre, grad_slots = expert_backward(grads, pre, "expert_back_second")
        layer_grad, grad_proj, low, grad_gains, grad_router = attn_backward(
            facts,
            grad_down,
            own_rows,
            exchange(grad_slots),
            expert_slots,
            saved,
            weights,
            plan,
            False,
        )

        if paired:
            out = expert_grads(facts, blocks, grads, act, grad_pre, True)
            sums = {}
            for step in (*order, 0):
                came = swap_rep(out[step])
                total = (out[4 + step].astype(F32) + came.astype(F32)).astype(BF)
                sums[step] = moved(total, across(step)) if step else total
            grad_expert_in, grad_expert_out = owner_grads(
                facts,
                [sums[step] for step in range(experts)],
                expert_in_weight.shape[1:],
                expert_out_weight.shape[1:],
            )
        else:

            def rep_scatter(each):
                return lax.psum_scatter(
                    each, "dp", axis_index_groups=rep_groups, scatter_dimension=0
                )

            def to_owner(grad, rows_each):
                each = grad.reshape(experts, reps, rows_each, -1).astype(BF)
                summed = rep_scatter(jnp.swapaxes(each, 0, 1))
                got = exchange([pick(summed, step) for step in range(experts)])
                got = jnp.stack(got)
                return jnp.stack([pick(got, owner) for owner in range(experts)]).astype(F32)

            grad_w_in, grad_w_out = expert_grads(facts, blocks, grads, act, grad_pre, False)
            grad_expert_in = to_owner(grad_w_in, in_rows)
            grad_expert_out = to_owner(grad_w_out, out_rows)

        grad_own, grad_other = attn_grads(attn_in, grad_proj, mixed, low)
        came = swap_core(grad_other)
        if paired:
            out = attn_split(facts, grad_own, came)
            total = None
            sums = {}
            for step in (*order, 0):
                came = swap_rep(out[step])
                both = out[4 + step].astype(F32) + came.astype(F32)
                sums[step] = moved(both.astype(BF), across(step)).astype(F32) if step else both
            total = sums[0] + sums[1] + sums[2] + sums[3]
        else:
            full = grad_own.astype(F32) + came.astype(F32)
            pieces_of = [
                full[source : source + rows * n_dp].reshape(n_dp, rows, cols)
                for source, rows, _ in attn_rows(width, shard)
            ]
            full = jnp.concatenate(pieces_of, axis=1).astype(BF)
            full = full.reshape((experts, reps) + full.shape[1:])
            full = rep_scatter(jnp.swapaxes(full, 0, 1))
            got = exchange([pick(full, step) for step in range(experts)])
            total = sum(each.astype(F32) for each in got)
        grad_attn = total[: 3 * shard].reshape(3, shard, cols)
        grad_attn = jnp.swapaxes(grad_attn, 0, 1)[None]
        rows = shard // 2
        grad_attn_out = jnp.concatenate(
            [total[3 * shard : 3 * shard + rows], total[3 * shard + rows :]], axis=1
        )[None]

        tiny = jnp.concatenate(
            [
                jnp.swapaxes(grad_gains.reshape(2, n_dev, -1), 0, 1).reshape(n_dev, -1),
                grad_router[:, :experts].reshape(n_dev, -1),
            ],
            axis=1,
        )
        tiny_count = tiny.shape[1]
        tiny = jnp.pad(tiny, ((0, 0), (0, -tiny_count % EXTRA))).reshape(n_dev, -1, EXTRA)
        tiny = lax.all_to_all(tiny, plane, split_axis=0, concat_axis=0, tiled=True)
        tiny = jnp.sum(tiny, axis=0).reshape(-1)[:tiny_count]
        tiny_gains = tiny[:gain_count].reshape(1, 2, -1)
        tiny_router = tiny[gain_count:].reshape(1, -1, experts)

        def sent_back(merge, rows, extra):
            own, other = sent_rows(facts, merge, rows, extra, place, width)
            full = own + swap_core(other)
            back = lax.all_to_all(full, plane, split_axis=0, concat_axis=0, tiled=True)
            return dot_tn(send_hot, back).astype(BF)[None]

        return (
            sent_back(True, mid, (slots, *expert_slots)),
            sent_back(False, layer_grad, ()),
            grad_attn,
            grad_attn_out,
            grad_expert_in[None],
            grad_expert_out[None],
            tiny_gains,
            tiny_router,
        )

    in_specs = (
        P(("dp", "tensor"), None),
        P(("dp", "tensor"), None),
        P(("dp", "tensor")),
        P(("dp", "tensor"), None),
        P(("dp", "tensor")),
        P("dp", None),
        P("pipe", "dp", None, "tensor"),
        P("pipe", ("tensor", "dp"), None),
        P("pipe", None, "dp", "tensor"),
        P("pipe", None, ("tensor", "dp"), None),
        P("pipe", None, ("dp", "tensor")),
        P("pipe", ("dp", "tensor"), None),
    )
    out_specs = (
        P("pipe", ("dp", "tensor"), None),
        P("pipe", ("dp", "tensor"), None),
        P("pipe", "dp", None, "tensor"),
        P("pipe", ("tensor", "dp"), None),
        P("pipe", None, "dp", "tensor"),
        P("pipe", None, ("tensor", "dp"), None),
        P("pipe", None, ("dp", "tensor")),
        P("pipe", ("dp", "tensor"), None),
    )
    return jax.shard_map(local, mesh=mesh, in_specs=in_specs, out_specs=out_specs, check_vma=False)
```

time: 618 us -> 501 us (0.81)
  Pallas kernels: 0 us -> 115 us
  matrix products: 116 us -> 4.48 us
  local copies, waits for them, and re-layouts: 83.8 us -> 27.6 us
  other arithmetic: 47.9 us -> 16.9 us
  starting transfers between devices: 145 us -> 122 us
  between operations: 16.5 us -> 2.11 us
    pallas_call x0 -> x20, Pallas kernels: none -> 115 us  [the longest x19 111 us: kernel_call(): pl.pallas_call(body, name=name, out_shape=[jax.ShapeDtypeStruct(shape, ki...]
    dot_general x22 -> x0, matrix products: 73.6 us -> none  [the longest x7 25.8 us: dot_nt(): lax.dot_general(a, b, (((1,), (1,)), ((), ())), preferred_element_type=F32)]
    ppermute x61 -> x80, waiting for transfers between devices: 198 us -> 166 us  [moved(): return lax.ppermute(value, axes, pairs)]
    all_to_all x0 -> x1, waiting for transfers between devices: none -> 28.4 us  [local(): tiny = lax.all_to_all(tiny, plane, split_axis=0, concat_axis=0, tiled=True)]
    ppermute x61 -> x80, starting transfers between devices: 129 us -> 102 us  [moved(): return lax.ppermute(value, axes, pairs)]
    reshape x19 -> x12, local copies, waits for them, and re-layouts: 29.1 us -> 2.06 us  [the longest x1 0.63 us: local(): jnp.pad(tiny, ((0, 0), (0, -tiny_count % EXTRA))).reshape(n_dev, -1, EXTRA)]
    dot_general x13 -> x1, matrix products: 17.6 us -> 0.32 us  [dot32(): return jnp.dot(a, b, preferred_element_type=F32)]
    slice x26 -> x10, local copies, waits for them, and re-layouts: 17.3 us -> 1.95 us  [the longest x1 0.79 us: local(): grad_attn = total[:3 * shard].reshape(3, shard, cols)]
  transfers between devices with their start and end apart: 65 -> 84, of which waited for: 26 -> 32; matrix products, arithmetic and copies ran while one was open for 29% -> 6% of each run, Pallas kernels for 0% -> 12%
where the time goes in v2:
time: 501 us; the launch traced here: 492 us
  waiting for transfers between devices  202 us (40%)
  starting transfers between devices  122 us (24%)
  Pallas kernels  115 us (23%)
  local copies, waits for them, and re-layouts  27.6 us (6%)
  other arithmetic  16.9 us (3%)
    ppermute x80, waiting for transfers between devices, moved(): return lax.ppermute(value, axes, pairs)  166 us
    pallas_call x19, Pallas kernels, kernel_call(): pl.pallas_call(body, name=name, out_shape=[jax.ShapeDtypeStruct(shape, ki...  111 us
    ppermute x80, starting transfers between devices, moved(): return lax.ppermute(value, axes, pairs)  102 us
    all_to_all x1, waiting for transfers between devices, local(): tiny = lax.all_to_all(tiny, plane, split_axis=0, concat_axis=0, tiled=True)  28.4 us
    unnamed x112, local copies, waits for them, and re-layouts  18.1 us
  transfers between devices with their start and end apart: 84, of which 32 were waited for; matrix products, arithmetic and copies ran while one was open for 6% of the time, Pallas kernels for 12%

profile of v2, /device:TPU:0, one launch (start us, length us, event | category | flops | bytes accessed | tf_op | source)
XLA Modules:
  0.0 492.3 jit_solution(8132375306432967213)
XLA Ops:
  5.0 3.0 collective-permute-start
  8.0 2.6 collective-permute-start.1
  16.7 3.9 collective-permute-done.refs_1_
  22.3 9.2 %collective-permute-done.1.refs_2_ = bf16[384,384]{1,0:T(8,128)(2,1)S(1)} collective-permute-done((bf16[384,384]{1,0:T(8,128)(2,1)S(1)}, bf16[384,384]{1,0:T(8,128)(2,1)S(1)}, u32[]{:S(2)}, u32[]{:S(2)}) %collective-permute-start.1) | collective-permute-done | bytes 294944 | tf_op jit(solution)/shard_map/ppermute | solution.py:713
  39.0 2.4 collective-permute-done.6.refs_7_
  46.0 4.5 gather_pieces.1.refs_1_.refs_6_.refs_15_
  51.7 6.5 %all-to-all-start = ((bf16[16,16,896]{2,1,0:T(8,128)(2,1)}), bf16[16,16,896]{2,1,0:T(8,128)(2,1)S(1)}, u32[]{:S(2)}, u32[]{:S(2)}) async-start(bf16[16,16,896]{2,1,0:T(8,128)(2,1)} %maximum_maximum_fusion), calls=%async_computation | async-start | bytes 917504 | tf_op jit(solution)/shard_map/all_to_all | solution.py:774
  60.0 2.0 collective-permute-start.16
  62.1 2.4 collective-permute-start.17
  65.6 1.9 collective-permute-start.19
  67.5 25.2 %collective-permute-done.16.refs_9_.refs_10_ = bf16[384,768]{1,0:T(8,128)(2,1)} collective-permute-done((bf16[384,768]{1,0:T(8,128)(2,1)S(1)}, bf16[384,768]{1,0:T(8,128)(2,1)}, u32[]{:S(2)}, u32[]{:S(2)}) %collective-permute-start.16) | collective-permute-done | bytes 589856 | tf_op jit(solution)/shard_map/ppermute | solution.py:713
  94.1 16.4 %collective-permute-done.17.refs_10_.refs_11_ = bf16[384,768]{1,0:T(8,128)(2,1)} collective-permute-done((bf16[384,768]{1,0:T(8,128)(2,1)S(1)}, bf16[384,768]{1,0:T(8,128)(2,1)}, u32[]{:S(2)}, u32[]{:S(2)}) %collective-permute-start.17) | collective-permute-done | bytes 589856 | tf_op jit(solution)/shard_map/ppermute | solution.py:713
  113.8 2.5 all_gather.3.both
  117.6 9.0 %attn_first.1 = (f32[256,896]{1,0:T(8,128)S(1)}, bf16[256,768]{1,0:T(8,128)(2,1)}, bf16[2,3,256,384]{3,2,1,0:T(8,128)(2,1)}, bf16[256,768]{1,0:T(8,128)(2,1)}, b...) custom-call(s32[8]{0:T(128)S(1)} %stack.33.facts.refs_7_.refs_2_, ...), custom_call_target="tpu_custom_call" | custom-call | flops 1509949440 | bytes 4718592 | tf_op jit(solution)/shard_map/attn_first/pallas_call | solution.py:48
  126.6 3.9 collective-permute-start.8
  130.6 12.2 %collective-permute-start.9 = (bf16[64,768]{1,0:T(8,128)(2,1)S(1)}, bf16[64,768]{1,0:T(8,128)(2,1)S(1)}, u32[]{:S(2)}, u32[]{:S(2)}) collective-permute-start(bf16[64,768]{1,0:T(8,128)(2,1)S(1)} %get-tuple-element.98), channel_id=1, source_target_pairs={{0,4},{1,5},{2,6},{3,7},{4,0},{5,1},{6,2},{7,3},{8,12},{9,13},{10,... | collective-permute-start | bytes 294920 | tf_op jit(solution)/shard_map/ppermute | solution.py:713
  142.9 2.4 collective-permute-start.11
  146.0 6.8 %collective-permute-done.10.refs_2_ = bf16[64,768]{1,0:T(8,128)(2,1)S(1)} collective-permute-done((bf16[64,768]{1,0:T(8,128)(2,1)S(1)}, bf16[64,768]{1,0:T(8,128)(2,1)S(1)}, u32[]{:S(2)}, u32[]{:S(2)}) %collective-permute-start.10) | collective-permute-done | bytes 98336 | tf_op jit(solution)/shard_map/ppermute | solution.py:713
  154.3 9.4 %expert_first.1 = (f32[512,1536]{1,0:T(8,128)}, bf16[512,1536]{1,0:T(8,128)(2,1)}, f32[256,768]{1,0:T(8,128)}, bf16[256,768]{1,0:T(8,128)(2,1)S(1)}) custom-call(s32[8]{0:T(128)S(1)} %stack.33.facts.refs_7_.refs_2_, bf16[64,768]{1,0:T(8,128)(2,1)S(1)} %get-tuple-element.97.refs_0_, bf16[64,768]{1,0:T(8,128)(2,1)S(1)} %collective-permute-done.9.refs_1_, ...), custom_call_target="tpu_custom_call" | custom-call | flops 2415919104 | bytes 7077888 | tf_op jit(solution)/shard_map/expert_first/pallas_call | solution.py:48
  168.2 2.6 collective-permute-start.25
  173.9 2.2 collective-permute-done.26.refs_4_
  178.3 9.5 %attn_second.1 = (f32[256,896]{1,0:T(8,128)}, bf16[256,768]{1,0:T(8,128)(2,1)S(1)}, bf16[2,3,256,384]{3,2,1,0:T(8,128)(2,1)}, bf16[256,768]{1,0:T(8,128)(2,1)S(1...) custom-call(s32[8]{0:T(128)S(1)} %stack.33.facts.refs_7_.refs_2_, ...), custom_call_target="tpu_custom_call" | custom-call | flops 1509949440 | bytes 4718592 | tf_op jit(solution)/shard_map/attn_second/pallas_call | solution.py:48
  189.4 4.1 collective-permute-start.28
  194.0 1.8 collective-permute-start.30
  197.0 2.8 collective-permute-start.41
  199.8 4.6 collective-permute-done.29.refs_2_
  204.4 2.0 collective-permute-start.42
  207.0 4.9 collective-permute-done.41.refs_2_
  212.9 9.3 %expert_second.1 = (f32[512,1536]{1,0:T(8,128)}, bf16[512,1536]{1,0:T(8,128)(2,1)}, f32[256,768]{1,0:T(8,128)}, bf16[256,768]{1,0:T(8,128)(2,1)S(1)}) custom-call(s32[8]{0:T(128)S(1)} %stack.33.facts.refs_7_.refs_2_, bf16[64,768]{1,0:T(8,128)(2,1)S(1)} %get-tuple-element.108.refs_0_, bf16[64,768]{1,0:T(8,128)(2,1)S(1)} %collective-permute-done.28.refs_1_, ...), custom_call_target="tpu_custom_call" | custom-call | flops 2415919104 | bytes 7077888 | tf_op jit(solution)/shard_map/expert_second/pallas_call | solution.py:48
  222.5 10.5 %expert_back_first.1 = (bf16[512,1536]{1,0:T(8,128)(2,1)}, f32[256,768]{1,0:T(8,128)}, bf16[256,768]{1,0:T(8,128)(2,1)S(1)}) custom-call(s32[8]{0:T(128)S(1)} %stack.33.facts.refs_7_.refs_2_, bf16[64,768]{1,0:T(8,128)(2,1)S(1)} %get-tuple-element.121.refs_0_, bf16[64,768]{1,0:T(8,128)(2,1)S(1)} %collective-permute-done.40.refs_1_, ...), custom_call_target="tpu_custom_call" | custom-call | flops 2415919104 | bytes 7077888 | tf_op jit(solution)/shard_map/expert_back_first/pallas_call | solution.py:48
  236.7 1.9 collective-permute-start.38
  239.7 2.0 collective-permute-start.49
  241.8 1.9 collective-permute-start.50
  244.3 2.3 collective-permute-done.37.refs_4_.refs_8_
  246.7 8.3 %collective-permute-done.49.refs_4_ = bf16[64,768]{1,0:T(8,128)(2,1)S(1)} collective-permute-done((bf16[64,768]{1,0:T(8,128)(2,1)}, bf16[64,768]{1,0:T(8,128)(2,1)S(1)}, u32[]{:S(2)}, u32[]{:S(2)}) %collective-permute-start.49) | collective-permute-done | bytes 98336 | tf_op jit(solution)/shard_map/ppermute | solution.py:713
  254.9 14.5 %attn_back_first.1 = (bf16[256,768]{1,0:T(8,128)(2,1)S(1)}, bf16[64,768]{1,0:T(8,128)(2,1)S(1)}, bf16[64,768]{1,0:T(8,128)(2,1)S(1)}, bf16[64,768]{1,0:T(8,128)(...) custom-call(s32[8]{0:T(128)S(1)} %stack.33.facts.refs_7_.refs_2_, ...), custom_call_target="tpu_custom_call" | custom-call | flops 2415919104 | bytes 4718592 | tf_op jit(solution)/shard_map/attn_back_first/pallas_call | solution.py:48
  276.3 3.8 collective-permute-done.53
  280.3 5.3 %collective-permute-done.54 = bf16[64,768]{1,0:T(8,128)(2,1)S(1)} collective-permute-done((bf16[64,768]{1,0:T(8,128)(2,1)S(1)}, bf16[64,768]{1,0:T(8,128)(2,1)S(1)}, u32[]{:S(2)}, u32[]{:S(2)}) %collective-permute-start.54) | collective-permute-done | bytes 98336 | tf_op jit(solution)/shard_map/ppermute | solution.py:713
  287.2 10.4 %expert_back_second.1 = (bf16[512,1536]{1,0:T(8,128)(2,1)}, f32[256,768]{1,0:T(8,128)}, bf16[256,768]{1,0:T(8,128)(2,1)S(1)}) custom-call(s32[8]{0:T(128)S(1)} %stack.33.facts.refs_7_.refs_2_, bf16[64,768]{1,0:T(8,128)(2,1)S(1)} %broadcast_select_fusion.4.refs_0_.refs_8_, bf16[64,768]{1,0:T(8,128)(2,1)S(1)} %broadcast_select_fusion.3.refs_1_.refs_9_, ...), custom_call_target="tpu_custom_call" | custom-call | flops 2415919104 | bytes 7077888 | tf_op jit(solution)/shard_map/expert_back_second/pallas_call | solution.py:48
  305.1 5.9 %collective-permute-done.51.refs_0_ = bf16[256,768]{1,0:T(8,128)(2,1)S(1)} collective-permute-done((bf16[256,768]{1,0:T(8,128)(2,1)S(1)}, bf16[256,768]{1,0:T(8,128)(2,1)S(1)}, u32[]{:S(2)}, u32[]{:S(2)}) %collective-permute-start.51) | collective-permute-done | bytes 393248 | tf_op jit(solution)/shard_map/ppermute | solution.py:713
  311.0 1.8 collective-permute-done.62.refs_4_
  312.8 14.7 %attn_back_second.1 = (bf16[256,768]{1,0:T(8,128)(2,1)S(1)}, bf16[2,3,256,384]{3,2,1,0:T(8,128)(2,1)}, bf16[256,768]{1,0:T(8,128)(2,1)S(1)}, f32[2,768]{1,0:T(2,128)S(1)}, f32[768,128]{1,0:T(8,128)S(1)}) custom-call(s32[8]{0:T(128)S(1)} %stack.33.facts.refs_7_.refs_2_, bf16[256,768]{1,0:T(8,128)(2,1)S(1)} %collective-permute-done.51.refs_0_, ...), custom_call_target="tpu_custom_call" | custom-call | flops 2415919104 | bytes 4718592 | tf_op jit(solution)/shard_map/attn_back_second/pallas_call | solution.py:48
  329.0 3.7 attn_grads.1
  332.9 8.7 %expert_grads.1 = (bf16[384,768]{1,0:T(8,128)(2,1)}, bf16[384,768]{1,0:T(8,128)(2,1)}, bf16[384,768]{1,0:T(8,128)(2,1)}, bf16[384,768]{1,0:T(8,128)(2,1)}, bf16[...) custom-call(s32[8]{0:T(128)S(1)} %stack.33.facts.refs_7_.refs_2_, ...), custom_call_target="tpu_custom_call" | custom-call | flops 2415919104 | bytes 9437184 | tf_op jit(solution)/shard_map/expert_grads/pallas_call | solution.py:48
  346.8 4.7 all-to-all-start.3
  351.5 2.0 collective-permute-start.73
  355.2 28.4 %all-to-all-done.3 = f32[16,3,128]{2,1,0:T(4,128)S(1)} async-done(((f32[16,3,128]{2,1,0:T(4,128)}), f32[16,3,128]{2,1,0:T(4,128)S(1)}, u32[]{:S(2)}, u32[]{:S(2)}) %all-to-all-start.3) | async-done | bytes 24608 | tf_op jit(solution)/shard_map/all_to_all | solution.py:1004
  383.6 4.2 all-to-all-start.1
  392.3 3.0 attn_split.1
  396.9 2.0 add_convert_fusion.1
  399.4 2.0 add_convert_fusion
  401.5 2.4 collective-permute-start.77
  404.7 2.0 collective-permute-done.71
  407.4 5.7 %collective-permute-done.69 = bf16[384,384]{1,0:T(8,128)(2,1)} collective-permute-done((bf16[384,384]{1,0:T(8,128)(2,1)S(1)}, bf16[384,384]{1,0:T(8,128)(2,1)}, u32[]{:S(2)}, u32[]{:S(2)}) %collective-permute-start.69) | collective-permute-done | bytes 294944 | tf_op jit(solution)/shard_map/ppermute | solution.py:713
  413.2 1.9 collective-permute-start.79
  415.1 4.2 all-to-all-start.2
  419.3 1.8 add_convert_fusion.5
  423.9 3.4 collective-permute-start.72
  427.4 33.6 %collective-permute-done.77.refs_2_ = bf16[384,768]{1,0:T(8,128)(2,1)S(1)} collective-permute-done((bf16[384,768]{1,0:T(8,128)(2,1)}, bf16[384,768]{1,0:T(8,128)(2,1)S(1)}, u32[]{:S(2)}, u32[]{:S(2)}) %collective-permute-start.77) | collective-permute-done | bytes 589856 | tf_op jit(solution)/shard_map/ppermute | solution.py:713
  462.2 2.1 fusion
  464.3 3.0 owner_grads.1
  467.3 7.9 %all-to-all-done.2 = bf16[16,16,768]{2,1,0:T(8,128)(2,1)} async-done(((bf16[16,16,768]{2,1,0:T(8,128)(2,1)}), bf16[16,16,768]{2,1,0:T(8,128)(2,1)}, u32[]{:S(2)}, u32[]{:S(2)}) %all-to-all-start.2) | async-done | bytes 393248 | tf_op jit(solution)/shard_map/all_to_all | solution.py:1012
  475.2 2.1 fusion.1
  477.3 11.8 %collective-permute-done.70 = bf16[384,384]{1,0:T(8,128)(2,1)} collective-permute-done((bf16[384,384]{1,0:T(8,128)(2,1)}, bf16[384,384]{1,0:T(8,128)(2,1)}, u32[]{:S(2)}, u32[]{:S(2)}) %collective-permute-start.70) | collective-permute-done | bytes 294944 | tf_op jit(solution)/shard_map/ppermute | solution.py:713
  (316 shorter events, 96.2 us)
Async XLA Ops:
  5.0 15.6 %collective-permute-start = (bf16[384,384]{1,0:T(8,128)(2,1)S(1)}, bf16[384,384]{1,0:T(8,128)(2,1)S(1)}, u32[]{:S(2)}, u32[]{:S(2)}) collective-permute-start(bf16[384,384]{1,0:T(8,128)(2,1)S(1)} %slice_dynamic-update-slice_fusion.refs_0_), channel_id=1, source_target_pairs={{0,4},{1,5},{2,6},{3,7},{4,0},{5,1},{6,2},{7,3},{8,12},{9,13},{10,... | collective-permute-start | bytes 884744 | tf_op jit(solution)/shard_map/ppermute | solution.py:713
  8.0 23.5 %collective-permute-start.1 = (bf16[384,384]{1,0:T(8,128)(2,1)S(1)}, bf16[384,384]{1,0:T(8,128)(2,1)S(1)}, u32[]{:S(2)}, u32[]{:S(2)}) collective-permute-start(bf16[384,384]{1,0:T(8,128)(2,1)S(1)} %slice_dynamic-update-slice_fusion.refs_0_), channel_id=1, source_target_pairs={{0,8},{1,9},{2,10},{3,11},{4,12},{5,13},{6,14},{7,15},{8,0},{9,1},... | collective-permute-start | bytes 884744 | tf_op jit(solution)/shard_map/ppermute | solution.py:713
  10.6 22.4 %collective-permute-start.2 = (bf16[384,384]{1,0:T(8,128)(2,1)S(1)}, bf16[384,384]{1,0:T(8,128)(2,1)S(1)}, u32[]{:S(2)}, u32[]{:S(2)}) collective-permute-start(bf16[384,384]{1,0:T(8,128)(2,1)S(1)} %slice_dynamic-update-slice_fusion.refs_0_), channel_id=1, source_target_pairs={{0,12},{1,13},{2,14},{3,15},{4,8},{5,9},{6,10},{7,11},{8,4},{9,5},... | collective-permute-start | bytes 884744 | tf_op jit(solution)/shard_map/ppermute | solution.py:713
  10.6 24.4 %collective-permute-start.3 = (bf16[384,384]{1,0:T(8,128)(2,1)S(1)}, bf16[384,384]{1,0:T(8,128)(2,1)S(1)}, u32[]{:S(2)}, u32[]{:S(2)}) collective-permute-start(bf16[384,384]{1,0:T(8,128)(2,1)S(1)} %slice_dynamic-update-slice_fusion.refs_0_), channel_id=1, source_target_pairs={{0,2},{1,3},{2,0},{3,1},{4,6},{5,7},{6,4},{7,5},{8,10},{9,11},{10,... | collective-permute-start | bytes 884744 | tf_op jit(solution)/shard_map/ppermute | solution.py:713
  20.6 15.2 %collective-permute-start.4 = (bf16[384,384]{1,0:T(8,128)(2,1)S(1)}, bf16[384,384]{1,0:T(8,128)(2,1)S(1)}, u32[]{:S(2)}, u32[]{:S(2)}) collective-permute-start(bf16[384,384]{1,0:T(8,128)(2,1)S(1)} %collective-permute-done.refs_1_), channel_id=1, source_target_pairs={{0,2},{1,3},{2,0},{3,1},{4,6},{5,7},{6,4},{7,5},{8,10},{9,11},{10,... | collective-permute-start | bytes 884744 | tf_op jit(solution)/shard_map/ppermute | solution.py:713
  33.0 8.4 %collective-permute-start.6 = (bf16[384,384]{1,0:T(8,128)(2,1)S(1)}, bf16[384,384]{1,0:T(8,128)(2,1)S(1)}, u32[]{:S(2)}, u32[]{:S(2)}) collective-permute-start(bf16[384,384]{1,0:T(8,128)(2,1)S(1)} %collective-permute-done.2.refs_3_), channel_id=1, source_target_pairs={{0,2},{1,3},{2,0},{3,1},{4,6},{5,7},{6,4},{7,5},{8,10},{9,11},{10,... | collective-permute-start | bytes 884744 | tf_op jit(solution)/shard_map/ppermute | solution.py:713
  50.5 67.1 %collective-permute-start.7 = (bf16[3072,384]{1,0:T(8,128)(2,1)S(1)}, bf16[3072,384]{1,0:T(8,128)(2,1)}, u32[]{:S(2)}, u32[]{:S(2)}) collective-permute-start(bf16[3072,384]{1,0:T(8,128)(2,1)S(1)} %gather_pieces.1.refs_1_.refs_6_.refs_15_), channel_id=1, source_target_pairs={{0,1},{1,0},{2,3},{3,2},{4,5},{5,4},{6,7},{7,6},{8,9},{9,8},{10,11... | collective-permute-start | bytes 7077896 | tf_op jit(solution)/shard_map/ppermute | solution.py:713
  51.7 60.9 %all-to-all-start = ((bf16[16,16,896]{2,1,0:T(8,128)(2,1)}), bf16[16,16,896]{2,1,0:T(8,128)(2,1)S(1)}, u32[]{:S(2)}, u32[]{:S(2)}) async-start(bf16[16,16,896]{2,1,0:T(8,128)(2,1)} %maximum_maximum_fusion), calls=%async_computation | async-start | bytes 917504 | tf_op jit(solution)/shard_map/all_to_all | solution.py:774
  60.0 32.6 %collective-permute-start.16 = (bf16[384,768]{1,0:T(8,128)(2,1)S(1)}, bf16[384,768]{1,0:T(8,128)(2,1)}, u32[]{:S(2)}, u32[]{:S(2)}) collective-permute-start(bf16[384,768]{1,0:T(8,128)(2,1)S(1)} %pad_maximum_fusion.1), channel_id=1, source_target_pairs={{0,4},{1,5},{2,6},{3,7},{4,0},{5,1},{6,2},{7,3},{8,12},{9,13},{10,... | collective-permute-start | bytes 1769480 | tf_op jit(solution)/shard_map/ppermute | solution.py:713
  62.1 48.5 %collective-permute-start.17 = (bf16[384,768]{1,0:T(8,128)(2,1)S(1)}, bf16[384,768]{1,0:T(8,128)(2,1)}, u32[]{:S(2)}, u32[]{:S(2)}) collective-permute-start(bf16[384,768]{1,0:T(8,128)(2,1)S(1)} %pad_maximum_fusion.2), channel_id=1, source_target_pairs={{0,8},{1,9},{2,10},{3,11},{4,12},{5,13},{6,14},{7,15},{8,0},{9,1},... | collective-permute-start | bytes 1769480 | tf_op jit(solution)/shard_map/ppermute | solution.py:713
  64.6 47.4 %collective-permute-start.18 = (bf16[384,768]{1,0:T(8,128)(2,1)S(1)}, bf16[384,768]{1,0:T(8,128)(2,1)}, u32[]{:S(2)}, u32[]{:S(2)}) collective-permute-start(bf16[384,768]{1,0:T(8,128)(2,1)S(1)} %pad_maximum_fusion.3), channel_id=1, source_target_pairs={{0,12},{1,13},{2,14},{3,15},{4,8},{5,9},{6,10},{7,11},{8,4},{9,5},... | collective-permute-start | bytes 1769480 | tf_op jit(solution)/shard_map/ppermute | solution.py:713
  65.6 64.9 %collective-permute-start.19 = (bf16[384,768]{1,0:T(8,128)(2,1)}, bf16[384,768]{1,0:T(8,128)(2,1)}, u32[]{:S(2)}, u32[]{:S(2)}) collective-permute-start(bf16[384,768]{1,0:T(8,128)(2,1)} %pad_maximum_fusion.refs_8_.refs_9_), channel_id=1, source_target_pairs={{0,2},{1,3},{2,0},{3,1},{4,6},{5,7},{6,4},{7,5},{8,10},{9,11},{10,... | collective-permute-start | bytes 1769480 | tf_op jit(solution)/shard_map/ppermute | solution.py:713
  92.7 50.1 %collective-permute-start.20 = (bf16[384,768]{1,0:T(8,128)(2,1)}, bf16[384,768]{1,0:T(8,128)(2,1)}, u32[]{:S(2)}, u32[]{:S(2)}) collective-permute-start(bf16[384,768]{1,0:T(8,128)(2,1)} %collective-permute-done.16.refs_9_.refs_10_), channel_id=1, source_target_pairs={{0,2},{1,3},{2,0},{3,1},{4,6},{5,7},{6,4},{7,5},{8,10},{9,11},{10,... | collective-permute-start | bytes 1769480 | tf_op jit(solution)/shard_map/ppermute | solution.py:713
  110.6 32.3 %collective-permute-start.21 = (bf16[384,768]{1,0:T(8,128)(2,1)}, bf16[384,768]{1,0:T(8,128)(2,1)}, u32[]{:S(2)}, u32[]{:S(2)}) collective-permute-start(bf16[384,768]{1,0:T(8,128)(2,1)} %collective-permute-done.17.refs_10_.refs_11_), channel_id=1, source_target_pairs={{0,2},{1,3},{2,0},{3,1},{4,6},{5,7},{6,4},{7,5},{8,10},{9,11},{10,... | collective-permute-start | bytes 1769480 | tf_op jit(solution)/shard_map/ppermute | solution.py:713
  112.0 33.3 %collective-permute-start.22 = (bf16[384,768]{1,0:T(8,128)(2,1)}, bf16[384,768]{1,0:T(8,128)(2,1)}, u32[]{:S(2)}, u32[]{:S(2)}) collective-permute-start(bf16[384,768]{1,0:T(8,128)(2,1)} %collective-permute-done.18.refs_11_.refs_12_), channel_id=1, source_target_pairs={{0,2},{1,3},{2,0},{3,1},{4,6},{5,7},{6,4},{7,5},{8,10},{9,11},{10,... | collective-permute-start | bytes 1769480 | tf_op jit(solution)/shard_map/ppermute | solution.py:713
  126.6 50.8 %collective-permute-start.8 = (f32[256,896]{1,0:T(8,128)S(1)}, f32[256,896]{1,0:T(8,128)S(1)}, u32[]{:S(2)}, u32[]{:S(2)}) collective-permute-start(f32[256,896]{1,0:T(8,128)S(1)} %get-tuple-element.96), channel_id=1, source_target_pairs={{0,16},{1,17},{2,18},{3,19},{4,20},{5,21},{6,22},{7,23},{8,24},{9,... | collective-permute-start | bytes 2752520 | tf_op jit(solution)/shard_map/ppermute | solution.py:713
  130.6 15.4 %collective-permute-start.9 = (bf16[64,768]{1,0:T(8,128)(2,1)S(1)}, bf16[64,768]{1,0:T(8,128)(2,1)S(1)}, u32[]{:S(2)}, u32[]{:S(2)}) collective-permute-start(bf16[64,768]{1,0:T(8,128)(2,1)S(1)} %get-tuple-element.98), channel_id=1, source_target_pairs={{0,4},{1,5},{2,6},{3,7},{4,0},{5,1},{6,2},{7,3},{8,12},{9,13},{10,... | collective-permute-start | bytes 294920 | tf_op jit(solution)/shard_map/ppermute | solution.py:713
  142.8 10.0 %collective-permute-start.10 = (bf16[64,768]{1,0:T(8,128)(2,1)S(1)}, bf16[64,768]{1,0:T(8,128)(2,1)S(1)}, u32[]{:S(2)}, u32[]{:S(2)}) collective-permute-start(bf16[64,768]{1,0:T(8,128)(2,1)S(1)} %get-tuple-element.99), channel_id=1, source_target_pairs={{0,8},{1,9},{2,10},{3,11},{4,12},{5,13},{6,14},{7,15},{8,0},{9,1},... | collective-permute-start | bytes 294920 | tf_op jit(solution)/shard_map/ppermute | solution.py:713
  142.9 10.0 %collective-permute-start.11 = (bf16[64,768]{1,0:T(8,128)(2,1)S(1)}, bf16[64,768]{1,0:T(8,128)(2,1)S(1)}, u32[]{:S(2)}, u32[]{:S(2)}) collective-permute-start(bf16[64,768]{1,0:T(8,128)(2,1)S(1)} %get-tuple-element.100), channel_id=1, source_target_pairs={{0,12},{1,13},{2,14},{3,15},{4,8},{5,9},{6,10},{7,11},{8,4},{9,5},... | collective-permute-start | bytes 294920 | tf_op jit(solution)/shard_map/ppermute | solution.py:713
  145.3 8.1 %collective-permute-start.12 = (bf16[64,768]{1,0:T(8,128)(2,1)S(1)}, bf16[64,768]{1,0:T(8,128)(2,1)S(1)}, u32[]{:S(2)}, u32[]{:S(2)}) collective-permute-start(bf16[64,768]{1,0:T(8,128)(2,1)S(1)} %get-tuple-element.97.refs_0_), channel_id=1, source_target_pairs={{0,1},{1,0},{2,3},{3,2},{4,5},{5,4},{6,7},{7,6},{8,9},{9,8},{10,11... | collective-permute-start | bytes 294920 | tf_op jit(solution)/shard_map/ppermute | solution.py:713
  189.4 7.6 %collective-permute-start.28 = (bf16[64,768]{1,0:T(8,128)(2,1)S(1)}, bf16[64,768]{1,0:T(8,128)(2,1)S(1)}, u32[]{:S(2)}, u32[]{:S(2)}) collective-permute-start(bf16[64,768]{1,0:T(8,128)(2,1)S(1)} %get-tuple-element.109), channel_id=1, source_target_pairs={{0,4},{1,5},{2,6},{3,7},{4,0},{5,1},{6,2},{7,3},{8,12},{9,13},{10,... | collective-permute-start | bytes 294920 | tf_op jit(solution)/shard_map/ppermute | solution.py:713
  193.5 10.9 %collective-permute-start.29 = (bf16[64,768]{1,0:T(8,128)(2,1)S(1)}, bf16[64,768]{1,0:T(8,128)(2,1)S(1)}, u32[]{:S(2)}, u32[]{:S(2)}) collective-permute-start(bf16[64,768]{1,0:T(8,128)(2,1)S(1)} %get-tuple-element.110), channel_id=1, source_target_pairs={{0,8},{1,9},{2,10},{3,11},{4,12},{5,13},{6,14},{7,15},{8,0},{9,1},... | collective-permute-start | bytes 294920 | tf_op jit(solution)/shard_map/ppermute | solution.py:713
  194.0 12.4 %collective-permute-start.30 = (bf16[64,768]{1,0:T(8,128)(2,1)S(1)}, bf16[64,768]{1,0:T(8,128)(2,1)S(1)}, u32[]{:S(2)}, u32[]{:S(2)}) collective-permute-start(bf16[64,768]{1,0:T(8,128)(2,1)S(1)} %get-tuple-element.111), channel_id=1, source_target_pairs={{0,12},{1,13},{2,14},{3,15},{4,8},{5,9},{6,10},{7,11},{8,4},{9,5},... | collective-permute-start | bytes 294920 | tf_op jit(solution)/shard_map/ppermute | solution.py:713
  195.8 10.6 %collective-permute-start.31 = (bf16[64,768]{1,0:T(8,128)(2,1)S(1)}, bf16[64,768]{1,0:T(8,128)(2,1)S(1)}, u32[]{:S(2)}, u32[]{:S(2)}) collective-permute-start(bf16[64,768]{1,0:T(8,128)(2,1)S(1)} %get-tuple-element.108.refs_0_), channel_id=1, source_target_pairs={{0,1},{1,0},{2,3},{3,2},{4,5},{5,4},{6,7},{7,6},{8,9},{9,8},{10,11... | collective-permute-start | bytes 294920 | tf_op jit(solution)/shard_map/ppermute | solution.py:713
  195.8 11.1 %collective-permute-start.40 = (bf16[64,768]{1,0:T(8,128)(2,1)S(1)}, bf16[64,768]{1,0:T(8,128)(2,1)S(1)}, u32[]{:S(2)}, u32[]{:S(2)}) collective-permute-start(bf16[64,768]{1,0:T(8,128)(2,1)S(1)} %get-tuple-element.122), channel_id=1, source_target_pairs={{0,4},{1,5},{2,6},{3,7},{4,0},{5,1},{6,2},{7,3},{8,12},{9,13},{10,... | collective-permute-start | bytes 294920 | tf_op jit(solution)/shard_map/ppermute | solution.py:713
  197.0 14.9 %collective-permute-start.41 = (bf16[64,768]{1,0:T(8,128)(2,1)S(1)}, bf16[64,768]{1,0:T(8,128)(2,1)S(1)}, u32[]{:S(2)}, u32[]{:S(2)}) collective-permute-start(bf16[64,768]{1,0:T(8,128)(2,1)S(1)} %get-tuple-element.123), channel_id=1, source_target_pairs={{0,8},{1,9},{2,10},{3,11},{4,12},{5,13},{6,14},{7,15},{8,0},{9,1},... | collective-permute-start | bytes 294920 | tf_op jit(solution)/shard_map/ppermute | solution.py:713
  211.9 10.6 %collective-permute-start.43 = (bf16[64,768]{1,0:T(8,128)(2,1)S(1)}, bf16[64,768]{1,0:T(8,128)(2,1)S(1)}, u32[]{:S(2)}, u32[]{:S(2)}) collective-permute-start(bf16[64,768]{1,0:T(8,128)(2,1)S(1)} %get-tuple-element.121.refs_0_), channel_id=1, source_target_pairs={{0,1},{1,0},{2,3},{3,2},{4,5},{5,4},{6,7},{7,6},{8,9},{9,8},{10,11... | collective-permute-start | bytes 294920 | tf_op jit(solution)/shard_map/ppermute | solution.py:713
  211.9 10.6 %collective-permute-start.44 = (bf16[64,768]{1,0:T(8,128)(2,1)S(1)}, bf16[64,768]{1,0:T(8,128)(2,1)S(1)}, u32[]{:S(2)}, u32[]{:S(2)}) collective-permute-start(bf16[64,768]{1,0:T(8,128)(2,1)S(1)} %collective-permute-done.40.refs_1_), channel_id=1, source_target_pairs={{0,1},{1,0},{2,3},{3,2},{4,5},{5,4},{6,7},{7,6},{8,9},{9,8},{10,11... | collective-permute-start | bytes 294920 | tf_op jit(solution)/shard_map/ppermute | solution.py:713
  212.4 10.1 %collective-permute-start.45 = (bf16[64,768]{1,0:T(8,128)(2,1)S(1)}, bf16[64,768]{1,0:T(8,128)(2,1)S(1)}, u32[]{:S(2)}, u32[]{:S(2)}) collective-permute-start(bf16[64,768]{1,0:T(8,128)(2,1)S(1)} %collective-permute-done.41.refs_2_), channel_id=1, source_target_pairs={{0,1},{1,0},{2,3},{3,2},{4,5},{5,4},{6,7},{7,6},{8,9},{9,8},{10,11... | collective-permute-start | bytes 294920 | tf_op jit(solution)/shard_map/ppermute | solution.py:713
  212.5 10.0 %collective-permute-start.46 = (bf16[64,768]{1,0:T(8,128)(2,1)S(1)}, bf16[64,768]{1,0:T(8,128)(2,1)S(1)}, u32[]{:S(2)}, u32[]{:S(2)}) collective-permute-start(bf16[64,768]{1,0:T(8,128)(2,1)S(1)} %collective-permute-done.42.refs_3_), channel_id=1, source_target_pairs={{0,1},{1,0},{2,3},{3,2},{4,5},{5,4},{6,7},{7,6},{8,9},{9,8},{10,11... | collective-permute-start | bytes 294920 | tf_op jit(solution)/shard_map/ppermute | solution.py:713
  222.3 11.2 %collective-permute-start.35 = (bf16[256,768]{1,0:T(8,128)(2,1)S(1)}, bf16[256,768]{1,0:T(8,128)(2,1)S(1)}, u32[]{:S(2)}, u32[]{:S(2)}) collective-permute-start(bf16[256,768]{1,0:T(8,128)(2,1)S(1)} %get-tuple-element.113), channel_id=1, source_target_pairs={{0,1},{1,0},{2,3},{3,2},{4,5},{5,4},{6,7},{7,6},{8,9},{9,8},{10,11... | collective-permute-start | bytes 1179656 | tf_op jit(solution)/shard_map/ppermute | solution.py:713
  234.2 7.6 %collective-permute-start.36 = (bf16[64,768]{1,0:T(8,128)(2,1)S(1)}, bf16[64,768]{1,0:T(8,128)(2,1)S(1)}, u32[]{:S(2)}, u32[]{:S(2)}) collective-permute-start(bf16[64,768]{1,0:T(8,128)(2,1)S(1)} %get-tuple-element.115), channel_id=1, source_target_pairs={{0,4},{1,5},{2,6},{3,7},{4,0},{5,1},{6,2},{7,3},{8,12},{9,13},{10,... | collective-permute-start | bytes 294920 | tf_op jit(solution)/shard_map/ppermute | solution.py:713
  235.5 11.0 %collective-permute-start.37 = (bf16[64,768]{1,0:T(8,128)(2,1)}, bf16[64,768]{1,0:T(8,128)(2,1)S(1)}, u32[]{:S(2)}, u32[]{:S(2)}) collective-permute-start(bf16[64,768]{1,0:T(8,128)(2,1)} %get-tuple-element.116), channel_id=1, source_target_pairs={{0,8},{1,9},{2,10},{3,11},{4,12},{5,13},{6,14},{7,15},{8,0},{9,1},... | collective-permute-start | bytes 294920 | tf_op jit(solution)/shard_map/ppermute | solution.py:713
  236.7 9.9 %collective-permute-start.38 = (bf16[64,768]{1,0:T(8,128)(2,1)}, bf16[64,768]{1,0:T(8,128)(2,1)S(1)}, u32[]{:S(2)}, u32[]{:S(2)}) collective-permute-start(bf16[64,768]{1,0:T(8,128)(2,1)} %get-tuple-element.117), channel_id=1, source_target_pairs={{0,12},{1,13},{2,14},{3,15},{4,8},{5,9},{6,10},{7,11},{8,4},{9,5},... | collective-permute-start | bytes 294920 | tf_op jit(solution)/shard_map/ppermute | solution.py:713
  239.7 15.2 %collective-permute-start.49 = (bf16[64,768]{1,0:T(8,128)(2,1)}, bf16[64,768]{1,0:T(8,128)(2,1)S(1)}, u32[]{:S(2)}, u32[]{:S(2)}) collective-permute-start(bf16[64,768]{1,0:T(8,128)(2,1)} %get-tuple-element.130), channel_id=1, source_target_pairs={{0,8},{1,9},{2,10},{3,11},{4,12},{5,13},{6,14},{7,15},{8,0},{9,1},... | collective-permute-start | bytes 294920 | tf_op jit(solution)/shard_map/ppermute | solution.py:713
  241.8 13.1 %collective-permute-start.50 = (bf16[64,768]{1,0:T(8,128)(2,1)}, bf16[64,768]{1,0:T(8,128)(2,1)S(1)}, u32[]{:S(2)}, u32[]{:S(2)}) collective-permute-start(bf16[64,768]{1,0:T(8,128)(2,1)} %get-tuple-element.131), channel_id=1, source_target_pairs={{0,12},{1,13},{2,14},{3,15},{4,8},{5,9},{6,10},{7,11},{8,4},{9,5},... | collective-permute-start | bytes 294920 | tf_op jit(solution)/shard_map/ppermute | solution.py:713
  270.7 9.4 %collective-permute-start.53 = (bf16[64,768]{1,0:T(8,128)(2,1)S(1)}, bf16[64,768]{1,0:T(8,128)(2,1)S(1)}, u32[]{:S(2)}, u32[]{:S(2)}) collective-permute-start(bf16[64,768]{1,0:T(8,128)(2,1)S(1)} %get-tuple-element.138), channel_id=1, source_target_pairs={{16,4},{17,5},{18,6},{19,7},{20,0},{21,1},{22,2},{23,3},{24,12},{2... | collective-permute-start | bytes 294920 | tf_op jit(solution)/shard_map/ppermute | solution.py:713
  272.0 13.5 %collective-permute-start.54 = (bf16[64,768]{1,0:T(8,128)(2,1)S(1)}, bf16[64,768]{1,0:T(8,128)(2,1)S(1)}, u32[]{:S(2)}, u32[]{:S(2)}) collective-permute-start(bf16[64,768]{1,0:T(8,128)(2,1)S(1)} %get-tuple-element.139), channel_id=1, source_target_pairs={{16,8},{17,9},{18,10},{19,11},{20,12},{21,13},{22,14},{23,15},{24,... | collective-permute-start | bytes 294920 | tf_op jit(solution)/shard_map/ppermute | solution.py:713
  273.3 12.3 %collective-permute-start.55 = (bf16[64,768]{1,0:T(8,128)(2,1)S(1)}, bf16[64,768]{1,0:T(8,128)(2,1)S(1)}, u32[]{:S(2)}, u32[]{:S(2)}) collective-permute-start(bf16[64,768]{1,0:T(8,128)(2,1)S(1)} %get-tuple-element.140), channel_id=1, source_target_pairs={{16,12},{17,13},{18,14},{19,15},{20,8},{21,9},{22,10},{23,11},{24,... | collective-permute-start | bytes 294920 | tf_op jit(solution)/shard_map/ppermute | solution.py:713
  276.3 10.0 %collective-permute-start.56 = (bf16[64,768]{1,0:T(8,128)(2,1)S(1)}, bf16[64,768]{1,0:T(8,128)(2,1)S(1)}, u32[]{:S(2)}, u32[]{:S(2)}) collective-permute-start(bf16[64,768]{1,0:T(8,128)(2,1)S(1)} %broadcast_select_fusion.4.refs_0_.refs_8_), channel_id=1, source_target_pairs={{0,1},{1,0},{2,3},{3,2},{4,5},{5,4},{6,7},{7,6},{8,9},{9,8},{10,11... | collective-permute-start | bytes 294920 | tf_op jit(solution)/shard_map/ppermute | solution.py:713
  298.0 13.0 %collective-permute-start.51 = (bf16[256,768]{1,0:T(8,128)(2,1)S(1)}, bf16[256,768]{1,0:T(8,128)(2,1)S(1)}, u32[]{:S(2)}, u32[]{:S(2)}) collective-permute-start(bf16[256,768]{1,0:T(8,128)(2,1)S(1)} %get-tuple-element.136), channel_id=1, source_target_pairs={{16,0},{17,1},{18,2},{19,3},{20,4},{21,5},{22,6},{23,7},{24,8},{25... | collective-permute-start | bytes 1179656 | tf_op jit(solution)/shard_map/ppermute | solution.py:713
  300.7 10.3 %collective-permute-start.61 = (bf16[64,768]{1,0:T(8,128)(2,1)S(1)}, bf16[64,768]{1,0:T(8,128)(2,1)S(1)}, u32[]{:S(2)}, u32[]{:S(2)}) collective-permute-start(bf16[64,768]{1,0:T(8,128)(2,1)S(1)} %get-tuple-element.144), channel_id=1, source_target_pairs={{0,4},{1,5},{2,6},{3,7},{4,0},{5,1},{6,2},{7,3},{8,12},{9,13},{10,... | collective-permute-start | bytes 294920 | tf_op jit(solution)/shard_map/ppermute | solution.py:713
  302.0 10.8 %collective-permute-start.62 = (bf16[64,768]{1,0:T(8,128)(2,1)S(1)}, bf16[64,768]{1,0:T(8,128)(2,1)S(1)}, u32[]{:S(2)}, u32[]{:S(2)}) collective-permute-start(bf16[64,768]{1,0:T(8,128)(2,1)S(1)} %get-tuple-element.145), channel_id=1, source_target_pairs={{0,8},{1,9},{2,10},{3,11},{4,12},{5,13},{6,14},{7,15},{8,0},{9,1},... | collective-permute-start | bytes 294920 | tf_op jit(solution)/shard_map/ppermute | solution.py:713
  303.4 9.4 %collective-permute-start.63 = (bf16[64,768]{1,0:T(8,128)(2,1)S(1)}, bf16[64,768]{1,0:T(8,128)(2,1)S(1)}, u32[]{:S(2)}, u32[]{:S(2)}) collective-permute-start(bf16[64,768]{1,0:T(8,128)(2,1)S(1)} %get-tuple-element.146), channel_id=1, source_target_pairs={{0,12},{1,13},{2,14},{3,15},{4,8},{5,9},{6,10},{7,11},{8,4},{9,5},... | collective-permute-start | bytes 294920 | tf_op jit(solution)/shard_map/ppermute | solution.py:713
  332.8 57.8 %collective-permute-start.65 = (bf16[3072,384]{1,0:T(8,128)(2,1)}, bf16[3072,384]{1,0:T(8,128)(2,1)}, u32[]{:S(2)}, u32[]{:S(2)}) collective-permute-start(bf16[3072,384]{1,0:T(8,128)(2,1)} %get-tuple-element.155), channel_id=1, source_target_pairs={{0,1},{1,0},{2,3},{3,2},{4,5},{5,4},{6,7},{7,6},{8,9},{9,8},{10,11... | collective-permute-start | bytes 7077896 | tf_op jit(solution)/shard_map/ppermute | solution.py:713
  341.6 47.7 %collective-permute-start.74 = (bf16[384,768]{1,0:T(8,128)(2,1)}, bf16[384,768]{1,0:T(8,128)(2,1)S(1)}, u32[]{:S(2)}, u32[]{:S(2)}) collective-permute-start(bf16[384,768]{1,0:T(8,128)(2,1)} %get-tuple-element.169), channel_id=1, source_target_pairs={{0,2},{1,3},{2,0},{3,1},{4,6},{5,7},{6,4},{7,5},{8,10},{9,11},{10,... | collective-permute-start | bytes 1769480 | tf_op jit(solution)/shard_map/ppermute | solution.py:713
  343.4 8.0 %collective-permute-start.39 = (bf16[256,768]{1,0:T(8,128)(2,1)S(1)}, bf16[256,768]{1,0:T(8,128)(2,1)S(1)}, u32[]{:S(2)}, u32[]{:S(2)}) collective-permute-start(bf16[256,768]{1,0:T(8,128)(2,1)S(1)} %get-tuple-element.120), channel_id=1, source_target_pairs={{0,1},{1,0},{2,3},{3,2},{4,5},{5,4},{6,7},{7,6},{8,9},{9,8},{10,11... | collective-permute-start | bytes 1179656 | tf_op jit(solution)/shard_map/ppermute | solution.py:713
  343.7 51.6 %collective-permute-start.76 = (bf16[384,768]{1,0:T(8,128)(2,1)}, bf16[384,768]{1,0:T(8,128)(2,1)}, u32[]{:S(2)}, u32[]{:S(2)}) collective-permute-start(bf16[384,768]{1,0:T(8,128)(2,1)} %get-tuple-element.171), channel_id=1, source_target_pairs={{0,2},{1,3},{2,0},{3,1},{4,6},{5,7},{6,4},{7,5},{8,10},{9,11},{10,... | collective-permute-start | bytes 1769480 | tf_op jit(solution)/shard_map/ppermute | solution.py:713
  345.1 53.8 %collective-permute-start.78 = (bf16[384,768]{1,0:T(8,128)(2,1)}, bf16[384,768]{1,0:T(8,128)(2,1)}, u32[]{:S(2)}, u32[]{:S(2)}) collective-permute-start(bf16[384,768]{1,0:T(8,128)(2,1)} %get-tuple-element.173), channel_id=1, source_target_pairs={{0,2},{1,3},{2,0},{3,1},{4,6},{5,7},{6,4},{7,5},{8,10},{9,11},{10,... | collective-permute-start | bytes 1769480 | tf_op jit(solution)/shard_map/ppermute | solution.py:713
  346.8 36.8 %all-to-all-start.3 = ((f32[16,3,128]{2,1,0:T(4,128)}), f32[16,3,128]{2,1,0:T(4,128)S(1)}, u32[]{:S(2)}, u32[]{:S(2)}) async-start(f32[16,3,128]{2,1,0:T(4,128)} %reshape.109), calls=%async_computation.3 | async-start | bytes 65536 | tf_op jit(solution)/shard_map/all_to_all | solution.py:1004
  351.5 72.5 %collective-permute-start.73 = (bf16[384,768]{1,0:T(8,128)(2,1)}, bf16[384,768]{1,0:T(8,128)(2,1)}, u32[]{:S(2)}, u32[]{:S(2)}) collective-permute-start(bf16[384,768]{1,0:T(8,128)(2,1)} %get-tuple-element.167), channel_id=1, source_target_pairs={{0,2},{1,3},{2,0},{3,1},{4,6},{5,7},{6,4},{7,5},{8,10},{9,11},{10,... | collective-permute-start | bytes 1769480 | tf_op jit(solution)/shard_map/ppermute | solution.py:713
  383.6 31.5 %all-to-all-start.1 = ((bf16[16,16,768]{2,1,0:T(8,128)(2,1)}), bf16[16,16,768]{2,1,0:T(8,128)(2,1)}, u32[]{:S(2)}, u32[]{:S(2)}) async-start(bf16[16,16,768]{2,1,0:T(8,128)(2,1)} %bitcast.22), calls=%async_computation.1 | async-start | bytes 786432 | tf_op jit(solution)/shard_map/all_to_all | solution.py:1012
  389.3 12.1 %collective-permute-start.64 = (bf16[256,768]{1,0:T(8,128)(2,1)S(1)}, bf16[256,768]{1,0:T(8,128)(2,1)S(1)}, u32[]{:S(2)}, u32[]{:S(2)}) collective-permute-start(bf16[256,768]{1,0:T(8,128)(2,1)S(1)} %get-tuple-element.149), channel_id=1, source_target_pairs={{0,1},{1,0},{2,3},{3,2},{4,5},{5,4},{6,7},{7,6},{8,9},{9,8},{10,11... | collective-permute-start | bytes 1179656 | tf_op jit(solution)/shard_map/ppermute | solution.py:713
  390.6 36.8 %collective-permute-start.75 = (bf16[384,768]{1,0:T(8,128)(2,1)}, bf16[384,768]{1,0:T(8,128)(2,1)S(1)}, u32[]{:S(2)}, u32[]{:S(2)}) collective-permute-start(bf16[384,768]{1,0:T(8,128)(2,1)} %add_convert_fusion.2), channel_id=1, source_target_pairs={{0,4},{1,5},{2,6},{3,7},{4,0},{5,1},{6,2},{7,3},{8,12},{9,13},{10,... | collective-permute-start | bytes 1769480 | tf_op jit(solution)/shard_map/ppermute | solution.py:713
  395.3 11.4 %collective-permute-start.71 = (bf16[384,384]{1,0:T(8,128)(2,1)S(1)}, bf16[384,384]{1,0:T(8,128)(2,1)S(1)}, u32[]{:S(2)}, u32[]{:S(2)}) collective-permute-start(bf16[384,384]{1,0:T(8,128)(2,1)S(1)} %get-tuple-element.163), channel_id=1, source_target_pairs={{0,2},{1,3},{2,0},{3,1},{4,6},{5,7},{6,4},{7,5},{8,10},{9,11},{10,... | collective-permute-start | bytes 884744 | tf_op jit(solution)/shard_map/ppermute | solution.py:713
  398.9 14.3 %collective-permute-start.69 = (bf16[384,384]{1,0:T(8,128)(2,1)S(1)}, bf16[384,384]{1,0:T(8,128)(2,1)}, u32[]{:S(2)}, u32[]{:S(2)}) collective-permute-start(bf16[384,384]{1,0:T(8,128)(2,1)S(1)} %get-tuple-element.161), channel_id=1, source_target_pairs={{0,2},{1,3},{2,0},{3,1},{4,6},{5,7},{6,4},{7,5},{8,10},{9,11},{10,... | collective-permute-start | bytes 884744 | tf_op jit(solution)/shard_map/ppermute | solution.py:713
  401.5 59.5 %collective-permute-start.77 = (bf16[384,768]{1,0:T(8,128)(2,1)}, bf16[384,768]{1,0:T(8,128)(2,1)S(1)}, u32[]{:S(2)}, u32[]{:S(2)}) collective-permute-start(bf16[384,768]{1,0:T(8,128)(2,1)} %add_convert_fusion.1), channel_id=1, source_target_pairs={{0,8},{1,9},{2,10},{3,11},{4,12},{5,13},{6,14},{7,15},{8,0},{9,1},... | collective-permute-start | bytes 1769480 | tf_op jit(solution)/shard_map/ppermute | solution.py:713
  406.7 14.4 %collective-permute-start.67 = (bf16[384,384]{1,0:T(8,128)(2,1)S(1)}, bf16[384,384]{1,0:T(8,128)(2,1)}, u32[]{:S(2)}, u32[]{:S(2)}) collective-permute-start(bf16[384,384]{1,0:T(8,128)(2,1)S(1)} %get-tuple-element.159), channel_id=1, source_target_pairs={{0,2},{1,3},{2,0},{3,1},{4,6},{5,7},{6,4},{7,5},{8,10},{9,11},{10,... | collective-permute-start | bytes 884744 | tf_op jit(solution)/shard_map/ppermute | solution.py:713
  413.2 51.1 %collective-permute-start.79 = (bf16[384,768]{1,0:T(8,128)(2,1)}, bf16[384,768]{1,0:T(8,128)(2,1)S(1)}, u32[]{:S(2)}, u32[]{:S(2)}) collective-permute-start(bf16[384,768]{1,0:T(8,128)(2,1)} %add_convert_fusion), channel_id=1, source_target_pairs={{0,12},{1,13},{2,14},{3,15},{4,8},{5,9},{6,10},{7,11},{8,4},{9,5},... | collective-permute-start | bytes 1769480 | tf_op jit(solution)/shard_map/ppermute | solution.py:713
  415.1 60.1 %all-to-all-start.2 = ((bf16[16,16,768]{2,1,0:T(8,128)(2,1)}), bf16[16,16,768]{2,1,0:T(8,128)(2,1)}, u32[]{:S(2)}, u32[]{:S(2)}) async-start(bf16[16,16,768]{2,1,0:T(8,128)(2,1)} %bitcast.67), calls=%async_computation.2 | async-start | bytes 786432 | tf_op jit(solution)/shard_map/all_to_all | solution.py:1012
  421.1 56.1 %collective-permute-start.66 = (bf16[384,384]{1,0:T(8,128)(2,1)S(1)}, bf16[384,384]{1,0:T(8,128)(2,1)S(1)}, u32[]{:S(2)}, u32[]{:S(2)}) collective-permute-start(bf16[384,384]{1,0:T(8,128)(2,1)S(1)} %get-tuple-element.157), channel_id=1, source_target_pairs={{0,2},{1,3},{2,0},{3,1},{4,6},{5,7},{6,4},{7,5},{8,10},{9,11},{10,... | collective-permute-start | bytes 884744 | tf_op jit(solution)/shard_map/ppermute | solution.py:713
  423.9 53.3 %collective-permute-start.72 = (bf16[384,384]{1,0:T(8,128)(2,1)S(1)}, bf16[384,384]{1,0:T(8,128)(2,1)S(1)}, u32[]{:S(2)}, u32[]{:S(2)}) collective-permute-start(bf16[384,384]{1,0:T(8,128)(2,1)S(1)} %add_convert_fusion.4), channel_id=1, source_target_pairs={{0,12},{1,13},{2,14},{3,15},{4,8},{5,9},{6,10},{7,11},{8,4},{9,5},... | collective-permute-start | bytes 884744 | tf_op jit(solution)/shard_map/ppermute | solution.py:713
  427.4 61.7 %collective-permute-start.70 = (bf16[384,384]{1,0:T(8,128)(2,1)}, bf16[384,384]{1,0:T(8,128)(2,1)}, u32[]{:S(2)}, u32[]{:S(2)}) collective-permute-start(bf16[384,384]{1,0:T(8,128)(2,1)} %add_convert_fusion.5), channel_id=1, source_target_pairs={{0,8},{1,9},{2,10},{3,11},{4,12},{5,13},{6,14},{7,15},{8,0},{9,1},... | collective-permute-start | bytes 884744 | tf_op jit(solution)/shard_map/ppermute | solution.py:713
  461.0 28.1 %collective-permute-start.68 = (bf16[384,384]{1,0:T(8,128)(2,1)S(1)}, bf16[384,384]{1,0:T(8,128)(2,1)}, u32[]{:S(2)}, u32[]{:S(2)}) collective-permute-start(bf16[384,384]{1,0:T(8,128)(2,1)S(1)} %add_convert_fusion.6), channel_id=1, source_target_pairs={{0,4},{1,5},{2,6},{3,7},{4,0},{5,1},{6,2},{7,3},{8,12},{9,13},{10,... | collective-permute-start | bytes 884744 | tf_op jit(solution)/shard_map/ppermute | solution.py:713
  (73 other events, 626.7 us)

commit v3 on v2

v3 whole, which is shorter than its diff:
```python
import functools

import jax
import jax.numpy as jnp
from jax import lax
from jax.experimental import pallas as pl
from jax.experimental.pallas import tpu as pltpu
from jax.sharding import PartitionSpec as P

HEAD_DIM = 64
EPSILON = 1e-06
NEGATIVE = -1e30
EXACT = lax.Precision.HIGHEST
EXTRA = 128
BF = jnp.bfloat16
F32 = jnp.float32
VM = pl.BlockSpec(memory_space=pltpu.VMEM)
SM = pl.BlockSpec(memory_space=pltpu.SMEM)
HB = pl.BlockSpec(memory_space=pltpu.HBM)
AFTER = pl.BlockSpec(memory_space=pl.ANY)
VH = pl.BlockSpec(memory_space=pltpu.VMEM)
FAR = True
PIPE, MINE, REP, CORE, SPLIT = range(5)


def dot32(a, b):
    return jnp.dot(a, b, preferred_element_type=F32)


def dot_nt(a, b):
    return lax.dot_general(a, b, (((1,), (1,)), ((), ())), preferred_element_type=F32)


def dot_tn(a, b):
    return lax.dot_general(a, b, (((0,), (0,)), ((), ())), preferred_element_type=F32)


def norm_scale(x):
    return lax.rsqrt(jnp.mean(x * x, axis=-1, keepdims=True) + EPSILON)


def norm_back(x, scale, gain, grad):
    weighted = grad * gain
    grad_x = scale * weighted - x * (scale * scale * scale) * jnp.mean(
        x * weighted, axis=-1, keepdims=True
    )
    return grad_x, jnp.sum(grad * (x * scale), axis=0, keepdims=True)


def pinned(value):
    return pltpu.with_memory_space_constraint(value, pltpu.HBM)


def kernel_call(body, name, outs, ins, specs, scratch=(), cost=1, room=24, hbm_outs=False):
    ins = [
        pinned(each) if spec is HB or spec is VH else each
        for each, spec in zip(ins, specs, strict=True)
    ]
    far = [hbm_outs or len(each) > 2 for each in outs]
    return pl.pallas_call(
        body,
        name=name,
        out_shape=[
            (pltpu.HBM if away else jax.ShapeDtypeStruct)(each[0], each[1])
            for each, away in zip(outs, far, strict=True)
        ],
        in_specs=specs,
        out_specs=[VM] * len(outs),
        scratch_shapes=list(scratch),
        compiler_params=pltpu.CompilerParams(vmem_limit_bytes=room << 20),
        cost_estimate=pl.CostEstimate(
            flops=int(cost * 1.1e9), bytes_accessed=0, transcendentals=0
        ),
    )(*ins)


def eye(count):
    rows = lax.broadcasted_iota(jnp.int32, (count, count), 0)
    return (rows == lax.broadcasted_iota(jnp.int32, (count, count), 1)).astype(F32).astype(BF)


def send_kernel(per, facts, inputs, cotangent, dealing, routes, order, router, gains, out, hot_out):
    rows, width = inputs.shape
    place = dealing[...]
    target = place >> 8
    numbers = [place & 255, routes[...], order[...] >> 8, order[...] & 255, target]
    numbers = [each.astype(F32) for each in numbers]
    numbers = jnp.concatenate(numbers + [jnp.zeros((EXTRA - 5, rows), F32)], axis=0)
    columns = dot_nt(eye(rows), numbers.astype(BF))
    targets = target.astype(F32)
    before = lax.broadcasted_iota(jnp.int32, (rows, rows), 0)
    after = lax.broadcasted_iota(jnp.int32, (rows, rows), 1)
    ahead = (columns[:, 4:5] == targets) & (before < after)
    slot = targets * per + jnp.sum(ahead.astype(F32), axis=0, keepdims=True)
    hot = (before.astype(F32) == slot).astype(F32).astype(BF)
    hot_out[...] = hot
    chosen = jnp.where(facts[PIPE] == 0, inputs[...], cotangent[...])
    out[:, :width] = dot32(hot, chosen).astype(BF)
    lane = lax.broadcasted_iota(jnp.int32, (rows, EXTRA), 1)
    tail = dot32(hot, jnp.where(lane < 4, columns, 0.0).astype(BF))
    parts = []
    for values in (router[...], gains[...]):
        high = values.astype(BF).astype(F32)
        mid = (values - high).astype(BF).astype(F32)
        parts += [high, mid, values - high - mid]
    count = gains.shape[1]
    blank = jnp.zeros((4, count), F32)
    block = jnp.concatenate([blank] + parts + [jnp.zeros((10, count), F32)], axis=0)
    block = dot_nt(eye(count), block.astype(BF))
    groups = [block[at * per : (at + 1) * per, :] for at in range(3)]
    block = jnp.concatenate(groups + [jnp.zeros((per, 32), F32)], axis=1)
    block = jnp.concatenate([block] * (rows // per), axis=0)
    out[:, width:] = (tail + block).astype(BF)


def deal_kernel(facts, both, own_rows, slots, onehot, place):
    width = own_rows.shape[1]
    pack = own_rows.shape[0]
    total = both.shape[0]
    half = pack // 2
    core = facts[CORE].astype(F32)
    numbers = both[:, width:]
    spot = numbers[:, 0:1].astype(F32)
    source = (lax.broadcasted_iota(jnp.int32, (total, 1), 0) >= pack).astype(F32)
    upper = (spot >= half).astype(F32)
    where = jnp.where(upper == core, source * half + spot - upper * half, -1.0)
    spots = lax.broadcasted_iota(jnp.int32, (total, pack), 1).astype(F32)
    hot = (spots == where).astype(F32).astype(BF)
    place[...] = hot
    own_rows[...] = dot_tn(hot, both[:, :width]).astype(BF)
    mine = dot_tn(hot, numbers)
    across = dot_nt(eye(EXTRA), mine.astype(BF))
    expert_col, expert_row = mine[:, 1:2], across[1:2, :]
    order_col = mine[:, 2:3] * 256.0 + mine[:, 3:4]
    order_row = across[2:3, :] * 256.0 + across[3:4, :]
    ahead = (expert_col == expert_row) & (order_col < order_row)
    rank = jnp.sum(ahead.astype(F32), axis=0, keepdims=True).astype(jnp.int32)
    experts = 4
    cap = pack // experts
    block = jnp.bitwise_xor(expert_row.astype(jnp.int32), facts[MINE])
    slot = jnp.where(rank < cap, block * cap + rank, -1)
    slots[...] = (lax.broadcasted_iota(jnp.int32, (pack, pack), 0) == slot).astype(F32).astype(BF)
    onehot[...] = (
        lax.broadcasted_iota(jnp.int32, (pack, EXTRA), 1) == expert_col.astype(jnp.int32)
    ).astype(F32)


def mask_of(facts, pack):
    query = lax.broadcasted_iota(jnp.int32, (pack, pack), 0)
    key = lax.broadcasted_iota(jnp.int32, (pack, pack), 1)
    split = facts[SPLIT]
    return ((query < split) == (key < split)) & (key <= query)


def stacked(refs):
    return jnp.concatenate([ref[...] for ref in refs], axis=0)


def flipped(params):
    flat = dot_nt(eye(EXTRA), params[...])
    router = flat[4:8] + flat[8:12] + flat[12:16]
    return router, flat[16:18] + flat[18:20] + flat[20:22]


def weight_copies(sources, scratch, sems, width, cols):
    copies = []
    for at in range(2):
        each = []
        for start, rows in (*((part * width, width) for part in range(3)), (3 * width, 2 * cols)):
            spot = pl.ds(start, rows)
            each.append(
                pltpu.make_async_copy(
                    sources[at].at[spot], scratch.at[at, spot], sems.at[4 * at + len(each)]
                )
            )
        copies.append(each)
    return copies


def attn_kernel(second, dropped, facts, *refs):
    refs = list(refs)
    weights, sems = refs[-2:] if second else refs[-4:-2]
    refs = refs[:-2] if second else refs[:-4] + refs[-2:]
    own_rows = refs.pop(0)
    if second:
        up = refs.pop(0)
        slots_in = [refs.pop(0) for _ in range(4)]
    attn_own, attn_other, params, slots, onehot = (refs.pop(0) for _ in range(5))
    refs = refs[dropped:]
    if second:
        mid, attn_in, proj, mixed, mlp_in, probs = (refs.pop(0) for _ in range(6))
    else:
        mid = refs.pop(0)
        proj, mixed = refs[4:]
    blocks = [refs.pop(0) for _ in range(4)]
    pack, width = own_rows.shape
    cols = attn_own.shape[1]
    cap = pack // 4
    copies = weight_copies((attn_own, attn_other), weights, sems, width, cols)
    for each in copies:
        for copy in each:
            copy.start()
    _, gains = flipped(params)
    hot = slots[...]
    if second:
        stream = refs.pop(0)
        grads = [refs.pop(0) for _ in range(4)]
        came = up[:, :width] + up[:, width : width + 1] * dot_tn(hot, stacked(slots_in))
        rows = jnp.where(facts[PIPE] == 0, own_rows[...], came.astype(BF))
        stream[...] = rows
    else:
        rows = own_rows[...]
    x = rows.astype(F32)
    normed = (x * norm_scale(x) * gains[0:1, :]).astype(BF)
    if second:
        attn_in[...] = normed
    allowed = mask_of(facts, pack)
    for at in range(2):
        for part in range(3):
            copies[at][part].wait()
            proj[at, part] = dot32(
                normed, weights[at, part * width : (part + 1) * width, :]
            ).astype(BF)
        for head in range(cols // HEAD_DIM):
            lanes = slice(head * HEAD_DIM, (head + 1) * HEAD_DIM)
            scores = dot_nt(proj[at, 0, :, lanes], proj[at, 1, :, lanes]) * HEAD_DIM ** (-0.5)
            scores = jnp.where(allowed, scores, NEGATIVE)
            share = jnp.exp(scores - jnp.max(scores, axis=-1, keepdims=True))
            share = (share * (1.0 / jnp.sum(share, axis=-1, keepdims=True))).astype(BF)
            spot = at * cols + head * HEAD_DIM
            mixed[:, spot : spot + HEAD_DIM] = dot32(share, proj[at, 2, :, lanes]).astype(BF)
    base = 3 * width
    copies[0][3].wait()
    copies[1][3].wait()
    for side in range(2):
        rows_at = slice(base + side * cols, base + (side + 1) * cols)
        lanes = slice(side * cols, (side + 1) * cols)
        mid[:, lanes] = (
            x[:, lanes]
            + dot32(mixed[:, :cols], weights[0, rows_at, :])
            + dot32(mixed[:, cols:], weights[1, rows_at, :])
        )
    m = mid[:, :width]
    low = (m * norm_scale(m) * gains[1:2, :]).astype(BF)
    if second:
        mlp_in[...] = low
    logits = dot32(low, params[...])
    lane = lax.broadcasted_iota(jnp.int32, logits.shape, 1)
    logits = sum(pltpu.roll(logits, EXTRA - 4 * at, 1) for at in (1, 2, 3))
    logits = jnp.where(lane < 4, logits, NEGATIVE)
    rel = jnp.exp(logits - jnp.max(logits, axis=-1, keepdims=True))
    share = rel / jnp.sum(rel, axis=-1, keepdims=True)
    if second:
        probs[...] = share
    gate = jnp.sum(share * onehot[...], axis=-1, keepdims=True)
    mid[:, width:] = jnp.broadcast_to(gate, (pack, EXTRA))
    for step in range(4):
        blocks[step][...] = dot32(hot[step * cap : (step + 1) * cap, :], low).astype(BF)
    if second:
        weighted = (gate * own_rows[...].astype(F32)).astype(BF)
        for step in range(4):
            grads[step][...] = dot32(hot[step * cap : (step + 1) * cap, :], weighted).astype(BF)


def attn_forward(facts, own_rows, weights, plan, came=None, after=()):
    attn_own, attn_other, params = weights
    slots, onehot = plan
    pack, width = own_rows.shape
    cols = attn_own.shape[1]
    cap = pack // 4
    second = came is not None
    ins = [facts, own_rows] + (list(came) if second else [])
    specs = [SM, VH] + ([VH] if second else []) + [VM] * (len(ins) - (3 if second else 2))
    specs += [HB] * 2 + [VH] * 3 + [AFTER] * len(after)
    ins += [attn_own, attn_other, params, slots, onehot, *after]
    if second:
        outs = [
            ((pack, width + EXTRA), F32, FAR),
            ((pack, width), BF, FAR),
            ((2, 3, pack, cols), BF, FAR),
            ((pack, width), BF, FAR),
            ((pack, width), BF, FAR),
            ((pack, EXTRA), F32, FAR),
        ]
    else:
        outs = [((pack, width + EXTRA), F32, FAR)]
    outs += [((cap, width), BF)] * 4
    if second:
        outs += [((pack, width), BF, FAR)] + [((cap, width), BF)] * 4
    return kernel_call(
        functools.partial(attn_kernel, second, len(after)),
        "attn_second" if second else "attn_first",
        outs,
        ins,
        specs,
        [pltpu.VMEM((2, 3 * width + 2 * cols, cols), BF), pltpu.SemaphoreType.DMA((8,))]
        + ([] if second else [pltpu.VMEM((2, 3, pack, cols), BF), pltpu.VMEM((pack, width), BF)]),
        cost=8,
    )


def attn_back_kernel(first, facts, *refs):
    refs = list(refs)
    weights, sems = refs[-2:]
    refs = refs[:-2]
    grad_out = refs.pop(0)
    if first:
        up = refs.pop(0)
    else:
        own_rows = refs.pop(0)
        refs.pop(0)
        refs.pop(0)
    grad_slots = [refs.pop(0) for _ in range(4)]
    stream, mid, proj, mlp_in, probs = (refs.pop(0) for _ in range(5))
    attn_own, attn_other, params, slots, onehot = (refs.pop(0) for _ in range(5))
    grad_stream = refs.pop(0)
    if first:
        blocks = [refs.pop(0) for _ in range(4)]
        grad_proj = refs.pop(0)
    else:
        grad_proj, grad_low, tiny = (refs.pop(0) for _ in range(3))
    pack, width = stream.shape
    cols = attn_own.shape[1]
    cap = pack // 4
    copies = weight_copies((attn_own, attn_other), weights, sems, width, cols)
    for part in (3, 0, 1, 2):
        for each in copies:
            each[part].start()
    router, gains = flipped(params)
    hot = slots[...]
    rows = grad_out[...]
    if not first:
        rows = jnp.where(facts[PIPE] == 0, rows, own_rows[...])
    g = rows.astype(F32)
    slot_rows = stacked(grad_slots)
    at_tokens = dot_tn(hot, slot_rows[:, width:])
    grad_logits = (at_tokens[:, 0:1] + at_tokens[:, 1:2]) * (onehot[...] - probs[...])
    m = mid[:, :width]
    wide = jnp.concatenate([router, jnp.zeros((EXTRA - 4, width), F32)], axis=0)
    grad_mlp = dot_tn(hot, slot_rows[:, :width]) + jnp.dot(
        grad_logits, wide, preferred_element_type=F32, precision=EXACT
    )
    grad_norm, gain_two = norm_back(m, norm_scale(m), gains[1:2, :], grad_mlp)
    grad_mid = g + grad_norm
    low = grad_mid.astype(BF)
    allowed = mask_of(facts, pack)
    grad_in = jnp.zeros((pack, width), F32)
    base = 3 * width
    copies[0][3].wait()
    copies[1][3].wait()
    for at in range(2):
        grad_mixed = (
            dot_nt(low[:, :cols], weights[at, base : base + cols, :])
            + dot_nt(low[:, cols:], weights[at, base + cols : base + 2 * cols, :])
        ).astype(BF)
        for head in range(cols // HEAD_DIM):
            lanes = slice(head * HEAD_DIM, (head + 1) * HEAD_DIM)
            query, key, value = (proj[at, part, :, lanes] for part in range(3))
            grad_head = grad_mixed[:, lanes]
            scores = dot_nt(query, key) * HEAD_DIM ** (-0.5)
            scores = jnp.where(allowed, scores, NEGATIVE)
            share = jnp.exp(scores - jnp.max(scores, axis=-1, keepdims=True))
            share = share * (1.0 / jnp.sum(share, axis=-1, keepdims=True))
            grad_share = dot_nt(grad_head, value)
            pulled = share * grad_share
            inner = jnp.sum(pulled, axis=-1, keepdims=True)
            grad_scores = ((pulled - share * inner) * HEAD_DIM ** (-0.5)).astype(BF)
            grad_proj[at, 0, :, lanes] = dot32(grad_scores, key).astype(BF)
            grad_proj[at, 1, :, lanes] = dot_tn(grad_scores, query).astype(BF)
            grad_proj[at, 2, :, lanes] = dot_tn(share.astype(BF), grad_head).astype(BF)
        for part in range(3):
            copies[at][part].wait()
            grad_in += dot_nt(
                grad_proj[at, part], weights[at, part * width : (part + 1) * width, :]
            )
    x = stream[...].astype(F32)
    grad_norm, gain_one = norm_back(x, norm_scale(x), gains[0:1, :], grad_in)
    result = (grad_mid + grad_norm).astype(BF)
    grad_stream[...] = result
    if first:
        weighted = (up[:, width : width + 1] * result.astype(F32)).astype(BF)
        for step in range(4):
            blocks[step][...] = dot32(hot[step * cap : (step + 1) * cap, :], weighted).astype(BF)
    else:
        grad_low[...] = low
        high = grad_logits.astype(BF)
        rest = (grad_logits - high.astype(F32)).astype(BF)
        lane = lax.broadcasted_iota(jnp.int32, (width, EXTRA), 1)
        both = dot_tn(mlp_in[...], high) + dot_tn(mlp_in[...], rest)
        both = jnp.where(lane < 4, both, 0.0)
        high = both.astype(BF).astype(F32)
        flat = [gain_one.astype(BF).astype(F32), gain_two.astype(BF).astype(F32)]
        flat += [gain_one - flat[0], gain_two - flat[1]]
        flat = jnp.concatenate(flat + [jnp.zeros((12, width), F32)], axis=0).astype(BF)
        spot = lax.broadcasted_iota(jnp.int32, (16, EXTRA), 0) + 8
        spot = spot == lax.broadcasted_iota(jnp.int32, (16, EXTRA), 1)
        turned = dot_tn(flat, spot.astype(F32).astype(BF))
        tiny[...] = (high + pltpu.roll(both - high, 4, 1) + turned).astype(BF)


def attn_backward(facts, grad_out, extra, grad_slots, saved, weights, plan, first):
    attn_own, attn_other, params = weights
    slots, onehot = plan
    stream, mid, proj, mlp_in, probs = saved
    pack, width = stream.shape
    cols = attn_own.shape[1]
    cap = pack // 4
    ins = [facts, grad_out, *extra, *grad_slots, stream, mid, proj, mlp_in, probs]
    specs = [SM, VH if first else VM, VH] + [AFTER] * (len(extra) - 1)
    specs += [VM] * 4 + [VH] * 5 + [HB] * 2 + [VH] * 3
    ins += [attn_own, attn_other, params, slots, onehot]
    outs = [((pack, width), BF)]
    if first:
        outs += [((cap, width), BF)] * 4
    outs += [((2, 3, pack, cols), BF)]
    if not first:
        outs += [((pack, width), BF), ((width, EXTRA), BF)]
    return kernel_call(
        functools.partial(attn_back_kernel, first),
        "attn_back_first" if first else "attn_back_second",
        outs,
        ins,
        specs,
        [pltpu.VMEM((2, 3 * width + 2 * cols, cols), BF), pltpu.SemaphoreType.DMA((8,))],
        cost=13,
    )


def gelu_both(u):
    square = u * u
    t = jnp.tanh(0.7978845608028654 * u * (1.0 + 0.044715 * square))
    half = 0.5 * (1.0 + t)
    inner = 0.7978845608028654 * (1.0 + 3.0 * 0.044715 * square)
    return half + 0.5 * u * (1.0 - t * t) * inner, half * u


def bring(facts, pieces, places, scratch, sems):
    copies = []
    for piece, spots in zip(pieces, places, strict=True):
        for source, target, rows, column, columns in spots(facts):
            copies.append(
                pltpu.make_async_copy(
                    piece.at[pl.ds(source, rows), pl.ds(0, columns)],
                    scratch.at[pl.ds(target, rows), pl.ds(column, columns)],
                    sems.at[len(copies)],
                )
            )
    for copy in copies:
        copy.start()
    return copies


TILE = 256


def expert_kernel(keep, places_in, places_out, facts, *refs):
    refs = list(refs)
    blocks = [refs.pop(0) for _ in range(8)]
    pieces = [refs.pop(0) for _ in range(len(places_in))]
    if keep:
        pre = refs.pop(0)
    if keep:
        act = refs.pop(0)
        rows = refs.pop(0)
        own, other, w_in, w_out, sems_in, sems_out = refs
    else:
        own, other, w_in, w_out, sems_in, sems_out, act, rows = refs
    arriving = bring(facts, pieces, places_in, w_in, sems_in)
    later = bring(facts, pieces, places_out, w_out, sems_out)
    cap = blocks[0].shape[0]
    for at, block in enumerate(blocks):
        rows[at * cap : (at + 1) * cap, :] = block[...]
    for copy in arriving:
        copy.wait()
    ff = w_in.shape[1]
    width = w_in.shape[0]

    @pl.loop(0, ff // TILE)
    def _(tile):
        lanes = pl.ds(pl.multiple_of(tile * TILE, TILE), TILE)
        value = dot32(rows[...], w_in[:, lanes])
        slope, result = gelu_both(value)
        act[:, lanes] = result.astype(BF)
        if keep:
            pre[:, lanes] = slope.astype(BF)

    for copy in later:
        copy.wait()
    count = 4 * cap

    @pl.loop(0, width // TILE)
    def _(tile):
        lanes = pl.ds(pl.multiple_of(tile * TILE, TILE), TILE)
        value = dot32(act[...], w_out[:, lanes])
        own[:, lanes] = value[:count]
        other[:, lanes] = value[count:].astype(BF)


def halves(value, shape):
    high = value.astype(BF).astype(F32)
    lane = lax.broadcasted_iota(jnp.int32, shape, 1)
    return jnp.where(lane == 0, high, jnp.where(lane == 1, value - high, 0.0))


def expert_back_kernel(chosen, places_in, places_out, facts, *refs):
    refs = list(refs)
    blocks = [refs.pop(0) for _ in range(8)]
    if chosen:
        others = refs.pop(0)
        refs.pop(0)
    pre, own_out, other_out = (refs.pop(0) for _ in range(3))
    pieces = [refs.pop(0) for _ in range(len(places_in))]
    grad_pre, own, other, rows = (refs.pop(0) for _ in range(4))
    w_in, w_out, sems_in, sems_out = refs
    arriving = bring(facts, pieces, places_out, w_out, sems_out)
    later = bring(facts, pieces, places_in, w_in, sems_in)
    cap = blocks[0].shape[0]
    for at, block in enumerate(blocks):
        value = block[...]
        if chosen:
            value = jnp.where(facts[PIPE] == 0, value, others[at * cap : (at + 1) * cap, :])
        rows[at * cap : (at + 1) * cap, :] = value
    for copy in arriving:
        copy.wait()
    ff = w_in.shape[1]
    width = w_in.shape[0]
    count = 4 * cap

    @pl.loop(0, ff // TILE)
    def _(tile):
        lanes = pl.ds(pl.multiple_of(tile * TILE, TILE), TILE)
        value = dot_nt(rows[...], w_out[lanes, :])
        grad_pre[:, lanes] = (value * pre[:, lanes].astype(F32)).astype(BF)

    for copy in later:
        copy.wait()

    @pl.loop(0, width // TILE)
    def _(tile):
        lanes = pl.ds(pl.multiple_of(tile * TILE, TILE), TILE)
        value = dot_nt(grad_pre[...], w_in[lanes, :])
        own[:, lanes] = value[:count]
        other[:, lanes] = value[count:].astype(BF)

    pull = jnp.sum(rows[:count, :].astype(F32) * own_out[...], axis=-1, keepdims=True)
    own[:, width:] = halves(pull, (count, EXTRA))
    pull = jnp.sum(
        rows[count:, :].astype(F32) * other_out[...].astype(F32), axis=-1, keepdims=True
    )
    other[:, width:] = halves(pull, (count, EXTRA)).astype(BF)


def expert_scratch(width, ff, places):
    numbers = jnp.zeros((8,), jnp.int32)
    sizes = [sum(len(spots(numbers)) for spots in each) for each in places]
    return (
        [pltpu.VMEM((width, ff), BF), pltpu.VMEM((ff, width), BF)],
        [pltpu.SemaphoreType.DMA((size,)) for size in sizes],
    )


def expert_call(name, keep, facts, blocks, pieces, places, width, ff):
    count = 4 * blocks[0].shape[0]
    ins = [facts, *blocks, *pieces]
    kept = [((2 * count, ff), BF, FAR)] * 2 + [((2 * count, width), BF, FAR)] if keep else []
    buffers, sems = expert_scratch(width, ff, places)
    scratch = [*buffers, *sems]
    if not keep:
        scratch += [pltpu.VMEM((2 * count, ff), BF), pltpu.VMEM((2 * count, width), BF)]
    return kernel_call(
        functools.partial(expert_kernel, keep, *places),
        name,
        kept + [((count, width), F32), ((count, width), BF)],
        ins,
        [SM] + [VM] * 8 + [HB] * len(pieces),
        scratch,
        cost=7,
    )


def expert_back_call(name, facts, blocks, others, after, saved, pieces, places, width, ff):
    count = 4 * blocks[0].shape[0]
    wide = width + EXTRA
    ins = [facts, *blocks, *others, *after, *saved, *pieces]
    buffers, sems = expert_scratch(width, ff, places)
    return kernel_call(
        functools.partial(expert_back_kernel, len(after) > 0, *places),
        name,
        [
            ((2 * count, ff), BF),
            ((count, wide), F32),
            ((count, wide), BF),
            ((2 * count, width), BF, FAR),
        ],
        ins,
        [SM]
        + [VM] * 8
        + [VH] * len(others)
        + [AFTER] * len(after)
        + [VH, VM, VM]
        + [HB] * len(pieces),
        [*buffers, *sems],
        cost=7,
    )


def fold_kernel(own, other, *blocks):
    cap = blocks[0].shape[0]
    width = own.shape[1] // TILE * TILE
    for step, block in enumerate(blocks):
        rows = slice(step * cap, (step + 1) * cap)
        block[:, :width] = (own[rows, :width] + other[rows, :width].astype(F32)).astype(BF)
        if own.shape[1] > width:
            both = own[rows, width:] + other[rows, width:].astype(F32)
            block[:, width:] = halves(both[:, 0:1] + both[:, 1:2], (cap, EXTRA)).astype(BF)


def fold(own, other, name):
    count, width = own.shape
    cap = count // 4
    return kernel_call(
        fold_kernel, name, [((cap, width), BF)] * 4, [own, other], [VM, VM], cost=1
    )


def return_kernel(merge, *refs):
    refs = list(refs)
    rows = refs.pop(0)
    if merge:
        hot = refs.pop(0)
        slots_in = [refs.pop(0) for _ in range(4)]
        width = slots_in[0].shape[1]
        values = rows[:, :width] + rows[:, width : width + 1] * dot_tn(hot[...], stacked(slots_in))
        values = values.astype(BF)
    else:
        values = rows[...]
    place, own, other, facts = refs[0], refs[2], refs[3], refs[1]
    pack = own.shape[0]
    core = facts[CORE]
    own[...] = dot32(place[pl.ds(pl.multiple_of(core * pack, pack), pack), :], values).astype(BF)
    other[...] = dot32(
        place[pl.ds(pl.multiple_of((1 - core) * pack, pack), pack), :], values
    ).astype(BF)


def sent_rows(facts, merge, rows, extra, place, width):
    pack = place.shape[1]
    ins = [rows, *extra, place, facts]
    outs = [((pack, width), BF)] * 2
    return kernel_call(
        functools.partial(return_kernel, merge),
        "return_merged" if merge else "return_rows",
        outs,
        ins,
        ([VH, VH] + [VM] * 4 if merge else [VM]) + [VH, SM],
        cost=1,
    )


def run_copies(moves, sems):
    copies = [
        pltpu.make_async_copy(source, target, sems.at[at])
        for at, (source, target) in enumerate(moves)
    ]
    for copy in copies:
        copy.start()
    for copy in copies:
        copy.wait()


def stack_kernel(count, facts, *refs):
    pieces, out, sems = refs[:count], refs[-2], refs[-1]
    run_copies(
        [
            (piece, out.at[jnp.bitwise_xor(facts[MINE], step)])
            for step, piece in enumerate(pieces)
        ],
        sems,
    )


def stack_pieces(facts, pieces, after):
    count = len(pieces)
    return kernel_call(
        functools.partial(stack_kernel, count),
        "stack_pieces",
        [((count, *pieces[0].shape), BF)],
        [facts, *pieces, *after],
        [SM] + [HB] * count + [AFTER] * len(after),
        [pltpu.SemaphoreType.DMA((count,))],
        room=12,
        hbm_outs=True,
    )[0]


def gather_kernel(facts, near, far, *refs):
    out, sems = refs[-2:]
    groups = near.shape[0]
    moves = []
    for rep, source in ((facts[REP], near), (1 - facts[REP], far)):
        for part in range(3):
            moves.append(
                (
                    source.at[:, pl.ds(2 * part, 2)],
                    out.at[pl.ds(part * groups, groups), pl.ds(2 * rep, 2)],
                )
            )
        for side in range(2):
            for group in range(groups):
                moves.append(
                    (
                        source.at[group, 6 + side],
                        out.at[3 * groups + 2 * side + group // 2, group % 2 * 2 + rep],
                    )
                )
    run_copies(moves, sems)


def pack_attn_kernel(attn, attn_out, bundle, sems):
    parts, shard, cols = attn.shape
    rows = attn_out.shape[0]
    moves = [(attn.at[part], bundle.at[pl.ds(part * shard, shard)]) for part in range(parts)]
    for side in range(2):
        moves.append(
            (
                attn_out.at[:, pl.ds(side * cols, cols)],
                bundle.at[pl.ds(parts * shard + side * rows, rows)],
            )
        )
    run_copies(moves, sems)


def pack_attn(attn, attn_out):
    parts, shard, cols = attn.shape
    rows = attn_out.shape[0]
    return kernel_call(
        pack_attn_kernel,
        "pack_attn",
        [((parts * shard + 2 * rows, cols), BF)],
        [attn, attn_out],
        [HB] * 2,
        [pltpu.SemaphoreType.DMA((parts + 2,))],
        room=12,
        hbm_outs=True,
    )[0]


def pack_expert_kernel(steps, facts, w_in, w_out, *refs):
    blocks, sems = refs[-1 - len(steps) : -1], refs[-1]
    in_rows, out_rows, width = w_in.shape[1], w_out.shape[1], w_out.shape[2]
    moves = []
    for step, block in zip(steps, blocks, strict=True):
        at = jnp.bitwise_xor(facts[MINE], step)
        for side in range(2):
            moves.append(
                (
                    w_in.at[at, :, pl.ds(side * width, width)],
                    block.at[pl.ds(side * in_rows, in_rows)],
                )
            )
        moves.append((w_out.at[at], block.at[pl.ds(2 * in_rows, out_rows)]))
    run_copies(moves, sems)


def pack_expert(facts, w_in, w_out, steps, after=()):
    block = (2 * w_in.shape[1] + w_out.shape[1], w_out.shape[2])
    return kernel_call(
        functools.partial(pack_expert_kernel, steps),
        "pack_expert",
        [(block, BF)] * len(steps),
        [facts, w_in, w_out, *after],
        [SM, HB, HB] + [AFTER] * len(after),
        [pltpu.SemaphoreType.DMA((3 * len(steps),))],
        room=12,
        hbm_outs=True,
    )


def expert_grad_kernel(split, facts, *refs):
    refs = list(refs)
    rows, grad_rows, act, grad_pre = (refs.pop(0) for _ in range(4))
    if split:
        sends = [refs.pop(0) for _ in range(4)]
        keeps = [refs.pop(0) for _ in range(4)]
        grad_in, grad_out = refs
    else:
        grad_in, grad_out = refs
    ff = act.shape[1]
    width = rows.shape[1]

    @pl.loop(0, ff // TILE)
    def _(tile):
        lanes = pl.ds(pl.multiple_of(tile * TILE, TILE), TILE)
        grad_in[:, lanes] = dot_tn(rows[...], grad_pre[:, lanes])
        grad_out[lanes, :] = dot_tn(act[:, lanes], grad_rows[...])

    if split:
        shard, out_shard = width // 8, ff // 8
        for step in range(4):
            owner = jnp.bitwise_xor(facts[MINE], step) * 2
            for rep, target in ((1 - facts[REP], sends[step]), (facts[REP], keeps[step])):
                spot = pl.ds(pl.multiple_of((owner + rep) * shard, shard), shard)
                target[0:shard, :] = grad_in[spot, :width].astype(BF)
                target[shard : 2 * shard, :] = grad_in[spot, width:].astype(BF)
                spot = pl.ds(pl.multiple_of((owner + rep) * out_shard, out_shard), out_shard)
                target[2 * shard :, :] = grad_out[spot, :].astype(BF)


def expert_grads(facts, rows, grad_rows, act, grad_pre, split):
    width = rows.shape[1]
    ff = act.shape[1]
    full = [((width, ff), F32), ((ff, width), F32)]
    if split:
        outs = [((width // 2, width), BF, FAR)] * 8
        scratch = [pltpu.VMEM(*each) for each in full]
    else:
        outs, scratch = full, []
    return kernel_call(
        functools.partial(expert_grad_kernel, split),
        "expert_grads",
        outs,
        [facts, rows, grad_rows, act, grad_pre],
        [SM, VH, VH, VH, VM],
        scratch,
        cost=6,
        room=32,
    )


def owner_kernel(facts, *refs):
    pieces, grad_in, grad_out = refs[:-2], refs[-2], refs[-1]
    shard = grad_in.shape[1]
    width = grad_out.shape[2]
    for step, piece in enumerate(pieces):
        at = jnp.bitwise_xor(facts[MINE], step)
        grad_in[at, :, :width] = piece[:shard, :].astype(F32)
        grad_in[at, :, width:] = piece[shard : 2 * shard, :].astype(F32)
        grad_out[at] = piece[2 * shard :, :].astype(F32)


def owner_grads(facts, pieces, in_shape, out_shape):
    return kernel_call(
        owner_kernel,
        "owner_grads",
        [(in_shape, F32), (out_shape, F32)],
        [facts, *pieces],
        [SM] + [VM] * len(pieces),
        cost=3,
    )


def attn_grad_kernel(attn_in, grad_proj, mixed, low, *refs):
    own, other = refs[-2:]
    width = attn_in.shape[1]
    cols = own.shape[1]
    for at, target in ((0, own), (1, other)):
        for part in range(3):
            target[part * width : (part + 1) * width, :] = dot_tn(
                attn_in[...], grad_proj[at, part]
            ).astype(BF)
        for side in range(2):
            spot = 3 * width + side * cols
            target[spot : spot + cols, :] = dot_tn(
                mixed[:, at * cols : (at + 1) * cols], low[:, side * cols : (side + 1) * cols]
            ).astype(BF)


def attn_grads(attn_in, grad_proj, mixed, low, after):
    pack, width = attn_in.shape
    cols = grad_proj.shape[3]
    return kernel_call(
        attn_grad_kernel,
        "attn_grads",
        [((3 * width + 2 * cols, cols), BF)] * 2,
        [attn_in, grad_proj, mixed, low, *after],
        [VH, VM, VH, VM] + [AFTER] * len(after),
        cost=3,
    )


SPLIT_ORDER = (2, 3, 1, 0)


def attn_split_kernel(facts, own, came, *refs):
    sends, keeps = refs[:2], refs[2:]
    cols = own.shape[1]
    width = 2 * cols
    shard = width // 8
    count = 4 * shard
    for at, step in enumerate(SPLIT_ORDER):
        owner = jnp.bitwise_xor(facts[MINE], step) * 2
        for rep, target, first in (
            (1 - facts[REP], sends[at // 2], at % 2 * count),
            (facts[REP], keeps[at // 2], at % 2 * count),
        ):
            for source, rows, spot in attn_rows(width, shard):
                where = pl.ds(pl.multiple_of(source + (owner + rep) * rows, rows), rows)
                target[first + spot : first + spot + rows, :] = (
                    own[where, :].astype(F32) + came[where, :].astype(F32)
                ).astype(BF)


def sum_kernel(steps, keep, came, *outs):
    count = outs[0].shape[0]
    for at, (step, out) in enumerate(zip(steps, outs, strict=True)):
        rows = slice(at * count, (at + 1) * count)
        both = keep[rows, :].astype(F32) + came[rows, :].astype(F32)
        out[...] = both.astype(out.dtype)


def sum_pieces(steps, keep, came):
    count = keep.shape[0] // len(steps)
    kinds = [F32 if step == 0 else BF for step in steps]
    return kernel_call(
        functools.partial(sum_kernel, steps),
        "sum_pieces",
        [((count, keep.shape[1]), kind) for kind in kinds],
        [keep, came],
        [VH] * 2,
    )


def attn_rows(width, shard):
    out = shard // 2
    return (
        (0, shard, 0),
        (width, shard, shard),
        (2 * width, shard, 2 * shard),
        (3 * width, out, 3 * shard),
        (3 * width + width // 2, out, 3 * shard + out),
    )


def attn_split(facts, own, came):
    rows, cols = own.shape
    return kernel_call(
        attn_split_kernel,
        "attn_split",
        [((rows // 4, cols), BF, FAR)] * 4,
        [facts, own, came],
        [SM, VM, VM],
        cost=3,
    )


def solution(mesh):
    shape = mesh.shape
    n_pipe, n_dp, n_t = shape["pipe"], shape["dp"], shape["tensor"]
    axes = ("pipe", "dp", "tensor")
    plane = ("dp", "tensor")
    n_dev = n_dp * n_t

    def local(
        inputs,
        cotangent,
        dealing,
        routes,
        slot_order,
        doc_lengths,
        attn_weight,
        attn_out_weight,
        expert_in_weight,
        expert_out_weight,
        norm_gains,
        router_weight,
    ):
        dev_rows, width = inputs.shape
        experts = expert_in_weight.shape[1]
        reps = n_dp // experts
        paired = reps == 2
        pack = dev_rows
        cap = pack // experts
        per = dev_rows // n_dev
        shard, cols = attn_weight.shape[1], attn_weight.shape[3]
        ff = expert_in_weight.shape[3]
        in_rows, out_rows = expert_in_weight.shape[2], expert_out_weight.shape[2]
        pipe = lax.axis_index("pipe")
        dp = lax.axis_index("dp")
        core = lax.axis_index("tensor")
        mine = dp // reps
        rep = dp % reps
        lengths = lax.dynamic_index_in_dim(doc_lengths, core, 0, keepdims=False)
        zero = jnp.int32(0)
        facts = jnp.stack([pipe, mine, rep, core, lengths[0], zero, zero, zero]).astype(jnp.int32)

        def moved(value, rule):
            pairs = []
            for a in range(n_pipe):
                for b in range(experts):
                    for c in range(reps):
                        for d in range(n_t):
                            to = rule(a, b, c, d)
                            if to is not None:
                                flat = [
                                    ((w * experts + x) * reps + y) * n_t + z
                                    for w, x, y, z in ((a, b, c, d), to)
                                ]
                                pairs.append(tuple(flat))
            return lax.ppermute(value, axes, pairs)

        def swap_core(value):
            return moved(value, lambda a, b, c, d: (a, b, c, 1 - d))

        def swap_rep(value):
            return moved(value, lambda a, b, c, d: (a, b, 1 - c, d))

        def across(step):
            return lambda a, b, c, d: (a, b ^ step, c, d)

        def up(step):
            return lambda a, b, c, d: (1, b ^ step, c, d) if a == 0 else None

        def down(step):
            return lambda a, b, c, d: (0, b ^ step, c, d) if a == 1 else None

        order = (2, 3, 1)

        def exchange(blocks):
            out = {0: blocks[0]}
            for step in order:
                out[step] = moved(blocks[step], across(step))
            return [out[step] for step in range(experts)]

        def crossed(blocks, way):
            out = {}
            for step in (*order, 0):
                out[step] = moved(blocks[step], way(step))
            return [out[step] for step in range(experts)]

        def with_other(blocks):
            out = {}
            for step in (0, 1, 2, 3):
                out[step] = swap_core(blocks[step])
            return list(blocks) + [out[step] for step in range(experts)]

        def pick(blocks, step):
            return lax.dynamic_index_in_dim(blocks, mine ^ step, 0, keepdims=False)

        rep_groups = [[b * reps + c for c in range(reps)] for b in range(experts)]

        payload, send_hot = kernel_call(
            functools.partial(send_kernel, per),
            "send",
            [((dev_rows, width + EXTRA), BF), ((dev_rows, dev_rows), BF)],
            [
                facts,
                inputs,
                cotangent,
                dealing.reshape(1, dev_rows),
                routes.reshape(1, dev_rows),
                slot_order.reshape(1, dev_rows),
                router_weight[0].T,
                norm_gains[0],
            ],
            [SM] + [VM] * 7,
            cost=2,
        )
        dealt = lax.all_to_all(payload, plane, split_axis=0, concat_axis=0, tiled=True)
        params = dealt[:, width:].reshape(n_dev, per, 4, 32)[:, :, :3]
        params = jnp.swapaxes(params, 1, 2).reshape(width, 32)
        params = jnp.pad(params, ((0, 0), (0, EXTRA - 32)))
        both = lax.all_gather(dealt, "tensor", axis=0, tiled=True)
        own_rows, slots, onehot, place = kernel_call(
            deal_kernel,
            "deal",
            [
                ((pack, width), BF, FAR),
                ((pack, pack), BF, FAR),
                ((pack, EXTRA), F32, FAR),
                ((2 * pack, pack), BF, FAR),
            ],
            [facts, both],
            [SM, VM],
            cost=1.5,
        )
        plan = (slots, onehot)

        out_shard = attn_out_weight[0]
        attn_shape = (4 * width, cols)

        def expert_places(way, step):
            def owner_of(numbers):
                owner = jnp.bitwise_xor(numbers[MINE], step) * 2
                return owner + (numbers[REP] if way == 0 else 1 - numbers[REP])

            def spots_in(numbers):
                at = pl.multiple_of(owner_of(numbers) * in_rows, in_rows)
                return [(0, at, in_rows, 0, width), (in_rows, at, in_rows, width, width)]

            def spots_out(numbers):
                at = pl.multiple_of(owner_of(numbers) * out_rows, out_rows)
                return [(2 * in_rows, at, out_rows, 0, width)]

            return spots_in, spots_out

        if paired:
            w_in_raw, w_out_raw = expert_in_weight[0], expert_out_weight[0]
            attn_bundle = pack_attn(jnp.swapaxes(attn_weight[0], 0, 1), out_shard)
            near, far = {}, {}
            near[0], first, bundle = pack_expert(facts, w_in_raw, w_out_raw, (0, 1, 2))
            near[1] = moved(first, across(1))
            far[0] = swap_rep(near[0])
            attn_near = exchange([attn_bundle] * experts)
            attn_near = stack_pieces(
                facts, [each.reshape(8, shard // 2, cols) for each in attn_near],
                [payload, near[1], far[0]],
            )
            attn_far = swap_rep(attn_near)
            near[2] = moved(bundle, across(2))
            attn_own = kernel_call(
                gather_kernel,
                "gather_attn",
                [((4 * experts, 4, shard // 2, cols), BF)],
                [facts, attn_near, attn_far, near[2], dealt],
                [SM, HB, HB] + [AFTER] * 2,
                [pltpu.SemaphoreType.DMA((22,))],
                room=12,
                hbm_outs=True,
            )[0].reshape(attn_shape)
            (bundle,) = pack_expert(facts, w_in_raw, w_out_raw, (3,), (near[2],))
            near[3] = moved(bundle, across(3))
            for step in (1, 2, 3):
                far[step] = swap_rep(near[step])
            pieces = [each[step] for each in (near, far) for step in range(experts)]
            ready = (far[2],)
            both_places = [
                expert_places(way, step) for way in range(2) for step in range(experts)
            ]
            places = ([each[0] for each in both_places], [each[1] for each in both_places])
        else:
            attn_bundle = jnp.concatenate(
                [attn_weight[0, :, part] for part in range(3)]
                + [out_shard[:, :cols], out_shard[:, cols:]],
                axis=0,
            )
            every = lax.all_gather(attn_bundle, "dp", axis=0)
            attn_own = jnp.concatenate(
                [
                    every[:, spot : spot + rows].reshape(-1, cols)
                    for _, rows, spot in attn_rows(width, shard)
                ],
                axis=0,
            )

            def assembled(blocks):
                got = exchange([pick(blocks, step) for step in range(experts)])
                got = jnp.stack(got)
                got = jnp.stack([pick(got, owner) for owner in range(experts)])
                got = lax.all_gather(got, "dp", axis_index_groups=rep_groups)
                return jnp.swapaxes(got, 0, 1)

            ready = ()
            pieces = [
                assembled(expert_in_weight[0]).reshape(width, ff),
                assembled(expert_out_weight[0]).reshape(ff, width),
            ]
            places = (
                [lambda numbers: [(0, 0, width, 0, ff)], lambda numbers: []],
                [lambda numbers: [], lambda numbers: [(0, 0, ff, 0, width)]],
            )
        attn_other = swap_core(attn_own)
        weights = (attn_own, attn_other, params)

        def expert_forward(blocks, name, keep):
            *kept, own, other = expert_call(name, keep, facts, blocks, pieces, places, width, ff)
            folded = fold(own, swap_core(other), "fold_" + name)
            return kept, own, other, folded

        def expert_backward(blocks, others, after, saved, name):
            grad_pre, own, other, rows = expert_back_call(
                name, facts, blocks, others, after, saved, pieces, places, width, ff
            )
            return grad_pre, rows, fold(own, swap_core(other), "fold_" + name)

        def sent_back(merge, rows, extra, tail):
            own, other = sent_rows(facts, merge, rows, extra, place, width)
            full = own + swap_core(other)
            if tail is not None:
                full = jnp.concatenate([full, tail], axis=1)
            return own, lax.all_to_all(full, plane, split_axis=0, concat_axis=0, tiled=True)

        def restored(back):
            return dot_tn(send_hot, back[:, :width]).astype(BF)[None]

        out = attn_forward(facts, own_rows, weights, plan, None, ready)
        mid_up = moved(out[0], lambda a, b, c, d: (1, b, c, d) if a == 0 else None)
        blocks = with_other(exchange(out[1:5]))
        _, _, _, expert_slots = expert_forward(blocks, "expert_first", False)
        from_first = crossed(expert_slots, up)

        out = attn_forward(facts, own_rows, weights, plan, (mid_up, *from_first))
        mid, attn_in, proj, mixed, mlp_in, probs = out[:6]
        stream = out[10]
        blocks = with_other(exchange(out[6:10]))
        kept_grads = with_other(exchange(out[11:15]))
        (slope, act, rows), own_out, other_out, expert_slots = expert_forward(blocks, "expert_second", True)
        expert_saved = (slope, own_out, other_out)

        saved = (stream, mid, proj, mlp_in, probs)
        _, kept_rows, grad_slots = expert_backward(kept_grads, [], [], expert_saved, "expert_back_first")
        back = attn_backward(
            facts, own_rows, [mid_up], exchange(grad_slots), saved, weights, plan, True
        )
        grad_down = moved(back[0], lambda a, b, c, d: (0, b, c, d) if a == 1 else None)
        expert_slots = exchange(expert_slots)
        marker, out_back = sent_back(True, mid, (slots, *expert_slots), None)

        grads = with_other(crossed(back[1:5], down))
        grad_pre, grad_rows, grad_slots = expert_backward(
            grads, [kept_rows], [marker], expert_saved, "expert_back_second"
        )
        grads_out = expert_grads(facts, rows, grad_rows, act, grad_pre, paired)
        layer_grad, grad_proj, low, tiny = attn_backward(
            facts,
            grad_down,
            [own_rows, grads_out[0], out_back],
            exchange(grad_slots),
            saved,
            weights,
            plan,
            False,
        )

        if paired:
            sums = {}
            for step in (*order, 0):
                (sums[step],) = sum_pieces(
                    (step,), grads_out[4 + step], swap_rep(grads_out[step])
                )
            marker = [sums[2]]
            for step in order:
                sums[step] = moved(sums[step], across(step))
            grad_expert_in, grad_expert_out = owner_grads(
                facts,
                [sums[step] for step in range(experts)],
                expert_in_weight.shape[1:],
                expert_out_weight.shape[1:],
            )
        else:

            def rep_scatter(each):
                return lax.psum_scatter(
                    each, "dp", axis_index_groups=rep_groups, scatter_dimension=0
                )

            def to_owner(grad, rows_each):
                each = grad.reshape(experts, reps, rows_each, -1).astype(BF)
                summed = rep_scatter(jnp.swapaxes(each, 0, 1))
                got = exchange([pick(summed, step) for step in range(experts)])
                got = jnp.stack(got)
                return jnp.stack([pick(got, owner) for owner in range(experts)]).astype(F32)

            marker = []
            grad_w_in, grad_w_out = grads_out
            grad_expert_in = to_owner(grad_w_in, in_rows)
            grad_expert_out = to_owner(grad_w_out, out_rows)

        grad_own, grad_other = attn_grads(attn_in, grad_proj, mixed, low, marker)
        came = swap_core(grad_other)
        if paired:
            out = attn_split(facts, grad_own, came)
            total = {}
            for at in range(2):
                steps = SPLIT_ORDER[2 * at : 2 * at + 2]
                for step, each in zip(
                    steps, sum_pieces(steps, out[2 + at], swap_rep(out[at])), strict=True
                ):
                    total[step] = moved(each, across(step)).astype(F32) if step else each
            total = total[0] + total[1] + total[2] + total[3]
        else:
            full = grad_own.astype(F32) + came.astype(F32)
            pieces_of = [
                full[source : source + rows * n_dp].reshape(n_dp, rows, cols)
                for source, rows, _ in attn_rows(width, shard)
            ]
            full = jnp.concatenate(pieces_of, axis=1).astype(BF)
            full = full.reshape((experts, reps) + full.shape[1:])
            full = rep_scatter(jnp.swapaxes(full, 0, 1))
            got = exchange([pick(full, step) for step in range(experts)])
            total = sum(each.astype(F32) for each in got)
        grad_attn = total[: 3 * shard].reshape(3, shard, cols)
        grad_attn = jnp.swapaxes(grad_attn, 0, 1)[None]
        rows = shard // 2
        grad_attn_out = jnp.concatenate(
            [total[3 * shard : 3 * shard + rows], total[3 * shard + rows :]], axis=1
        )[None]

        tiny = jnp.swapaxes(tiny[:, :32].reshape(n_dev, 3, per, 32), 1, 2)
        tiny = jnp.pad(tiny.reshape(dev_rows, 96), ((0, 0), (0, EXTRA - 96)))
        _, grad_back = sent_back(False, layer_grad, (), tiny)
        tiny = grad_back[:, width:].reshape(n_dev, per, EXTRA).astype(F32)
        tiny = jnp.sum(tiny, axis=0).reshape(per, 4, 32)[:, :3]
        tiny = jnp.swapaxes(tiny, 0, 1).reshape(3 * per, 32)
        grad_router = (tiny[:, :experts] + tiny[:, experts : 2 * experts])[None]
        grad_gains = (tiny[:, 8:10] + tiny[:, 10:12]).T[None]

        return (
            restored(out_back),
            restored(grad_back),
            grad_attn,
            grad_attn_out,
            grad_expert_in[None],
            grad_expert_out[None],
            grad_gains,
            grad_router,
        )

    in_specs = (
        P(("dp", "tensor"), None),
        P(("dp", "tensor"), None),
        P(("dp", "tensor")),
        P(("dp", "tensor"), None),
        P(("dp", "tensor")),
        P("dp", None),
        P("pipe", "dp", None, "tensor"),
        P("pipe", ("tensor", "dp"), None),
        P("pipe", None, "dp", "tensor"),
        P("pipe", None, ("tensor", "dp"), None),
        P("pipe", None, ("dp", "tensor")),
        P("pipe", ("dp", "tensor"), None),
    )
    out_specs = (
        P("pipe", ("dp", "tensor"), None),
        P("pipe", ("dp", "tensor"), None),
        P("pipe", "dp", None, "tensor"),
        P("pipe", ("tensor", "dp"), None),
        P("pipe", None, "dp", "tensor"),
        P("pipe", None, ("tensor", "dp"), None),
        P("pipe", None, ("dp", "tensor")),
        P("pipe", ("dp", "tensor"), None),
    )
    return jax.shard_map(local, mesh=mesh, in_specs=in_specs, out_specs=out_specs, check_vma=False)
```

time: 501 us -> 487 us (0.972)
  the two profiles are of different devices: /device:TPU:0 before, /device:TPU:21 now
where the time goes in v3:
time: 487 us; the launch traced here: 478 us
  waiting for transfers between devices  206 us (42%)
  Pallas kernels  139 us (29%)
  starting transfers between devices  105 us (22%)
  local copies, waits for them, and re-layouts  15.9 us (3%)
    ppermute x75, waiting for transfers between devices, moved(): return lax.ppermute(value, axes, pairs)  206 us
    pallas_call x31, Pallas kernels, kernel_call(): pl.pallas_call(body, name=name, out_shape=[(pltpu.HBM if away else jax.Sh...  139 us
    ppermute x75, starting transfers between devices, moved(): return lax.ppermute(value, axes, pairs)  78.4 us
    all_to_all x1, starting transfers between devices, local(): lax.all_to_all(payload, plane, split_axis=0, concat_axis=0, tiled=True)  14.4 us
    unnamed x70, local copies, waits for them, and re-layouts  12.5 us
    all_to_all x2, starting transfers between devices, sent_back(): lax.all_to_all(full, plane, split_axis=0, concat_axis=0, tiled=True)  12.1 us
  transfers between devices with their start and end apart: 78, of which 22 were waited for; matrix products, arithmetic and copies ran while one was open for 2% of the time, Pallas kernels for 18%

profile of v3, /device:TPU:21, one launch (start us, length us, event | category | flops | bytes accessed | tf_op | source)
XLA Modules:
  0.0 477.6 jit_solution(696444884417453248)
XLA Ops:
  1.4 3.3 pack_expert.2
  6.4 1.8 pack_attn.1
  8.4 2.5 collective-permute-start.2
  10.9 1.9 send.1
  12.8 18.1 %collective-permute-done = bf16[384,384]{1,0:T(8,128)(2,1)S(1)} collective-permute-done((bf16[384,384]{1,0:T(8,128)(2,1)}, bf16[384,384]{1,0:T(8,128)(2,1)S(1)}, u32[]{:S(2)}, u32[]{:S(2)}) %collective-permute-start) | collective-permute-done | bytes 294944 | tf_op jit(solution)/shard_map/ppermute | solution.py:999
  32.5 2.8 stack_pieces.1.near
  36.6 14.4 %all-to-all-start = ((bf16[16,16,896]{2,1,0:T(8,128)(2,1)}), bf16[16,16,896]{2,1,0:T(8,128)(2,1)S(1)}, u32[]{:S(2)}, u32[]{:S(2)}) async-start(bf16[16,16,896]{2,1,0:T(8,128)(2,1)} %bitcast.11), calls=%async_computation | async-start | bytes 917504 | tf_op jit(solution)/shard_map/all_to_all | solution.py:1058
  51.4 35.0 %collective-permute-done.6.refs_0_.refs_10_.refs_13_.refs_15_ = bf16[384,768]{1,0:T(8,128)(2,1)S(1)} collective-permute-done((bf16[384,768]{1,0:T(8,128)(2,1)S(1)}, bf16[384,768]{1,0:T(8,128)(2,1)S(1)}, u32[]{:S(2)}, u32[]{:S(2)}) %collective-permute-start.6) | collective-permute-done | bytes 589856 | tf_op jit(solution)/shard_map/ppermute | solution.py:999
  87.5 3.7 gather_attn.1
  92.1 2.5 pack_expert.3
  97.4 2.9 all_gather.3.both
  100.3 2.1 deal.1
  102.3 20.2 %collective-permute-done.17.refs_11_.refs_14_.refs_16_ = bf16[384,768]{1,0:T(8,128)(2,1)S(1)} collective-permute-done((bf16[384,768]{1,0:T(8,128)(2,1)}, bf16[384,768]{1,0:T(8,128)(2,1)S(1)}, u32[]{:S(2)}, u32[]{:S(2)}) %collective-permute-start.17) | collective-permute-done | bytes 589856 | tf_op jit(solution)/shard_map/ppermute | solution.py:999
  122.9 10.3 %attn_first.1 = (f32[256,896]{1,0:T(8,128)}, bf16[64,768]{1,0:T(8,128)(2,1)S(1)}, bf16[64,768]{1,0:T(8,128)(2,1)S(1)}, bf16[64,768]{1,0:T(8,128)(2,1)S(1)}, bf16[64,768]{1,0:T(8,128)(2,1)S(1)}) custom-call(s32[8]{0:T(128)S(1)} %stack.19.facts.refs_7_.refs_2_, bf16[256,768]{1,0:T(8,128)(2,1)} %get-tuple-element.102.refs_0_.refs_1_, ...), custom_call_target="tpu_custom_call" | custom-call | flops 8800000000 | tf_op jit(solution)/shard_map/attn_first/pallas_call | solution.py:60
  133.3 1.5 collective-permute-start.11
  135.9 1.8 collective-permute-start.13
  137.8 2.2 collective-permute-start.14
  140.0 3.1 collective-permute-start.15
  143.1 1.7 collective-permute-done.12.refs_3_
  145.9 3.2 collective-permute-start.9
  149.1 7.4 %expert_first.1 = (f32[256,768]{1,0:T(8,128)S(1)}, bf16[256,768]{1,0:T(8,128)(2,1)S(1)}) custom-call(s32[8]{0:T(128)S(1)} %stack.19.facts.refs_7_.refs_2_, bf16[64,768]{1,0:T(8,128)(2,1)S(1)} %get-tuple-element.109.refs_0_, bf16[64,768]{1,0:T(8,128)(2,1)S(1)} %collective-permute-done.10.refs_1_, bf16[64,768]{1,0:T(8,128)(2,1)S(1)} %collective-permute-done.11.refs_2_, ...), custom_call_target="tpu_custom_call" | custom-call | flops 7699999744 | tf_op jit(solution)/shard_map/expert_first/pallas_call | solution.py:60
  162.4 1.5 collective-permute-start.24
  163.9 13.5 %collective-permute-done.21.refs_2_ = bf16[64,768]{1,0:T(8,128)(2,1)S(1)} collective-permute-done((bf16[64,768]{1,0:T(8,128)(2,1)S(1)}, bf16[64,768]{1,0:T(8,128)(2,1)S(1)}, u32[]{:S(2)}, u32[]{:S(2)}) %collective-permute-start.21) | collective-permute-done | bytes 98336 | tf_op jit(solution)/shard_map/ppermute | solution.py:999
  178.4 11.3 %attn_second.1 = (f32[256,896]{1,0:T(8,128)}, bf16[256,768]{1,0:T(8,128)(2,1)}, bf16[2,3,256,384]{3,2,1,0:T(8,128)(2,1)}, bf16[256,768]{1,0:T(8,128)(2,1)}, bf16...) custom-call(s32[8]{0:T(128)S(1)} %stack.19.facts.refs_7_.refs_2_, ...), custom_call_target="tpu_custom_call" | custom-call | flops 8800000000 | tf_op jit(solution)/shard_map/attn_second/pallas_call | solution.py:60
  189.7 1.6 collective-permute-start.26
  192.4 1.6 collective-permute-start.28
  196.7 7.8 %collective-permute-done.27.refs_3_ = bf16[64,768]{1,0:T(8,128)(2,1)S(1)} collective-permute-done((bf16[64,768]{1,0:T(8,128)(2,1)S(1)}, bf16[64,768]{1,0:T(8,128)(2,1)S(1)}, u32[]{:S(2)}, u32[]{:S(2)}) %collective-permute-start.27) | collective-permute-done | bytes 98336 | tf_op jit(solution)/shard_map/ppermute | solution.py:999
  204.5 1.8 collective-permute-start.29
  208.0 1.7 collective-permute-done.39.refs_3_
  211.4 9.7 %expert_second.1 = (bf16[512,1536]{1,0:T(8,128)(2,1)}, bf16[512,1536]{1,0:T(8,128)(2,1)}, bf16[512,768]{1,0:T(8,128)(2,1)}, f32[256,768]{1,0:T(8,128)S(1)}, bf16[256,768]{1,0:T(8,128)(2,1)S(1)}) custom-call(s32[8]{0:T(128)S(1)} %stack.19.facts.refs_7_.refs_2_, bf16[64,768]{1,0:T(8,128)(2,1)S(1)} %get-tuple-element.120.refs_0_, ...), custom_call_target="tpu_custom_call" | custom-call | flops 7699999744 | tf_op jit(solution)/shard_map/expert_second/pallas_call | solution.py:60
  221.1 10.0 %expert_back_first.1 = (bf16[512,1536]{1,0:T(8,128)(2,1)}, f32[256,896]{1,0:T(8,128)S(1)}, bf16[256,896]{1,0:T(8,128)(2,1)S(1)}, bf16[512,768]{1,0:T(8,128)(2,1)}) custom-call(s32[8]{0:T(128)S(1)} %stack.19.facts.refs_7_.refs_2_, bf16[64,768]{1,0:T(8,128)(2,1)S(1)} %get-tuple-element.133.refs_0_, bf16[64,768]{1,0:T(8,128)(2,1)S(1)} %collective-permute-done.37.refs_1_, ...), custom_call_target="tpu_custom_call" | custom-call | flops 7699999744 | tf_op jit(solution)/shard_map/expert_back_first/pallas_call | solution.py:60
  233.4 1.6 collective-permute-start.46
  238.0 2.6 collective-permute-done.46.refs_4_
  240.6 7.7 %collective-permute-done.47.refs_5_ = bf16[64,896]{1,0:T(8,128)(2,1)S(1)} collective-permute-done((bf16[64,896]{1,0:T(8,128)(2,1)S(1)}, bf16[64,896]{1,0:T(8,128)(2,1)S(1)}, u32[]{:S(2)}, u32[]{:S(2)}) %collective-permute-start.47) | collective-permute-done | bytes 114720 | tf_op jit(solution)/shard_map/ppermute | solution.py:999
  248.3 15.3 %attn_back_first.1 = (bf16[256,768]{1,0:T(8,128)(2,1)S(1)}, bf16[64,768]{1,0:T(8,128)(2,1)S(1)}, bf16[64,768]{1,0:T(8,128)(2,1)S(1)}, bf16[64,768]{1,0:T(8,128)(...) custom-call(s32[8]{0:T(128)S(1)} %stack.19.facts.refs_7_.refs_2_, ...), custom_call_target="tpu_custom_call" | custom-call | flops 14300000256 | tf_op jit(solution)/shard_map/attn_back_first/pallas_call | solution.py:60
  269.1 3.8 collective-permute-start.53
  272.9 2.8 collective-permute-start.54
  275.7 2.0 collective-permute-start.55
  277.7 2.8 collective-permute-done.52.refs_3_
  280.5 3.0 collective-permute-start.56
  283.6 1.9 return_merged.1
  285.6 9.4 %expert_back_second.1 = (bf16[512,1536]{1,0:T(8,128)(2,1)S(1)}, f32[256,896]{1,0:T(8,128)S(1)}, bf16[256,896]{1,0:T(8,128)(2,1)S(1)}, bf16[512,768]{1,0:T(8,128)(2,1)}) custom-call(s32[8]{0:T(128)S(1)} %stack.19.facts.refs_7_.refs_2_, bf16[64,768]{1,0:T(8,128)(2,1)S(1)} %collective-permute-done.49.refs_0_, ...), custom_call_target="tpu_custom_call" | custom-call | flops 7699999744 | tf_op jit(solution)/shard_map/expert_back_second/pallas_call | solution.py:60
  297.0 5.2 %all-to-all-start.1 = ((bf16[16,16,768]{2,1,0:T(8,128)(2,1)}), bf16[16,16,768]{2,1,0:T(8,128)(2,1)S(1)}, u32[]{:S(2)}, u32[]{:S(2)}) async-start(bf16[16,16,768]{2,1,0:T(8,128)(2,1)} %bitcast.25), calls=%async_computation.1 | async-start | bytes 786432 | tf_op jit(solution)/shard_map/all_to_all | solution.py:1180
  303.6 8.3 %expert_grads.1 = (bf16[384,768]{1,0:T(8,128)(2,1)}, bf16[384,768]{1,0:T(8,128)(2,1)}, bf16[384,768]{1,0:T(8,128)(2,1)}, bf16[384,768]{1,0:T(8,128)(2,1)}, bf16[...) custom-call(s32[8]{0:T(128)S(1)} %stack.19.facts.refs_7_.refs_2_, ...), custom_call_target="tpu_custom_call" | custom-call | flops 6600000000 | tf_op jit(solution)/shard_map/expert_grads/pallas_call | solution.py:60
  312.9 1.5 collective-permute-start.48
  317.3 9.4 %collective-permute-done.62.came = bf16[384,768]{1,0:T(8,128)(2,1)S(1)} collective-permute-done((bf16[384,768]{1,0:T(8,128)(2,1)}, bf16[384,768]{1,0:T(8,128)(2,1)S(1)}, u32[]{:S(2)}, u32[]{:S(2)}) %collective-permute-start.62) | collective-permute-done | bytes 589856 | tf_op jit(solution)/shard_map/ppermute | solution.py:999
  327.5 2.2 sum_pieces.6.refs_0_
  329.8 14.0 %attn_back_second.1 = (bf16[256,768]{1,0:T(8,128)(2,1)S(1)}, bf16[2,3,256,384]{3,2,1,0:T(8,128)(2,1)S(1)}, bf16[256,768]{1,0:T(8,128)(2,1)S(1)}, bf16[768,128]{1,0:T(8,128)(2,1)S(1)}) custom-call(s32[8]{0:T(128)S(1)} %stack.19.facts.refs_7_.refs_2_, bf16[256,768]{1,0:T(8,128)(2,1)S(1)} %collective-permute-done.48.refs_0_, ...), custom_call_target="tpu_custom_call" | custom-call | flops 14300000256 | tf_op jit(solution)/shard_map/attn_back_second/pallas_call | solution.py:60
  343.8 4.7 attn_grads.1
  352.8 2.1 return_rows.1
  355.7 10.3 %collective-permute-done.73.came = bf16[384,768]{1,0:T(8,128)(2,1)S(1)} collective-permute-done((bf16[384,768]{1,0:T(8,128)(2,1)S(1)}, bf16[384,768]{1,0:T(8,128)(2,1)S(1)}, u32[]{:S(2)}, u32[]{:S(2)}) %collective-permute-start.73) | collective-permute-done | bytes 589856 | tf_op jit(solution)/shard_map/ppermute | solution.py:999
  366.8 2.2 sum_pieces.11
  369.0 9.7 %collective-permute-done.70.came = bf16[384,768]{1,0:T(8,128)(2,1)S(1)} collective-permute-done((bf16[384,768]{1,0:T(8,128)(2,1)S(1)}, bf16[384,768]{1,0:T(8,128)(2,1)S(1)}, u32[]{:S(2)}, u32[]{:S(2)}) %collective-permute-start.70) | collective-permute-done | bytes 589856 | tf_op jit(solution)/shard_map/ppermute | solution.py:999
  384.8 1.7 fusion.3
  386.5 6.9 %all-to-all-start.2 = ((bf16[16,16,896]{2,1,0:T(8,128)(2,1)}), bf16[16,16,896]{2,1,0:T(8,128)(2,1)S(1)}, u32[]{:S(2)}, u32[]{:S(2)}) async-start(bf16[16,16,896]{2,1,0:T(8,128)(2,1)} %bitcast.83), calls=%async_computation.2 | async-start | bytes 917504 | tf_op jit(solution)/shard_map/all_to_all | solution.py:1180
  393.4 1.5 sum_pieces.9.refs_0_
  396.0 2.4 attn_split.1
  398.7 26.6 %collective-permute-done.74.refs_3_ = bf16[384,768]{1,0:T(8,128)(2,1)} collective-permute-done((bf16[384,768]{1,0:T(8,128)(2,1)}, bf16[384,768]{1,0:T(8,128)(2,1)}, u32[]{:S(2)}, u32[]{:S(2)}) %collective-permute-start.74) | collective-permute-done | bytes 589856 | tf_op jit(solution)/shard_map/ppermute | solution.py:999
  425.3 3.9 owner_grads.1
  429.2 2.2 collective-permute-start.66
  434.6 10.1 %collective-permute-done.66.came = bf16[768,384]{1,0:T(8,128)(2,1)S(1)} collective-permute-done((bf16[768,384]{1,0:T(8,128)(2,1)S(1)}, bf16[768,384]{1,0:T(8,128)(2,1)S(1)}, u32[]{:S(2)}, u32[]{:S(2)}) %collective-permute-start.66) | collective-permute-done | bytes 589856 | tf_op jit(solution)/shard_map/ppermute | solution.py:999
  447.0 2.4 collective-permute-start.68
  451.2 14.1 %collective-permute-done.67 = bf16[384,384]{1,0:T(8,128)(2,1)S(1)} collective-permute-done((bf16[384,384]{1,0:T(8,128)(2,1)S(1)}, bf16[384,384]{1,0:T(8,128)(2,1)S(1)}, u32[]{:S(2)}, u32[]{:S(2)}) %collective-permute-start.67) | collective-permute-done | bytes 294944 | tf_op jit(solution)/shard_map/ppermute | solution.py:999
  465.3 10.4 %collective-permute-done.68 = bf16[384,384]{1,0:T(8,128)(2,1)S(1)} collective-permute-done((bf16[384,384]{1,0:T(8,128)(2,1)S(1)}, bf16[384,384]{1,0:T(8,128)(2,1)S(1)}, u32[]{:S(2)}, u32[]{:S(2)}) %collective-permute-start.68) | collective-permute-done | bytes 294944 | tf_op jit(solution)/shard_map/ppermute | solution.py:999
  (219 shorter events, 68.0 us)
Async XLA Ops:
  4.8 26.9 %collective-permute-start.4 = (bf16[384,768]{1,0:T(8,128)(2,1)}, bf16[384,768]{1,0:T(8,128)(2,1)S(1)}, u32[]{:S(2)}, u32[]{:S(2)}) collective-permute-start(bf16[384,768]{1,0:T(8,128)(2,1)} %get-tuple-element.104.refs_8_.refs_11_.refs_13_), channel_id=1, source_target_pairs={{0,2},{1,3},{2,0},{3,1},{4,6},{5,7},{6,4},{7,5},{8,10},{9,11},{10,... | collective-permute-start | bytes 1769480 | tf_op jit(solution)/shard_map/ppermute | solution.py:999
  5.1 26.6 %collective-permute-start.3 = (bf16[384,768]{1,0:T(8,128)(2,1)}, bf16[384,768]{1,0:T(8,128)(2,1)S(1)}, u32[]{:S(2)}, u32[]{:S(2)}) collective-permute-start(bf16[384,768]{1,0:T(8,128)(2,1)} %get-tuple-element.103), channel_id=1, source_target_pairs={{0,4},{1,5},{2,6},{3,7},{4,0},{5,1},{6,2},{7,3},{8,12},{9,13},{10,... | collective-permute-start | bytes 1769480 | tf_op jit(solution)/shard_map/ppermute | solution.py:999
  8.2 22.8 %collective-permute-start = (bf16[384,384]{1,0:T(8,128)(2,1)}, bf16[384,384]{1,0:T(8,128)(2,1)S(1)}, u32[]{:S(2)}, u32[]{:S(2)}) collective-permute-start(bf16[384,384]{1,0:T(8,128)(2,1)} %pack_attn.1), channel_id=1, source_target_pairs={{0,4},{1,5},{2,6},{3,7},{4,0},{5,1},{6,2},{7,3},{8,12},{9,13},{10,... | collective-permute-start | bytes 884744 | tf_op jit(solution)/shard_map/ppermute | solution.py:999
  8.4 23.2 %collective-permute-start.1 = (bf16[384,384]{1,0:T(8,128)(2,1)}, bf16[384,384]{1,0:T(8,128)(2,1)S(1)}, u32[]{:S(2)}, u32[]{:S(2)}) collective-permute-start(bf16[384,384]{1,0:T(8,128)(2,1)} %pack_attn.1), channel_id=1, source_target_pairs={{0,8},{1,9},{2,10},{3,11},{4,12},{5,13},{6,14},{7,15},{8,0},{9,1},... | collective-permute-start | bytes 884744 | tf_op jit(solution)/shard_map/ppermute | solution.py:999
  8.4 23.2 %collective-permute-start.2 = (bf16[384,384]{1,0:T(8,128)(2,1)}, bf16[384,384]{1,0:T(8,128)(2,1)S(1)}, u32[]{:S(2)}, u32[]{:S(2)}) collective-permute-start(bf16[384,384]{1,0:T(8,128)(2,1)} %pack_attn.1), channel_id=1, source_target_pairs={{0,12},{1,13},{2,14},{3,15},{4,8},{5,9},{6,10},{7,11},{8,4},{9,5},... | collective-permute-start | bytes 884744 | tf_op jit(solution)/shard_map/ppermute | solution.py:999
  35.3 51.1 %collective-permute-start.5 = (bf16[4,8,48,384]{3,2,1,0:T(8,128)(2,1)}, bf16[4,8,48,384]{3,2,1,0:T(8,128)(2,1)S(1)}, u32[]{:S(2)}, u32[]{:S(2)}) collective-permute-start(bf16[4,8,48,384]{3,2,1,0:T(8,128)(2,1)} %stack_pieces.1.near), channel_id=1, source_target_pairs={{0,2},{1,3},{2,0},{3,1},{4,6},{5,7},{6,4},{7,5},{8,10},{9,11},{10,... | collective-permute-start | bytes 3538952 | tf_op jit(solution)/shard_map/ppermute | solution.py:999
  36.6 49.8 %all-to-all-start = ((bf16[16,16,896]{2,1,0:T(8,128)(2,1)}), bf16[16,16,896]{2,1,0:T(8,128)(2,1)S(1)}, u32[]{:S(2)}, u32[]{:S(2)}) async-start(bf16[16,16,896]{2,1,0:T(8,128)(2,1)} %bitcast.11), calls=%async_computation | async-start | bytes 917504 | tf_op jit(solution)/shard_map/all_to_all | solution.py:1058
  51.1 35.3 %collective-permute-start.6 = (bf16[384,768]{1,0:T(8,128)(2,1)S(1)}, bf16[384,768]{1,0:T(8,128)(2,1)S(1)}, u32[]{:S(2)}, u32[]{:S(2)}) collective-permute-start(bf16[384,768]{1,0:T(8,128)(2,1)S(1)} %copy-done.25), channel_id=1, source_target_pairs={{0,8},{1,9},{2,10},{3,11},{4,12},{5,13},{6,14},{7,15},{8,0},{9,1},... | collective-permute-start | bytes 1769480 | tf_op jit(solution)/shard_map/ppermute | solution.py:999
  91.2 31.7 %collective-permute-start.7 = (bf16[3072,384]{1,0:T(8,128)(2,1)}, bf16[3072,384]{1,0:T(8,128)(2,1)}, u32[]{:S(2)}, u32[]{:S(2)}) collective-permute-start(bf16[3072,384]{1,0:T(8,128)(2,1)} %bitcast.76), channel_id=1, source_target_pairs={{0,1},{1,0},{2,3},{3,2},{4,5},{5,4},{6,7},{7,6},{8,9},{9,8},{10,11... | collective-permute-start | bytes 7077896 | tf_op jit(solution)/shard_map/ppermute | solution.py:999
  94.6 28.0 %collective-permute-start.17 = (bf16[384,768]{1,0:T(8,128)(2,1)}, bf16[384,768]{1,0:T(8,128)(2,1)S(1)}, u32[]{:S(2)}, u32[]{:S(2)}) collective-permute-start(bf16[384,768]{1,0:T(8,128)(2,1)} %pack_expert.3), channel_id=1, source_target_pairs={{0,12},{1,13},{2,14},{3,15},{4,8},{5,9},{6,10},{7,11},{8,4},{9,5},... | collective-permute-start | bytes 1769480 | tf_op jit(solution)/shard_map/ppermute | solution.py:999
  94.9 27.9 %collective-permute-start.8 = (bf16[384,768]{1,0:T(8,128)(2,1)S(1)}, bf16[384,768]{1,0:T(8,128)(2,1)S(1)}, u32[]{:S(2)}, u32[]{:S(2)}) collective-permute-start(bf16[384,768]{1,0:T(8,128)(2,1)S(1)} %collective-permute-done.6.refs_0_.refs_10_.refs_13_.refs_15_), channel_id=1, source_target_pairs={{0,2},{1,3},{2,0},{3,1},{4,6},{5,7},{6,4},{7,5},{8,10},{9,11},{10,... | collective-permute-start | bytes 1769480 | tf_op jit(solution)/shard_map/ppermute | solution.py:999
  95.3 40.7 %collective-permute-start.18 = (bf16[384,768]{1,0:T(8,128)(2,1)S(1)}, bf16[384,768]{1,0:T(8,128)(2,1)}, u32[]{:S(2)}, u32[]{:S(2)}) collective-permute-start(bf16[384,768]{1,0:T(8,128)(2,1)S(1)} %collective-permute-done.3.refs_5_.refs_9_.refs_12_.refs_14_), channel_id=1, source_target_pairs={{0,2},{1,3},{2,0},{3,1},{4,6},{5,7},{6,4},{7,5},{8,10},{9,11},{10,... | collective-permute-start | bytes 1769480 | tf_op jit(solution)/shard_map/ppermute | solution.py:999
  122.6 23.3 %collective-permute-start.19 = (bf16[384,768]{1,0:T(8,128)(2,1)S(1)}, bf16[384,768]{1,0:T(8,128)(2,1)S(1)}, u32[]{:S(2)}, u32[]{:S(2)}) collective-permute-start(bf16[384,768]{1,0:T(8,128)(2,1)S(1)} %collective-permute-done.17.refs_11_.refs_14_.refs_16_), channel_id=1, source_target_pairs={{0,2},{1,3},{2,0},{3,1},{4,6},{5,7},{6,4},{7,5},{8,10},{9,11},{10,... | collective-permute-start | bytes 1769480 | tf_op jit(solution)/shard_map/ppermute | solution.py:999
  133.3 6.7 %collective-permute-start.11 = (bf16[64,768]{1,0:T(8,128)(2,1)S(1)}, bf16[64,768]{1,0:T(8,128)(2,1)S(1)}, u32[]{:S(2)}, u32[]{:S(2)}) collective-permute-start(bf16[64,768]{1,0:T(8,128)(2,1)S(1)} %get-tuple-element.111), channel_id=1, source_target_pairs={{0,8},{1,9},{2,10},{3,11},{4,12},{5,13},{6,14},{7,15},{8,0},{9,1},... | collective-permute-start | bytes 294920 | tf_op jit(solution)/shard_map/ppermute | solution.py:999
  134.8 10.0 %collective-permute-start.12 = (bf16[64,768]{1,0:T(8,128)(2,1)S(1)}, bf16[64,768]{1,0:T(8,128)(2,1)S(1)}, u32[]{:S(2)}, u32[]{:S(2)}) collective-permute-start(bf16[64,768]{1,0:T(8,128)(2,1)S(1)} %get-tuple-element.112), channel_id=1, source_target_pairs={{0,12},{1,13},{2,14},{3,15},{4,8},{5,9},{6,10},{7,11},{8,4},{9,5},... | collective-permute-start | bytes 294920 | tf_op jit(solution)/shard_map/ppermute | solution.py:999
  135.9 13.1 %collective-permute-start.13 = (bf16[64,768]{1,0:T(8,128)(2,1)S(1)}, bf16[64,768]{1,0:T(8,128)(2,1)S(1)}, u32[]{:S(2)}, u32[]{:S(2)}) collective-permute-start(bf16[64,768]{1,0:T(8,128)(2,1)S(1)} %get-tuple-element.109.refs_0_), channel_id=1, source_target_pairs={{0,1},{1,0},{2,3},{3,2},{4,5},{5,4},{6,7},{7,6},{8,9},{9,8},{10,11... | collective-permute-start | bytes 294920 | tf_op jit(solution)/shard_map/ppermute | solution.py:999
  137.8 11.3 %collective-permute-start.14 = (bf16[64,768]{1,0:T(8,128)(2,1)S(1)}, bf16[64,768]{1,0:T(8,128)(2,1)S(1)}, u32[]{:S(2)}, u32[]{:S(2)}) collective-permute-start(bf16[64,768]{1,0:T(8,128)(2,1)S(1)} %collective-permute-done.10.refs_1_), channel_id=1, source_target_pairs={{0,1},{1,0},{2,3},{3,2},{4,5},{5,4},{6,7},{7,6},{8,9},{9,8},{10,11... | collective-permute-start | bytes 294920 | tf_op jit(solution)/shard_map/ppermute | solution.py:999
  140.0 9.1 %collective-permute-start.15 = (bf16[64,768]{1,0:T(8,128)(2,1)S(1)}, bf16[64,768]{1,0:T(8,128)(2,1)S(1)}, u32[]{:S(2)}, u32[]{:S(2)}) collective-permute-start(bf16[64,768]{1,0:T(8,128)(2,1)S(1)} %collective-permute-done.11.refs_2_), channel_id=1, source_target_pairs={{0,1},{1,0},{2,3},{3,2},{4,5},{5,4},{6,7},{7,6},{8,9},{9,8},{10,11... | collective-permute-start | bytes 294920 | tf_op jit(solution)/shard_map/ppermute | solution.py:999
  145.9 31.5 %collective-permute-start.9 = (f32[256,896]{1,0:T(8,128)}, f32[256,896]{1,0:T(8,128)S(1)}, u32[]{:S(2)}, u32[]{:S(2)}) collective-permute-start(f32[256,896]{1,0:T(8,128)} %get-tuple-element.108), channel_id=1, source_target_pairs={{0,16},{1,17},{2,18},{3,19},{4,20},{5,21},{6,22},{7,23},{8,24},{9,... | collective-permute-start | bytes 2752520 | tf_op jit(solution)/shard_map/ppermute | solution.py:999
  158.4 19.0 %collective-permute-start.21 = (bf16[64,768]{1,0:T(8,128)(2,1)S(1)}, bf16[64,768]{1,0:T(8,128)(2,1)S(1)}, u32[]{:S(2)}, u32[]{:S(2)}) collective-permute-start(bf16[64,768]{1,0:T(8,128)(2,1)S(1)} %get-tuple-element.115), channel_id=1, source_target_pairs={{0,16},{1,17},{2,18},{3,19},{4,20},{5,21},{6,22},{7,23},{8,24},{9,... | collective-permute-start | bytes 294920 | tf_op jit(solution)/shard_map/ppermute | solution.py:999
  159.7 17.7 %collective-permute-start.22 = (bf16[64,768]{1,0:T(8,128)(2,1)S(1)}, bf16[64,768]{1,0:T(8,128)(2,1)S(1)}, u32[]{:S(2)}, u32[]{:S(2)}) collective-permute-start(bf16[64,768]{1,0:T(8,128)(2,1)S(1)} %get-tuple-element.116), channel_id=1, source_target_pairs={{0,20},{1,21},{2,22},{3,23},{4,16},{5,17},{6,18},{7,19},{8,28},{9,... | collective-permute-start | bytes 294920 | tf_op jit(solution)/shard_map/ppermute | solution.py:999
  161.0 16.4 %collective-permute-start.23 = (bf16[64,768]{1,0:T(8,128)(2,1)S(1)}, bf16[64,768]{1,0:T(8,128)(2,1)S(1)}, u32[]{:S(2)}, u32[]{:S(2)}) collective-permute-start(bf16[64,768]{1,0:T(8,128)(2,1)S(1)} %get-tuple-element.117), channel_id=1, source_target_pairs={{0,24},{1,25},{2,26},{3,27},{4,28},{5,29},{6,30},{7,31},{8,16},{9,... | collective-permute-start | bytes 294920 | tf_op jit(solution)/shard_map/ppermute | solution.py:999
  162.4 15.0 %collective-permute-start.24 = (bf16[64,768]{1,0:T(8,128)(2,1)S(1)}, bf16[64,768]{1,0:T(8,128)(2,1)S(1)}, u32[]{:S(2)}, u32[]{:S(2)}) collective-permute-start(bf16[64,768]{1,0:T(8,128)(2,1)S(1)} %get-tuple-element.118), channel_id=1, source_target_pairs={{0,28},{1,29},{2,30},{3,31},{4,24},{5,25},{6,26},{7,27},{8,20},{9,... | collective-permute-start | bytes 294920 | tf_op jit(solution)/shard_map/ppermute | solution.py:999
  191.3 13.2 %collective-permute-start.27 = (bf16[64,768]{1,0:T(8,128)(2,1)S(1)}, bf16[64,768]{1,0:T(8,128)(2,1)S(1)}, u32[]{:S(2)}, u32[]{:S(2)}) collective-permute-start(bf16[64,768]{1,0:T(8,128)(2,1)S(1)} %get-tuple-element.123), channel_id=1, source_target_pairs={{0,12},{1,13},{2,14},{3,15},{4,8},{5,9},{6,10},{7,11},{8,4},{9,5},... | collective-permute-start | bytes 294920 | tf_op jit(solution)/shard_map/ppermute | solution.py:999
  192.4 13.9 %collective-permute-start.28 = (bf16[64,768]{1,0:T(8,128)(2,1)S(1)}, bf16[64,768]{1,0:T(8,128)(2,1)S(1)}, u32[]{:S(2)}, u32[]{:S(2)}) collective-permute-start(bf16[64,768]{1,0:T(8,128)(2,1)S(1)} %get-tuple-element.120.refs_0_), channel_id=1, source_target_pairs={{0,1},{1,0},{2,3},{3,2},{4,5},{5,4},{6,7},{7,6},{8,9},{9,8},{10,11... | collective-permute-start | bytes 294920 | tf_op jit(solution)/shard_map/ppermute | solution.py:999
  194.0 12.3 %collective-permute-start.37 = (bf16[64,768]{1,0:T(8,128)(2,1)S(1)}, bf16[64,768]{1,0:T(8,128)(2,1)S(1)}, u32[]{:S(2)}, u32[]{:S(2)}) collective-permute-start(bf16[64,768]{1,0:T(8,128)(2,1)S(1)} %get-tuple-element.134), channel_id=1, source_target_pairs={{0,4},{1,5},{2,6},{3,7},{4,0},{5,1},{6,2},{7,3},{8,12},{9,13},{10,... | collective-permute-start | bytes 294920 | tf_op jit(solution)/shard_map/ppermute | solution.py:999
  194.8 12.1 %collective-permute-start.38 = (bf16[64,768]{1,0:T(8,128)(2,1)S(1)}, bf16[64,768]{1,0:T(8,128)(2,1)S(1)}, u32[]{:S(2)}, u32[]{:S(2)}) collective-permute-start(bf16[64,768]{1,0:T(8,128)(2,1)S(1)} %get-tuple-element.135), channel_id=1, source_target_pairs={{0,8},{1,9},{2,10},{3,11},{4,12},{5,13},{6,14},{7,15},{8,0},{9,1},... | collective-permute-start | bytes 294920 | tf_op jit(solution)/shard_map/ppermute | solution.py:999
  195.6 14.1 %collective-permute-start.39 = (bf16[64,768]{1,0:T(8,128)(2,1)S(1)}, bf16[64,768]{1,0:T(8,128)(2,1)S(1)}, u32[]{:S(2)}, u32[]{:S(2)}) collective-permute-start(bf16[64,768]{1,0:T(8,128)(2,1)S(1)} %get-tuple-element.136), channel_id=1, source_target_pairs={{0,12},{1,13},{2,14},{3,15},{4,8},{5,9},{6,10},{7,11},{8,4},{9,5},... | collective-permute-start | bytes 294920 | tf_op jit(solution)/shard_map/ppermute | solution.py:999
  206.8 14.3 %collective-permute-start.40 = (bf16[64,768]{1,0:T(8,128)(2,1)S(1)}, bf16[64,768]{1,0:T(8,128)(2,1)S(1)}, u32[]{:S(2)}, u32[]{:S(2)}) collective-permute-start(bf16[64,768]{1,0:T(8,128)(2,1)S(1)} %get-tuple-element.133.refs_0_), channel_id=1, source_target_pairs={{0,1},{1,0},{2,3},{3,2},{4,5},{5,4},{6,7},{7,6},{8,9},{9,8},{10,11... | collective-permute-start | bytes 294920 | tf_op jit(solution)/shard_map/ppermute | solution.py:999
  209.7 11.4 %collective-permute-start.41 = (bf16[64,768]{1,0:T(8,128)(2,1)S(1)}, bf16[64,768]{1,0:T(8,128)(2,1)S(1)}, u32[]{:S(2)}, u32[]{:S(2)}) collective-permute-start(bf16[64,768]{1,0:T(8,128)(2,1)S(1)} %collective-permute-done.37.refs_1_), channel_id=1, source_target_pairs={{0,1},{1,0},{2,3},{3,2},{4,5},{5,4},{6,7},{7,6},{8,9},{9,8},{10,11... | collective-permute-start | bytes 294920 | tf_op jit(solution)/shard_map/ppermute | solution.py:999
  210.9 10.3 %collective-permute-start.42 = (bf16[64,768]{1,0:T(8,128)(2,1)S(1)}, bf16[64,768]{1,0:T(8,128)(2,1)S(1)}, u32[]{:S(2)}, u32[]{:S(2)}) collective-permute-start(bf16[64,768]{1,0:T(8,128)(2,1)S(1)} %collective-permute-done.38.refs_2_), channel_id=1, source_target_pairs={{0,1},{1,0},{2,3},{3,2},{4,5},{5,4},{6,7},{7,6},{8,9},{9,8},{10,11... | collective-permute-start | bytes 294920 | tf_op jit(solution)/shard_map/ppermute | solution.py:999
  210.9 10.3 %collective-permute-start.43 = (bf16[64,768]{1,0:T(8,128)(2,1)S(1)}, bf16[64,768]{1,0:T(8,128)(2,1)S(1)}, u32[]{:S(2)}, u32[]{:S(2)}) collective-permute-start(bf16[64,768]{1,0:T(8,128)(2,1)S(1)} %collective-permute-done.39.refs_3_), channel_id=1, source_target_pairs={{0,1},{1,0},{2,3},{3,2},{4,5},{5,4},{6,7},{7,6},{8,9},{9,8},{10,11... | collective-permute-start | bytes 294920 | tf_op jit(solution)/shard_map/ppermute | solution.py:999
  233.4 7.2 %collective-permute-start.46 = (bf16[64,896]{1,0:T(8,128)(2,1)S(1)}, bf16[64,896]{1,0:T(8,128)(2,1)S(1)}, u32[]{:S(2)}, u32[]{:S(2)}) collective-permute-start(bf16[64,896]{1,0:T(8,128)(2,1)S(1)} %get-tuple-element.142), channel_id=1, source_target_pairs={{0,8},{1,9},{2,10},{3,11},{4,12},{5,13},{6,14},{7,15},{8,0},{9,1},... | collective-permute-start | bytes 344072 | tf_op jit(solution)/shard_map/ppermute | solution.py:999
  234.9 13.4 %collective-permute-start.47 = (bf16[64,896]{1,0:T(8,128)(2,1)S(1)}, bf16[64,896]{1,0:T(8,128)(2,1)S(1)}, u32[]{:S(2)}, u32[]{:S(2)}) collective-permute-start(bf16[64,896]{1,0:T(8,128)(2,1)S(1)} %get-tuple-element.143), channel_id=1, source_target_pairs={{0,12},{1,13},{2,14},{3,15},{4,8},{5,9},{6,10},{7,11},{8,4},{9,5},... | collective-permute-start | bytes 344072 | tf_op jit(solution)/shard_map/ppermute | solution.py:999
  236.1 31.5 %collective-permute-start.33 = (bf16[64,768]{1,0:T(8,128)(2,1)S(1)}, bf16[64,768]{1,0:T(8,128)(2,1)S(1)}, u32[]{:S(2)}, u32[]{:S(2)}) collective-permute-start(bf16[64,768]{1,0:T(8,128)(2,1)S(1)} %get-tuple-element.127), channel_id=1, source_target_pairs={{0,4},{1,5},{2,6},{3,7},{4,0},{5,1},{6,2},{7,3},{8,12},{9,13},{10,... | collective-permute-start | bytes 294920 | tf_op jit(solution)/shard_map/ppermute | solution.py:999
  237.1 31.7 %collective-permute-start.34 = (bf16[64,768]{1,0:T(8,128)(2,1)S(1)}, bf16[64,768]{1,0:T(8,128)(2,1)S(1)}, u32[]{:S(2)}, u32[]{:S(2)}) collective-permute-start(bf16[64,768]{1,0:T(8,128)(2,1)S(1)} %get-tuple-element.128), channel_id=1, source_target_pairs={{0,8},{1,9},{2,10},{3,11},{4,12},{5,13},{6,14},{7,15},{8,0},{9,1},... | collective-permute-start | bytes 294920 | tf_op jit(solution)/shard_map/ppermute | solution.py:999
  264.9 8.0 %collective-permute-start.50 = (bf16[64,768]{1,0:T(8,128)(2,1)S(1)}, bf16[64,768]{1,0:T(8,128)(2,1)S(1)}, u32[]{:S(2)}, u32[]{:S(2)}) collective-permute-start(bf16[64,768]{1,0:T(8,128)(2,1)S(1)} %get-tuple-element.151), channel_id=1, source_target_pairs={{16,4},{17,5},{18,6},{19,7},{20,0},{21,1},{22,2},{23,3},{24,12},{2... | collective-permute-start | bytes 294920 | tf_op jit(solution)/shard_map/ppermute | solution.py:999
  266.2 9.5 %collective-permute-start.51 = (bf16[64,768]{1,0:T(8,128)(2,1)S(1)}, bf16[64,768]{1,0:T(8,128)(2,1)S(1)}, u32[]{:S(2)}, u32[]{:S(2)}) collective-permute-start(bf16[64,768]{1,0:T(8,128)(2,1)S(1)} %get-tuple-element.152), channel_id=1, source_target_pairs={{16,8},{17,9},{18,10},{19,11},{20,12},{21,13},{22,14},{23,15},{24,... | collective-permute-start | bytes 294920 | tf_op jit(solution)/shard_map/ppermute | solution.py:999
  267.5 13.0 %collective-permute-start.52 = (bf16[64,768]{1,0:T(8,128)(2,1)S(1)}, bf16[64,768]{1,0:T(8,128)(2,1)S(1)}, u32[]{:S(2)}, u32[]{:S(2)}) collective-permute-start(bf16[64,768]{1,0:T(8,128)(2,1)S(1)} %get-tuple-element.153), channel_id=1, source_target_pairs={{16,12},{17,13},{18,14},{19,15},{20,8},{21,9},{22,10},{23,11},{24,... | collective-permute-start | bytes 294920 | tf_op jit(solution)/shard_map/ppermute | solution.py:999
  268.8 14.7 %collective-permute-start.35 = (bf16[64,768]{1,0:T(8,128)(2,1)S(1)}, bf16[64,768]{1,0:T(8,128)(2,1)S(1)}, u32[]{:S(2)}, u32[]{:S(2)}) collective-permute-start(bf16[64,768]{1,0:T(8,128)(2,1)S(1)} %get-tuple-element.129), channel_id=1, source_target_pairs={{0,12},{1,13},{2,14},{3,15},{4,8},{5,9},{6,10},{7,11},{8,4},{9,5},... | collective-permute-start | bytes 294920 | tf_op jit(solution)/shard_map/ppermute | solution.py:999
  269.1 16.5 %collective-permute-start.53 = (bf16[64,768]{1,0:T(8,128)(2,1)S(1)}, bf16[64,768]{1,0:T(8,128)(2,1)S(1)}, u32[]{:S(2)}, u32[]{:S(2)}) collective-permute-start(bf16[64,768]{1,0:T(8,128)(2,1)S(1)} %collective-permute-done.49.refs_0_), channel_id=1, source_target_pairs={{0,1},{1,0},{2,3},{3,2},{4,5},{5,4},{6,7},{7,6},{8,9},{9,8},{10,11... | collective-permute-start | bytes 294920 | tf_op jit(solution)/shard_map/ppermute | solution.py:999
  272.9 12.7 %collective-permute-start.54 = (bf16[64,768]{1,0:T(8,128)(2,1)S(1)}, bf16[64,768]{1,0:T(8,128)(2,1)S(1)}, u32[]{:S(2)}, u32[]{:S(2)}) collective-permute-start(bf16[64,768]{1,0:T(8,128)(2,1)S(1)} %collective-permute-done.50.refs_1_), channel_id=1, source_target_pairs={{0,1},{1,0},{2,3},{3,2},{4,5},{5,4},{6,7},{7,6},{8,9},{9,8},{10,11... | collective-permute-start | bytes 294920 | tf_op jit(solution)/shard_map/ppermute | solution.py:999
  275.7 9.9 %collective-permute-start.55 = (bf16[64,768]{1,0:T(8,128)(2,1)S(1)}, bf16[64,768]{1,0:T(8,128)(2,1)S(1)}, u32[]{:S(2)}, u32[]{:S(2)}) collective-permute-start(bf16[64,768]{1,0:T(8,128)(2,1)S(1)} %collective-permute-done.51.refs_2_), channel_id=1, source_target_pairs={{0,1},{1,0},{2,3},{3,2},{4,5},{5,4},{6,7},{7,6},{8,9},{9,8},{10,11... | collective-permute-start | bytes 294920 | tf_op jit(solution)/shard_map/ppermute | solution.py:999
  285.5 10.7 %collective-permute-start.36 = (bf16[256,768]{1,0:T(8,128)(2,1)S(1)}, bf16[256,768]{1,0:T(8,128)(2,1)S(1)}, u32[]{:S(2)}, u32[]{:S(2)}) collective-permute-start(bf16[256,768]{1,0:T(8,128)(2,1)S(1)} %get-tuple-element.132), channel_id=1, source_target_pairs={{0,1},{1,0},{2,3},{3,2},{4,5},{5,4},{6,7},{7,6},{8,9},{9,8},{10,11... | collective-permute-start | bytes 1179656 | tf_op jit(solution)/shard_map/ppermute | solution.py:999
  297.0 32.8 %all-to-all-start.1 = ((bf16[16,16,768]{2,1,0:T(8,128)(2,1)}), bf16[16,16,768]{2,1,0:T(8,128)(2,1)S(1)}, u32[]{:S(2)}, u32[]{:S(2)}) async-start(bf16[16,16,768]{2,1,0:T(8,128)(2,1)} %bitcast.25), calls=%async_computation.1 | async-start | bytes 786432 | tf_op jit(solution)/shard_map/all_to_all | solution.py:1180
  311.9 14.8 %collective-permute-start.62 = (bf16[384,768]{1,0:T(8,128)(2,1)}, bf16[384,768]{1,0:T(8,128)(2,1)S(1)}, u32[]{:S(2)}, u32[]{:S(2)}) collective-permute-start(bf16[384,768]{1,0:T(8,128)(2,1)} %get-tuple-element.174), channel_id=1, source_target_pairs={{0,2},{1,3},{2,0},{3,1},{4,6},{5,7},{6,4},{7,5},{8,10},{9,11},{10,... | collective-permute-start | bytes 1769480 | tf_op jit(solution)/shard_map/ppermute | solution.py:999
  312.9 16.9 %collective-permute-start.48 = (bf16[256,768]{1,0:T(8,128)(2,1)S(1)}, bf16[256,768]{1,0:T(8,128)(2,1)S(1)}, u32[]{:S(2)}, u32[]{:S(2)}) collective-permute-start(bf16[256,768]{1,0:T(8,128)(2,1)S(1)} %get-tuple-element.148), channel_id=1, source_target_pairs={{16,0},{17,1},{18,2},{19,3},{20,4},{21,5},{22,6},{23,7},{24,8},{25... | collective-permute-start | bytes 1179656 | tf_op jit(solution)/shard_map/ppermute | solution.py:999
  314.6 15.2 %collective-permute-start.58 = (bf16[64,896]{1,0:T(8,128)(2,1)S(1)}, bf16[64,896]{1,0:T(8,128)(2,1)S(1)}, u32[]{:S(2)}, u32[]{:S(2)}) collective-permute-start(bf16[64,896]{1,0:T(8,128)(2,1)S(1)} %get-tuple-element.162), channel_id=1, source_target_pairs={{0,4},{1,5},{2,6},{3,7},{4,0},{5,1},{6,2},{7,3},{8,12},{9,13},{10,... | collective-permute-start | bytes 344072 | tf_op jit(solution)/shard_map/ppermute | solution.py:999
  315.8 13.9 %collective-permute-start.59 = (bf16[64,896]{1,0:T(8,128)(2,1)S(1)}, bf16[64,896]{1,0:T(8,128)(2,1)S(1)}, u32[]{:S(2)}, u32[]{:S(2)}) collective-permute-start(bf16[64,896]{1,0:T(8,128)(2,1)S(1)} %get-tuple-element.163), channel_id=1, source_target_pairs={{0,8},{1,9},{2,10},{3,11},{4,12},{5,13},{6,14},{7,15},{8,0},{9,1},... | collective-permute-start | bytes 344072 | tf_op jit(solution)/shard_map/ppermute | solution.py:999
  316.1 13.7 %collective-permute-start.60 = (bf16[64,896]{1,0:T(8,128)(2,1)S(1)}, bf16[64,896]{1,0:T(8,128)(2,1)S(1)}, u32[]{:S(2)}, u32[]{:S(2)}) collective-permute-start(bf16[64,896]{1,0:T(8,128)(2,1)S(1)} %get-tuple-element.164), channel_id=1, source_target_pairs={{0,12},{1,13},{2,14},{3,15},{4,8},{5,9},{6,10},{7,11},{8,4},{9,5},... | collective-permute-start | bytes 344072 | tf_op jit(solution)/shard_map/ppermute | solution.py:999
  349.8 46.1 %collective-permute-start.63 = (bf16[3072,384]{1,0:T(8,128)(2,1)}, bf16[3072,384]{1,0:T(8,128)(2,1)S(1)}, u32[]{:S(2)}, u32[]{:S(2)}) collective-permute-start(bf16[3072,384]{1,0:T(8,128)(2,1)} %get-tuple-element.176), channel_id=1, source_target_pairs={{0,1},{1,0},{2,3},{3,2},{4,5},{5,4},{6,7},{7,6},{8,9},{9,8},{10,11... | collective-permute-start | bytes 7077896 | tf_op jit(solution)/shard_map/ppermute | solution.py:999
  351.0 15.0 %collective-permute-start.73 = (bf16[384,768]{1,0:T(8,128)(2,1)S(1)}, bf16[384,768]{1,0:T(8,128)(2,1)S(1)}, u32[]{:S(2)}, u32[]{:S(2)}) collective-permute-start(bf16[384,768]{1,0:T(8,128)(2,1)S(1)} %copy-done.23), channel_id=1, source_target_pairs={{0,2},{1,3},{2,0},{3,1},{4,6},{5,7},{6,4},{7,5},{8,10},{9,11},{10,... | collective-permute-start | bytes 1769480 | tf_op jit(solution)/shard_map/ppermute | solution.py:999
  351.3 27.4 %collective-permute-start.70 = (bf16[384,768]{1,0:T(8,128)(2,1)S(1)}, bf16[384,768]{1,0:T(8,128)(2,1)S(1)}, u32[]{:S(2)}, u32[]{:S(2)}) collective-permute-start(bf16[384,768]{1,0:T(8,128)(2,1)S(1)} %copy-done.22), channel_id=1, source_target_pairs={{0,2},{1,3},{2,0},{3,1},{4,6},{5,7},{6,4},{7,5},{8,10},{9,11},{10,... | collective-permute-start | bytes 1769480 | tf_op jit(solution)/shard_map/ppermute | solution.py:999
  352.5 40.9 %collective-permute-start.69 = (bf16[384,768]{1,0:T(8,128)(2,1)}, bf16[384,768]{1,0:T(8,128)(2,1)}, u32[]{:S(2)}, u32[]{:S(2)}) collective-permute-start(bf16[384,768]{1,0:T(8,128)(2,1)} %get-tuple-element.158.refs_2_), channel_id=1, source_target_pairs={{0,2},{1,3},{2,0},{3,1},{4,6},{5,7},{6,4},{7,5},{8,10},{9,11},{10,... | collective-permute-start | bytes 1769480 | tf_op jit(solution)/shard_map/ppermute | solution.py:999
  354.9 27.8 %collective-permute-start.61 = (bf16[256,768]{1,0:T(8,128)(2,1)}, bf16[256,768]{1,0:T(8,128)(2,1)}, u32[]{:S(2)}, u32[]{:S(2)}) collective-permute-start(bf16[256,768]{1,0:T(8,128)(2,1)} %get-tuple-element.167), channel_id=1, source_target_pairs={{0,1},{1,0},{2,3},{3,2},{4,5},{5,4},{6,7},{7,6},{8,9},{9,8},{10,11... | collective-permute-start | bytes 1179656 | tf_op jit(solution)/shard_map/ppermute | solution.py:999
  366.0 59.3 %collective-permute-start.72 = (bf16[384,768]{1,0:T(8,128)(2,1)}, bf16[384,768]{1,0:T(8,128)(2,1)}, u32[]{:S(2)}, u32[]{:S(2)}) collective-permute-start(bf16[384,768]{1,0:T(8,128)(2,1)} %sum_pieces.6.refs_0_), channel_id=1, source_target_pairs={{0,8},{1,9},{2,10},{3,11},{4,12},{5,13},{6,14},{7,15},{8,0},{9,1},... | collective-permute-start | bytes 1769480 | tf_op jit(solution)/shard_map/ppermute | solution.py:999
  378.7 46.6 %collective-permute-start.74 = (bf16[384,768]{1,0:T(8,128)(2,1)}, bf16[384,768]{1,0:T(8,128)(2,1)}, u32[]{:S(2)}, u32[]{:S(2)}) collective-permute-start(bf16[384,768]{1,0:T(8,128)(2,1)} %sum_pieces.11), channel_id=1, source_target_pairs={{0,12},{1,13},{2,14},{3,15},{4,8},{5,9},{6,10},{7,11},{8,4},{9,5},... | collective-permute-start | bytes 1769480 | tf_op jit(solution)/shard_map/ppermute | solution.py:999
  382.7 42.7 %collective-permute-start.71 = (bf16[384,768]{1,0:T(8,128)(2,1)}, bf16[384,768]{1,0:T(8,128)(2,1)}, u32[]{:S(2)}, u32[]{:S(2)}) collective-permute-start(bf16[384,768]{1,0:T(8,128)(2,1)} %copy-done.6), channel_id=1, source_target_pairs={{0,4},{1,5},{2,6},{3,7},{4,0},{5,1},{6,2},{7,3},{8,12},{9,13},{10,... | collective-permute-start | bytes 1769480 | tf_op jit(solution)/shard_map/ppermute | solution.py:999
  386.5 42.7 %all-to-all-start.2 = ((bf16[16,16,896]{2,1,0:T(8,128)(2,1)}), bf16[16,16,896]{2,1,0:T(8,128)(2,1)S(1)}, u32[]{:S(2)}, u32[]{:S(2)}) async-start(bf16[16,16,896]{2,1,0:T(8,128)(2,1)} %bitcast.83), calls=%async_computation.2 | async-start | bytes 917504 | tf_op jit(solution)/shard_map/all_to_all | solution.py:1180
  398.4 33.8 %collective-permute-start.64 = (bf16[768,384]{1,0:T(8,128)(2,1)}, bf16[768,384]{1,0:T(8,128)(2,1)S(1)}, u32[]{:S(2)}, u32[]{:S(2)}) collective-permute-start(bf16[768,384]{1,0:T(8,128)(2,1)} %get-tuple-element.178), channel_id=1, source_target_pairs={{0,2},{1,3},{2,0},{3,1},{4,6},{5,7},{6,4},{7,5},{8,10},{9,11},{10,... | collective-permute-start | bytes 1769480 | tf_op jit(solution)/shard_map/ppermute | solution.py:999
  429.2 15.4 %collective-permute-start.66 = (bf16[768,384]{1,0:T(8,128)(2,1)S(1)}, bf16[768,384]{1,0:T(8,128)(2,1)S(1)}, u32[]{:S(2)}, u32[]{:S(2)}) collective-permute-start(bf16[768,384]{1,0:T(8,128)(2,1)S(1)} %copy-done.24), channel_id=1, source_target_pairs={{0,2},{1,3},{2,0},{3,1},{4,6},{5,7},{6,4},{7,5},{8,10},{9,11},{10,... | collective-permute-start | bytes 1769480 | tf_op jit(solution)/shard_map/ppermute | solution.py:999
  434.5 16.7 %collective-permute-start.65 = (bf16[384,384]{1,0:T(8,128)(2,1)S(1)}, bf16[384,384]{1,0:T(8,128)(2,1)S(1)}, u32[]{:S(2)}, u32[]{:S(2)}) collective-permute-start(bf16[384,384]{1,0:T(8,128)(2,1)S(1)} %get-tuple-element.180), channel_id=1, source_target_pairs={{0,4},{1,5},{2,6},{3,7},{4,0},{5,1},{6,2},{7,3},{8,12},{9,13},{10,... | collective-permute-start | bytes 884744 | tf_op jit(solution)/shard_map/ppermute | solution.py:999
  446.9 18.4 %collective-permute-start.67 = (bf16[384,384]{1,0:T(8,128)(2,1)S(1)}, bf16[384,384]{1,0:T(8,128)(2,1)S(1)}, u32[]{:S(2)}, u32[]{:S(2)}) collective-permute-start(bf16[384,384]{1,0:T(8,128)(2,1)S(1)} %get-tuple-element.183), channel_id=1, source_target_pairs={{0,8},{1,9},{2,10},{3,11},{4,12},{5,13},{6,14},{7,15},{8,0},{9,1},... | collective-permute-start | bytes 884744 | tf_op jit(solution)/shard_map/ppermute | solution.py:999
  447.0 28.8 %collective-permute-start.68 = (bf16[384,384]{1,0:T(8,128)(2,1)S(1)}, bf16[384,384]{1,0:T(8,128)(2,1)S(1)}, u32[]{:S(2)}, u32[]{:S(2)}) collective-permute-start(bf16[384,384]{1,0:T(8,128)(2,1)S(1)} %get-tuple-element.184), channel_id=1, source_target_pairs={{0,12},{1,13},{2,14},{3,15},{4,8},{5,9},{6,10},{7,11},{8,4},{9,5},... | collective-permute-start | bytes 884744 | tf_op jit(solution)/shard_map/ppermute | solution.py:999
  (48 other events, 275.7 us)
